TPU v7x, 128 devices: a whole 4x4x4 slice. The times are simulated.
128 devices in a mesh: member: 4 (over y_lo, core), space: 32 (over y_hi, z, x).
Axes of the slice: x: 4, y: 4 (y_hi: 2, y_lo: 2; y = y_hi * 2 + y_lo), z: 4, core: 2. Of those that a mesh axis runs over, the one named last changes fastest.
Arguments:
- latent: bfloat16 [4, 65536, 1024], P('member', 'space'), may hold values from -6 to 6
- target: float32 [100, 65536], P(None, 'space'), may hold values from -6 to 6
- area_weight: float32 [65536], P('space'), may hold values from 0.2 to 3.1, as said below
- var_weight: float32 [100], replicated, may hold values from 0.3 to 3
- w_hidden: bfloat16 [1024, 1024], replicated, may hold values from -0.1875 to 0.1875
- b_hidden: float32 [1024], replicated, may hold values from -3 to 3
- w_output: bfloat16 [100, 1024], replicated, may hold values from -0.1875 to 0.1875
- b_output: float32 [100], replicated, may hold values from -3 to 3
Outputs:
- loss: float32 [], replicated
- grad_w_hidden: float32 [1024, 1024], replicated
- grad_b_hidden: float32 [1024], replicated
- grad_w_output: float32 [100, 1024], replicated
- grad_b_output: float32 [100], replicated
- latent_grad: bfloat16 [4, 65536, 1024], P('member', 'space')
Inputs may be any that keep to these rules, and one draw needn't show every extreme that they name: `area_weight`: positive.
All inputs are finite; a program needn't handle non-finite values.
Results may differ from a plain program's by a relative error of at most 0.003.
The roundings to bfloat16 on the way count: a program that leaves them out, or rounds other values in their place, can miss the bound.
Values sent between devices are 32-bit elements; how exact they have to be, the bound alone decides.
No kernel may reach another device: no remote copies, remote signals or barrier semaphores. Data moves between devices by JAX's collectives and lax.ppermute only.
A program may use at most 128 MiB of HBM per device.

v0:
```python
import jax
import jax.numpy as jnp
from jax import lax
from jax.sharding import PartitionSpec as P

DELTA = 0.05


def smooth(diff):
    return jnp.sqrt(diff * diff + DELTA * DELTA) - DELTA


def slope(diff):
    return diff / jnp.sqrt(diff * diff + DELTA * DELTA)


def shards(latent, target, area_weight, var_weight, w_hidden, b_hidden, w_output, b_output):
    members = lax.axis_size("member")
    points_all = target.shape[1] * lax.axis_size("space")
    n_vars = target.shape[0]
    eps = 0.05 / members
    pair_coef = (1.0 - eps) / (members * (members - 1))
    scale_root = jnp.sqrt(jnp.float32(members * points_all))
    own_latent = latent[0]
    pre = jnp.dot(own_latent, w_hidden, preferred_element_type=jnp.float32) + b_hidden
    hid = jax.nn.silu(pre).astype(jnp.bfloat16)
    own = (
        lax.dot_general(w_output, hid, (((1,), (1,)), ((), ())), preferred_element_type=jnp.float32)
        + b_output[:, None]
    )
    every = lax.all_gather(own[None], "member", axis=0, tiled=True)
    diffs = own[None] - every
    pair_mag = jnp.sum(smooth(diffs), axis=0)
    pair_slope = jnp.sum(slope(diffs), axis=0)
    weights = var_weight[:, None] * area_weight[None, :]
    term = smooth(own - target) / members - 0.5 * pair_coef * pair_mag
    loss_part = jnp.sum(weights * term) / (points_all * n_vars)
    loss_whole = lax.psum(loss_part, ("member", "space"))
    cot = (weights * (slope(own - target) / members - pair_coef * pair_slope)).astype(jnp.bfloat16)
    part_b_output = jnp.sum(cot.astype(jnp.float32), axis=1) / scale_root
    part_w_output = jnp.dot(cot, hid, preferred_element_type=jnp.float32) / scale_root
    back = lax.dot_general(
        cot, w_output, (((0,), (0,)), ((), ())), preferred_element_type=jnp.float32
    )
    sig = jax.nn.sigmoid(pre)
    dpre = (back * sig * (1.0 + pre * (1.0 - sig))).astype(jnp.bfloat16)
    part_b_hidden = jnp.sum(dpre.astype(jnp.float32), axis=0) / scale_root
    part_w_hidden = (
        lax.dot_general(
            own_latent, dpre, (((0,), (0,)), ((), ())), preferred_element_type=jnp.float32
        )
        / scale_root
    )
    loss_term = jnp.float32(0.0)
    summed = lax.psum(
        (part_w_hidden, part_b_hidden, part_w_output, part_b_output, loss_term), ("member", "space")
    )
    grad_w_hidden, grad_b_hidden, grad_w_output, grad_b_output, loss_joined = summed
    latent_grad = lax.dot_general(
        dpre, w_hidden, (((1,), (1,)), ((), ())), preferred_element_type=jnp.float32
    ).astype(jnp.bfloat16)
    return (
        loss_whole,
        grad_w_hidden,
        grad_b_hidden,
        grad_w_output,
        grad_b_output,
        latent_grad[None],
    )


def solution(mesh):
    return jax.shard_map(
        shards,
        mesh=mesh,
        in_specs=(
            P("member", "space", None),
            P(None, "space"),
            P("space"),
            P(),
            P(),
            P(),
            P(),
            P(),
        ),
        out_specs=(P(), P(), P(), P(), P(), P("member", "space", None)),
        check_vma=False,
    )
```

profile of v0, /device:TPU:1, one launch (start us, length us, event | category | flops | bytes accessed | tf_op | source)
XLA Modules:
  0.0 256.6 jit_solution(8420907953652094041)
XLA Ops:
  7.2 0.0 copy-start
  7.2 0.0 copy-start.6
  7.2 0.0 copy-start.8
  7.2 0.0 all-gather.4.cloned.1.call-start
  7.2 1.5 copy-done
  8.8 10.2 %multiply_convert_fusion.1 = (bf16[2048,1024]{1,0:T(8,128)(2,1)S(1)}, f32[2048,1024]{1,0:T(8,128)}) fusion(f32[1024]{0:T(1024)} %param.13, bf16[1024,1024]{1,0:T(8,128)(2,1)S(1)} %copy-done, bf16[1,2048,1024]{2,1,0:T(8,128)(2,1)} %param.8), kind=kOutput, calls=%fused_computation.2 | convolution fusion | flops 4307550208 | bytes 18878464 | tf_op jit(solution)/shard_map/dot_general | solution.py:25
  19.0 0.0 copy-start.1
  19.0 2.0 copy-done.1
  21.0 0.0 copy-done.6
  21.0 0.0 copy-done.8
  21.0 2.4 convolution_add_fusion
  23.3 0.0 copy-start.3
  23.3 0.0 copy-start.7
  23.3 0.0 copy-start.9
  23.3 0.0 all-gather.4.cloned.1.call-update
  23.4 0.2 all-reduce.4.cloned.1.call-start
  23.6 43.6 %all-gather.4.cloned.1.call-done = f32[4,100,2048]{2,1,0:T(8,128)} async-done(((f32[1,100,2048]{2,1,0:T(8,128)}), f32[4,100,2048]{2,1,0:T(8,128)}) %all-gather.4.cloned.1.call-update) | async-done | bytes 3276816 | tf_op jit(solution)/shard_map/all_gather | solution.py:31
  67.1 0.0 copy-start.4
  67.1 0.0 copy-start.2
  67.2 4.7 %divide_reduce_fusion = (f32[100,2048]{1,0:T(8,128)S(1)}, f32[100,2048]{1,0:T(8,128)S(1)}) fusion(f32[4,100,2048]{2,1,0:T(8,128)} %all-gather.4.cloned.1.call-done, f32[100,2048]{1,0:T(8,128)} %bitcast.30), kind=kLoop, calls=%fused_computation.10 | loop fusion | flops 5324800 | bytes 5734400 | tf_op jit(solution)/shard_map/reduce_sum | solution.py:34
  71.8 0.0 copy-done.3
  71.8 0.0 copy-done.7
  71.8 0.0 copy-done.9
  71.8 0.0 copy-done.4
  71.9 0.0 copy-start.11
  71.9 0.0 copy-start.13
  71.9 1.5 convert_reduce_fusion.1
  73.4 0.0 copy-done.2
  73.4 1.5 convolution_multiply_fusion
  74.9 0.0 copy-done.11
  74.9 0.5 copy-done.13
  75.4 0.0 copy-start.10
  75.4 4.0 %convert_reduce_fusion = (f32[1024]{0:T(1024)S(1)}, bf16[2048,1024]{1,0:T(8,128)(2,1)S(1)}) fusion(f32[2048,1024]{1,0:T(8,128)S(1)} %copy-done.13, f32[1024]{0:T(1024)S(1)} %copy-done.11, bf16[100,2048]{1,0:T(8,128)(2,1)S(1)} %get-tuple-element.26, bf16[100,1024]{1,0:T(8,128)(2,1)S(1)} %copy-done.6), kind=kOutput, calls=%fused_computation | convolution fusion | flops 444595200 | bytes 13205504 | tf_op jit(solution)/shard_map/dot_general | solution.py:42
  79.4 0.0 copy-start.12
  79.4 2.0 copy-done.12
  81.4 0.0 copy-done.10
  81.4 6.1 %multiply_bitcast_fusion = f32[1024,1024]{0,1:T(8,128)} fusion(bf16[2048,1024]{1,0:T(8,128)(2,1)S(1)} %get-tuple-element.31, bf16[1,2048,1024]{2,1,0:T(8,128)(2,1)S(1)} %copy-done.10), kind=kOutput, calls=%fused_computation.9 | convolution fusion | flops 4296015872 | bytes 12582912 | tf_op jit(solution)/shard_map/dot_general | solution.py:49
  87.5 0.0 all-reduce.4.cloned.1.call-update
  88.2 66.3 %all-reduce = (f32[]{:T(128)}, f32[1024]{0:T(1024)}, f32[100]{0:T(128)}) all-reduce(f32[]{:T(128)S(6)} %div.48, f32[1024]{0:T(1024)S(1)} %broadcast_multiply_fusion, f32[100]{0:T(128)S(1)} %broadcast_multiply_fusion.1), channel_id=1, replica_groups=mesh['member'=4,'space'=32] {'member','space'}, use_global_device_ids=true, to_apply=%region_2.3 | all-reduce | flops 1125 | bytes 9000 | tf_op jit(solution)/shard_map/psum | solution.py:38
  154.5 8.3 %convert_bitcast_fusion = bf16[1,2048,1024]{2,1,0:T(8,128)(2,1)} fusion(bf16[2048,1024]{1,0:T(8,128)(2,1)} %copy-done.12, bf16[1024,1024]{1,0:T(8,128)(2,1)S(1)} %copy-done), kind=kOutput, calls=%fused_computation.8 | convolution fusion | flops 4297064448 | bytes 10485760 | tf_op jit(solution)/shard_map/dot_general | solution.py:59
  162.8 80.8 %all-reduce.4.cloned.1.call-done = (f32[1024,1024]{0,1:T(8,128)}, f32[100,1024]{1,0:T(8,128)}) async-done(((f32[1024,1024]{0,1:T(8,128)}, f32[100,1024]{1,0:T(8,128)}), (f32[1024,1024]{0,1:T(8,128)}, f32[100,1024]{1,0:T(8,128)})) %all-reduce.4.cloned.1.call-update) | async-done | bytes 4603920 | tf_op jit(solution)/shard_map/psum | solution.py:55
  243.6 0.0 copy-start.5
  243.6 5.4 %copy.15 = f32[1024,1024]{1,0:T(8,128)} copy(f32[1024,1024]{0,1:T(8,128)} %get-tuple-element.23) | data formatting | bytes 8388608
  249.0 0.0 copy-done.5
  249.0 0.8 copy.18
  (2 shorter events, 0.0 us)
Async XLA Ops:
  7.2 1.6 copy-start
  7.2 13.8 %copy-start.6 = (bf16[100,1024]{1,0:T(8,128)(2,1)S(1)}, bf16[100,1024]{1,0:T(8,128)(2,1)}, u32[]{:S(2)}) copy-start(bf16[100,1024]{1,0:T(8,128)(2,1)} %param.14) | copy-start | bytes 614404
  7.2 13.8 %copy-start.8 = (f32[100]{0:T(128)S(1)}, f32[100]{0:T(128)}, u32[]{:S(2)}) copy-start(f32[100]{0:T(128)} %param.15) | copy-start | bytes 1204
  7.2 59.9 %all-gather.4.cloned.1.call-start = ((), (), s32[]{:S(2)}) async-start(), calls=%async_computation | async-start | bytes 4259840 | tf_op jit(solution)/shard_map/all_gather | solution.py:31
  19.0 2.0 copy-start.1
  23.3 48.5 %copy-start.3 = (f32[2048,100]{0,1:T(8,128)S(1)}, f32[2048,100]{0,1:T(8,128)}, u32[]{:S(2)}) copy-start(f32[2048,100]{0,1:T(8,128)} %convolution_add_fusion) | copy-start | bytes 2457604
  23.3 48.5 %copy-start.7 = (f32[2048]{0:T(1024)S(1)}, f32[2048]{0:T(1024)}, u32[]{:S(2)}) copy-start(f32[2048]{0:T(1024)} %param.10) | copy-start | bytes 24580
  23.3 48.5 %copy-start.9 = (f32[100]{0:T(128)S(1)}, f32[100]{0:T(128)}, u32[]{:S(2)}) copy-start(f32[100]{0:T(128)} %param.11) | copy-start | bytes 1204
  23.4 220.2 %all-reduce.4.cloned.1.call-start = ((), (), s32[]{:S(2)}) async-start(), calls=%async_computation.1 | async-start | bytes 9240576 | tf_op jit(solution)/shard_map/psum | solution.py:55
  67.1 4.7 %copy-start.4 = (f32[100,2048]{1,0:T(8,128)S(1)}, f32[100,2048]{1,0:T(8,128)}, u32[]{:S(2)}) copy-start(f32[100,2048]{1,0:T(8,128)} %param.9) | copy-start | bytes 2457604
  67.1 6.2 %copy-start.2 = (bf16[2048,1024]{1,0:T(8,128)(2,1)S(1)}, bf16[2048,1024]{1,0:T(8,128)(2,1)}, u32[]{:S(2)}) copy-start(bf16[2048,1024]{1,0:T(8,128)(2,1)} %copy-done.1) | copy-start | bytes 12582916
  71.9 3.1 %copy-start.11 = (f32[1024]{0:T(1024)S(1)}, f32[1024]{0:T(1024)}, u32[]{:S(2)}) copy-start(f32[1024]{0:T(1024)} %param.13) | copy-start | bytes 12292
  71.9 3.5 %copy-start.13 = (f32[2048,1024]{1,0:T(8,128)S(1)}, f32[2048,1024]{1,0:T(8,128)}, u32[]{:S(2)}) copy-start(f32[2048,1024]{1,0:T(8,128)} %get-tuple-element.29) | copy-start | bytes 25165828
  75.4 6.0 %copy-start.10 = (bf16[1,2048,1024]{2,1,0:T(8,128)(2,1)S(1)}, bf16[1,2048,1024]{2,1,0:T(8,128)(2,1)}, u32[]{:S(2)}) copy-start(bf16[1,2048,1024]{2,1,0:T(8,128)(2,1)} %param.8) | copy-start | bytes 12582916
  79.4 2.0 copy-start.12
  243.6 5.4 %copy-start.5 = (f32[100,1024]{1,0:T(8,128)S(1)}, f32[100,1024]{1,0:T(8,128)}, u32[]{:S(2)}) copy-start(f32[100,1024]{1,0:T(8,128)} %get-tuple-element.35) | copy-start | bytes 1228804
Sparse Core Ops, SparseCore 0:
  23.5 43.6 all-gather.3
  87.6 155.9 all-reduce.3
where the time goes:
time: 257 us
  waiting for transfers between devices  124 us (48%)
  blocking collectives  66.3 us (26%)
  matrix products  32.5 us (13%)
  between operations  14.8 us (6%)
  local copies, waits for them, and re-layouts  12.2 us (5%)
  other arithmetic  6.18 us (2%)
    psum x1, waiting for transfers between devices, shards(): lax.psum((part_w_hidden, part_b_hidden, part_w_output, part_b_output, los...  80.8 us
    psum x1, blocking collectives, shards(): loss_whole = lax.psum(loss_part, ('member', 'space'))  66.3 us
    all_gather x1, waiting for transfers between devices, shards(): every = lax.all_gather(own[None], 'member', axis=0, tiled=True)  43.6 us
    unnamed x30, local copies, waits for them, and re-layouts  12.2 us
    dot_general x1, matrix products, shards(): jnp.dot(own_latent, w_hidden, preferred_element_type=jnp.float32) + b_hidden  10.2 us
    dot_general x1, matrix products, shards(): lax.dot_general(dpre, w_hidden, (((1,), (1,)), ((), ())), preferred_eleme...  8.31 us
    dot_general x1, matrix products, shards(): lax.dot_general(own_latent, dpre, (((0,), (0,)), ((), ())), preferred_ele...  6.09 us
  transfers between devices with their start and end apart: 2, of which 2 were waited for; matrix products, arithmetic and copies ran while one was open for 3% of the time, Pallas kernels for 0%

commit v1 on v0

v1 whole, which is shorter than its diff:
```python
import math

import jax
import jax.numpy as jnp
from jax import lax
from jax.sharding import Mesh, PartitionSpec as P

DELTA = 0.05
ALL = ("ylo", "core", "yhi", "z", "x")


def flat(core, x, y, z):
    return ((y % 2) * 2 + core) * 32 + (y // 2) * 16 + z * 4 + x


def moved(where):
    pairs = []
    for core in range(2):
        for x in range(4):
            for y in range(4):
                for z in range(4):
                    pairs.append((flat(core, x, y, z), flat(*where(core, x, y, z))))
    return pairs


SWAP = moved(lambda c, x, y, z: (1 - c, x, y, z))
NEAR = moved(lambda c, x, y, z: (c, x, y ^ 1, z))


def first(k):
    return moved(lambda c, x, y, z: (c, x, y, (z + k) % 4) if c == 0 else (c, (x + k) % 4, y, z))


def second(k):
    return moved(lambda c, x, y, z: (c, x, y, (z + k) % 4) if c == 1 else (c, (x + k) % 4, y, z))


def along_y(k):
    return moved(lambda c, x, y, z: (c, x, (y + k) % 4, z))


def send(array, pairs):
    return lax.ppermute(array, ALL, pairs)


def grad_sum(own, sibling):
    core, x, z = lax.axis_index("core"), lax.axis_index("x"), lax.axis_index("z")
    place = jnp.where(core == 0, x, z)
    got = send(sibling, SWAP)
    held = [own[k] + got[k] for k in range(4)]
    block = held[0]
    for k in (1, 3, 2):
        block = block + send(held[k], first(k))
    rows = block.shape[0] // 4
    quarters = block.reshape((4, rows) + block.shape[1:])
    pick = lambda k: lax.dynamic_index_in_dim(quarters, (place + k) % 4, 0, keepdims=False)
    quarter = pick(0)
    for k in (1, 3, 2):
        quarter = quarter + send(pick(k), second(k))
    quarter = quarter + send(quarter, along_y(1)) + send(quarter, along_y(3)) + send(quarter, along_y(2))
    came = [quarter] + [send(quarter, second(k)) for k in (1, 2, 3)]
    twice = jnp.concatenate([came[3], came[2], came[1], came[0], came[3], came[2], came[1]], 0)
    block = lax.dynamic_slice_in_dim(twice, ((3 - place) % 4) * rows, 4 * rows, 0)
    mine = [block] + [send(block, first(k)) for k in (1, 2, 3)]
    return mine, [send(m, SWAP) for m in mine]


def smooth(diff):
    return jnp.sqrt(diff * diff + DELTA * DELTA) - DELTA


def slope(diff):
    return diff / jnp.sqrt(diff * diff + DELTA * DELTA)


def shards(latent, target, area_weight, var_weight, w_hidden, b_hidden, w_output, b_output):
    members = 4
    n_vars, points = target.shape
    points_all = points * 32
    depth, width = w_hidden.shape
    eps = 0.05 / members
    pair_coef = (1.0 - eps) / (members * (members - 1))
    scale = 1.0 / math.sqrt(members * points_all)
    core, x, z = lax.axis_index("core"), lax.axis_index("x"), lax.axis_index("z")
    place_own = jnp.where(core == 0, z, x)
    place_sib = jnp.where(core == 0, x, z)
    own_latent = latent[0]
    pre = jnp.dot(own_latent, w_hidden, preferred_element_type=jnp.float32) + b_hidden
    sig = jax.nn.sigmoid(pre)
    hid = (pre * sig).astype(jnp.bfloat16)
    own = (
        lax.dot_general(w_output, hid, (((1,), (1,)), ((), ())), preferred_element_type=jnp.float32)
        + b_output[:, None]
    )
    near = send(own, NEAR)
    others = (send(own, SWAP), near, send(near, SWAP))
    pair_mag = sum(smooth(own - other) for other in others)
    pair_slope = sum(slope(own - other) for other in others)
    weights = var_weight[:, None] * area_weight[None, :]
    term = smooth(own - target) / members - 0.5 * pair_coef * pair_mag
    loss_part = jnp.sum(weights * term) / (points_all * n_vars)
    cot = (weights * (slope(own - target) / members - pair_coef * pair_slope)).astype(jnp.bfloat16)
    part_b_output = jnp.sum(cot.astype(jnp.float32), axis=1) * scale
    part_w_output = jnp.dot(cot, hid, preferred_element_type=jnp.float32) * scale
    back = lax.dot_general(
        cot, w_output, (((0,), (0,)), ((), ())), preferred_element_type=jnp.float32
    )
    dpre = (back * sig * (1.0 + pre * (1.0 - sig))).astype(jnp.bfloat16)
    part_b_hidden = jnp.sum(dpre.astype(jnp.float32), axis=0) * scale
    part_w_hidden = (
        lax.dot_general(
            own_latent, dpre, (((0,), (0,)), ((), ())), preferred_element_type=jnp.float32
        )
        * scale
    )
    misc = jnp.concatenate([part_b_output, loss_part[None], jnp.zeros((width - n_vars - 1,), jnp.float32)])
    rest = jnp.concatenate(
        [part_w_output, part_b_hidden[None], misc[None], jnp.zeros((128 - n_vars - 2, width), jnp.float32)], 0
    )
    blocks = jnp.concatenate([part_w_hidden.reshape(4, depth // 4, width), rest.reshape(4, 32, width)], 1)
    half = width // 2

    def ordered(which, place):
        mine = lax.dynamic_slice_in_dim(blocks, which * half, half, 2)
        twice = jnp.concatenate([mine, mine[:3]], 0)
        return lax.dynamic_slice_in_dim(twice, place, 4, 0)

    out_own, out_sib = grad_sum(ordered(core, place_own), ordered(1 - core, place_sib))
    latent_grad = lax.dot_general(
        dpre, w_hidden, (((1,), (1,)), ((), ())), preferred_element_type=jnp.float32
    ).astype(jnp.bfloat16)

    def in_place(outs, place):
        return jnp.take(jnp.stack(outs), (place - jnp.arange(4)) % 4, axis=0)

    o, s = in_place(out_own, place_own), in_place(out_sib, place_sib)
    whole = jnp.concatenate([jnp.where(core == 0, o, s), jnp.where(core == 0, s, o)], 2)
    grad_w_hidden = whole[:, : depth // 4].reshape(depth, width)
    rest = whole[:, depth // 4 :].reshape(128, width)
    return (
        rest[n_vars + 1, n_vars],
        grad_w_hidden,
        rest[n_vars],
        rest[:n_vars],
        rest[n_vars + 1, :n_vars],
        latent_grad[None],
    )


def solution(mesh):
    fine = Mesh(mesh.devices.reshape(2, 2, 2, 4, 4), ALL)
    member, space = ("ylo", "core"), ("yhi", "z", "x")
    return jax.shard_map(
        shards,
        mesh=fine,
        in_specs=(P(member, space, None), P(None, space), P(space), P(), P(), P(), P(), P()),
        out_specs=(P(), P(), P(), P(), P(), P(member, space, None)),
        check_vma=False,
    )
```

time: 257 us -> 176 us (0.68)
  waiting for transfers between devices: 124 us -> 48.2 us
  blocking collectives: 66.3 us -> 0 us
  starting transfers between devices: 0.26 us -> 47.4 us
  other arithmetic: 6.18 us -> 28 us
  between operations: 14.8 us -> 1.56 us
  local copies, waits for them, and re-layouts: 12.2 us -> 17.1 us
    psum x1 -> x0, waiting for transfers between devices: 80.8 us -> none  [shards(): lax.psum((part_w_hidden, part_b_hidden, part_w_output, part_b_output, los...]
    psum x1 -> x0, blocking collectives: 66.3 us -> none  [shards(): loss_whole = lax.psum(loss_part, ('member', 'space'))]
    ppermute x0 -> x23, waiting for transfers between devices: none -> 48.2 us  [send(): return lax.ppermute(array, ALL, pairs)]
    ppermute x0 -> x23, starting transfers between devices: none -> 47.4 us  [send(): return lax.ppermute(array, ALL, pairs)]
    all_gather x1 -> x0, waiting for transfers between devices: 43.6 us -> none  [shards(): every = lax.all_gather(own[None], 'member', axis=0, tiled=True)]
    concatenate x0 -> x6, other arithmetic: none -> 9.55 us  [the longest x1 4.36 us: shards(): jnp.concatenate([part_w_hidden.reshape(4, depth // 4, width), rest.reshap...]
    unnamed x30 -> x32, local copies, waits for them, and re-layouts: 12.2 us -> 3.45 us
    gather x0 -> x2, local copies, waits for them, and re-layouts: none -> 7.57 us  [in_place(): return jnp.take(jnp.stack(outs), (place - jnp.arange(4)) % 4, axis=0)]
  transfers between devices with their start and end apart: 2 -> 23, of which waited for: 2 -> 13; matrix products, arithmetic and copies ran while one was open for 3% -> 10% of each run, Pallas kernels for 0% -> 0%
where the time goes in v1:
time: 176 us
  waiting for transfers between devices  48.2 us (27%)
  starting transfers between devices  47.4 us (27%)
  matrix products  33.3 us (19%)
  other arithmetic  28 us (16%)
  local copies, waits for them, and re-layouts  17.1 us (10%)
    ppermute x23, waiting for transfers between devices, send(): return lax.ppermute(array, ALL, pairs)  48.2 us
    ppermute x23, starting transfers between devices, send(): return lax.ppermute(array, ALL, pairs)  47.4 us
    dot_general x1, matrix products, shards(): jnp.dot(own_latent, w_hidden, preferred_element_type=jnp.float32) + b_hidden  10.3 us
    dot_general x1, matrix products, shards(): lax.dot_general(dpre, w_hidden, (((1,), (1,)), ((), ())), preferred_eleme...  8.3 us
    gather x2, local copies, waits for them, and re-layouts, in_place(): return jnp.take(jnp.stack(outs), (place - jnp.arange(4)) % 4, axis=0)  7.57 us
    dot_general x1, matrix products, shards(): lax.dot_general(cot, w_output, (((0,), (0,)), ((), ())), preferred_elemen...  6.28 us
    dot_general x1, matrix products, shards(): lax.dot_general(own_latent, dpre, (((0,), (0,)), ((), ())), preferred_ele...  6.2 us
    another operation x2, other arithmetic, in_place(): return jnp.take(jnp.stack(outs), (place - jnp.arange(4)) % 4, axis=0)  5.99 us
  transfers between devices with their start and end apart: 23, of which 13 were waited for; matrix products, arithmetic and copies ran while one was open for 10% of the time, Pallas kernels for 0%

profile of v1, /device:TPU:1, one launch (start us, length us, event | category | flops | bytes accessed | tf_op | source)
XLA Modules:
  0.0 175.6 jit_solution(201982425200353390)
XLA Ops:
  0.7 1.6 copy-done
  2.2 10.3 %multiply_convert_fusion.1 = (bf16[2048,1024]{1,0:T(8,128)(2,1)S(1)}, f32[2048,1024]{1,0:T(8,128)}) fusion(f32[1024]{0:T(1024)} %param.15, bf16[1024,1024]{1,0:T(8,128)(2,1)S(1)} %copy-done, bf16[1,2048,1024]{2,1,0:T(8,128)(2,1)} %param.10), kind=kOutput, calls=%fused_computation.4 | convolution fusion | flops 4307550208 | bytes 18878464 | tf_op jit(solution)/shard_map/dot_general | solution.py:88
  12.5 1.5 fusion.4
  14.5 2.1 %collective-permute-start.1 = (f32[100,2048]{1,0:T(8,128)S(1)}, f32[100,2048]{1,0:T(8,128)}, u32[]{:S(2)}, u32[]{:S(2)}) collective-permute-start(f32[100,2048]{1,0:T(8,128)S(1)} %fusion.4), channel_id=1, source_target_pairs={{0,64},{4,68},{8,72},{12,76},{64,0},{68,4},{72,8},{76,12},{16,80},... | collective-permute-start | bytes 2457608 | tf_op jit(solution)/shard_map/ppermute | solution.py:43
  16.6 1.0 collective-permute-start
  17.6 17.4 %collective-permute-done.1 = f32[100,2048]{1,0:T(8,128)} collective-permute-done((f32[100,2048]{1,0:T(8,128)S(1)}, f32[100,2048]{1,0:T(8,128)}, u32[]{:S(2)}, u32[]{:S(2)}) %collective-permute-start.1) | collective-permute-done | bytes 819232 | tf_op jit(solution)/shard_map/ppermute | solution.py:43
  35.0 1.6 collective-permute-start.2
  36.7 2.3 %collective-permute-done.2 = f32[100,2048]{1,0:T(8,128)} collective-permute-done((f32[100,2048]{1,0:T(8,128)}, f32[100,2048]{1,0:T(8,128)}, u32[]{:S(2)}, u32[]{:S(2)}) %collective-permute-start.2) | collective-permute-done | bytes 819232 | tf_op jit(solution)/shard_map/ppermute | solution.py:43
  39.0 4.6 %convert_reduce_fusion.1 = (f32[100]{0:T(128)S(1)}, bf16[100,2048]{1,0:T(8,128)(2,1)S(1)}, f32[]{:T(128)}) fusion(f32[100,2048]{1,0:T(8,128)S(1)} %fusion.4, f32[100,2048]{1,0:T(8,128)} %collective-permute-done.2, f32[100,2048]{1,0:T(8,128)} %collective-permute-done.1, f32[100,2048]{1,0:T(8,128)} %collective-permute-done, f32[100,2048]{1,0:T(8,128)} %param.11, ...), kind=kLoop, calls=%fused_computation.36 | loop fusion | flops 7577499 | bytes 4514596 | tf_op jit(solution)/shard_map/reduce_sum | solution.py:103
  44.4 6.3 %convert_reduce_fusion = (f32[1024]{0:T(1024)S(1)}, bf16[2048,1024]{1,0:T(8,128)(2,1)S(1)}) fusion(f32[2048,1024]{1,0:T(8,128)} %get-tuple-element.21, f32[1024]{0:T(1024)S(1)} %copy-done.11, bf16[100,2048]{1,0:T(8,128)(2,1)S(1)} %get-tuple-element.8, bf16[100,1024]{1,0:T(8,128)(2,1)S(1)} %copy-done.6), kind=kOutput, calls=%fused_computation.2 | convolution fusion | flops 444595200 | bytes 13205504 | tf_op jit(solution)/shard_map/dot_general | solution.py:105
  50.7 6.2 %fusion.9 = f32[1024,1024]{0,1:T(8,128)} fusion(bf16[2048,1024]{1,0:T(8,128)(2,1)S(1)} %get-tuple-element.23, bf16[1,2048,1024]{2,1,0:T(8,128)(2,1)S(1)} %copy-done.10), kind=kOutput, calls=%fused_computation.30 | convolution fusion | flops 4296015872 | bytes 12582912 | tf_op jit(solution)/shard_map/dot_general | solution.py:111
  57.8 4.4 %fusion.8 = (f32[4,288,512]{2,1,0:T(8,128)}, f32[4,288,512]{2,1,0:T(8,128)S(1)}) fusion(s32[]{:T(128)S(6)} %select_n.88, f32[4,256,1024]{2,1,0:T(8,128)} %bitcast.72, f32[4,32,1024]{2,1,0:T(8,128)S(1)} %bitcast.76, s32[]{:T(128)S(6)} %select_n.91), kind=kLoop, calls=%fused_computation.25 | loop fusion | flops 1179648 | bytes 9437192 | tf_op jit(solution)/shard_map/concatenate | solution.py:120
  62.3 2.0 %fusion.5 = f32[4,288,512]{2,1,0:T(8,128)} fusion(s32[]{:T(128)S(6)} %select_n.93, f32[4,288,512]{2,1,0:T(8,128)S(1)} %get-tuple-element.15, f32[3,288,512]{2,1,0:T(8,128)S(1)} %slice.70), kind=kLoop, calls=%fused_computation.22 | loop fusion | flops 589824 | bytes 6488068 | tf_op jit(solution)/shard_map/concatenate | solution.py:125
  64.7 1.8 %slice.68 = f32[3,288,512]{2,1,0:T(8,128)S(1)} slice(f32[4,288,512]{2,1,0:T(8,128)} %get-tuple-element.14), slice={[0:3], [0:288], [0:512]} | slice | bytes 3538944 | tf_op jit(solution)/shard_map/slice | solution.py:125
  67.4 1.7 collective-permute-done.3
  69.2 2.8 %fusion.16 = (f32[288,512]{1,0:T(8,128)}, f32[288,512]{1,0:T(8,128)}, f32[288,512]{1,0:T(8,128)}) fusion(f32[4,288,512]{2,1,0:T(8,128)} %collective-permute-done.3, f32[4,288,512]{2,1,0:T(8,128)S(1)} %fusion.6), kind=kLoop, calls=%fused_computation.46 | loop fusion | flops 442368 | bytes 5308416 | tf_op jit(solution)/shard_map/add | solution.py:50
  71.9 1.4 collective-permute-start.4
  73.3 1.3 collective-permute-start.5
  74.6 1.7 collective-permute-start.6
  76.3 6.1 %collective-permute-done.4 = f32[288,512]{1,0:T(8,128)S(1)} collective-permute-done((f32[288,512]{1,0:T(8,128)}, f32[288,512]{1,0:T(8,128)S(1)}, u32[]{:S(2)}, u32[]{:S(2)}) %collective-permute-start.4) | collective-permute-done | bytes 589856 | tf_op jit(solution)/shard_map/ppermute | solution.py:43
  83.4 6.6 %collective-permute-done.6 = f32[288,512]{1,0:T(8,128)} collective-permute-done((f32[288,512]{1,0:T(8,128)}, f32[288,512]{1,0:T(8,128)}, u32[]{:S(2)}, u32[]{:S(2)}) %collective-permute-start.6) | collective-permute-done | bytes 589856 | tf_op jit(solution)/shard_map/ppermute | solution.py:43
  90.0 1.9 %fusion.20 = f32[288,512]{1,0:T(8,128)S(1)} fusion(f32[288,512]{1,0:T(8,128)} %collective-permute-done.6, f32[288,512]{1,0:T(8,128)} %copy-done.5, f32[288,512]{1,0:T(8,128)S(1)} %collective-permute-done.4, f32[4,288,512]{2,1,0:T(8,128)} %collective-permute-done.3, f32[4,288,512]{2,1,0:T(8,128)} %copy-done.4), kind=kLoop, calls=%fused_computation.51 | loop fusion | flops 589824 | bytes 3538944 | tf_op jit(solution)/shard_map/add | solution.py:53
  92.6 1.3 collective-permute-start.7
  93.9 2.1 %collective-permute-start.8 = (f32[72,512]{1,0:T(8,128)S(1)}, f32[72,512]{1,0:T(8,128)S(1)}, u32[]{:S(2)}, u32[]{:S(2)}) collective-permute-start(f32[72,512]{1,0:T(8,128)S(1)} %get-tuple-element.19), channel_id=1, source_target_pairs={{0,3},{4,7},{8,11},{12,15},{64,67},{68,71},{72,75},{76,79},{16,19}... | collective-permute-start | bytes 442376 | tf_op jit(solution)/shard_map/ppermute | solution.py:43
  96.0 1.3 collective-permute-start.9
  97.4 1.4 collective-permute-done.7
  98.8 2.8 %collective-permute-done.9 = f32[72,512]{1,0:T(8,128)S(1)} collective-permute-done((f32[72,512]{1,0:T(8,128)S(1)}, f32[72,512]{1,0:T(8,128)S(1)}, u32[]{:S(2)}, u32[]{:S(2)}) %collective-permute-start.9) | collective-permute-done | bytes 147488 | tf_op jit(solution)/shard_map/ppermute | solution.py:43
  101.6 1.4 collective-permute-start.10
  103.0 1.5 collective-permute-start.11
  104.5 1.6 collective-permute-start.12
  107.0 3.1 %collective-permute-done.12 = f32[72,512]{1,0:T(8,128)S(1)} collective-permute-done((f32[72,512]{1,0:T(8,128)S(1)}, f32[72,512]{1,0:T(8,128)S(1)}, u32[]{:S(2)}, u32[]{:S(2)}) %collective-permute-start.12) | collective-permute-done | bytes 147488 | tf_op jit(solution)/shard_map/ppermute | solution.py:43
  110.1 1.4 collective-permute-start.13
  111.6 1.2 collective-permute-start.14
  112.8 1.7 collective-permute-done.13
  114.5 2.6 %collective-permute-done.14 = f32[72,512]{1,0:T(8,128)S(1)} collective-permute-done((f32[72,512]{1,0:T(8,128)S(1)}, f32[72,512]{1,0:T(8,128)S(1)}, u32[]{:S(2)}, u32[]{:S(2)}) %collective-permute-start.14) | collective-permute-done | bytes 147488 | tf_op jit(solution)/shard_map/ppermute | solution.py:43
  117.1 1.5 collective-permute-done.15
  119.6 1.1 collective-permute-start.16
  120.7 3.5 %collective-permute-start.17 = (f32[288,512]{1,0:T(8,128)}, f32[288,512]{1,0:T(8,128)S(1)}, u32[]{:S(2)}, u32[]{:S(2)}) collective-permute-start(f32[288,512]{1,0:T(8,128)} %constant_dynamic-slice_fusion), channel_id=1, source_target_pairs={{0,8},{4,12},{8,0},{12,4},{64,72},{68,76},{72,64},{76,68},{16,24},... | collective-permute-start | bytes 1769480 | tf_op jit(solution)/shard_map/ppermute | solution.py:43
  124.4 7.1 %collective-permute-start.19 = (f32[288,512]{1,0:T(8,128)}, f32[288,512]{1,0:T(8,128)}, u32[]{:S(2)}, u32[]{:S(2)}) collective-permute-start(f32[288,512]{1,0:T(8,128)} %constant_dynamic-slice_fusion), channel_id=1, source_target_pairs={{0,32},{4,36},{8,40},{12,44},{64,96},{68,100},{72,104},{76,108},{1... | collective-permute-start | bytes 1769480 | tf_op jit(solution)/shard_map/ppermute | solution.py:43
  131.4 6.9 %collective-permute-start.20 = (f32[288,512]{1,0:T(8,128)S(1)}, f32[288,512]{1,0:T(8,128)}, u32[]{:S(2)}, u32[]{:S(2)}) collective-permute-start(f32[288,512]{1,0:T(8,128)S(1)} %collective-permute-done.16), channel_id=1, source_target_pairs={{0,32},{4,36},{8,40},{12,44},{64,96},{68,100},{72,104},{76,108},{1... | collective-permute-start | bytes 1769480 | tf_op jit(solution)/shard_map/ppermute | solution.py:43
  138.3 7.3 %collective-permute-start.21 = (f32[288,512]{1,0:T(8,128)S(1)}, f32[288,512]{1,0:T(8,128)}, u32[]{:S(2)}, u32[]{:S(2)}) collective-permute-start(f32[288,512]{1,0:T(8,128)S(1)} %collective-permute-done.17), channel_id=1, source_target_pairs={{0,32},{4,36},{8,40},{12,44},{64,96},{68,100},{72,104},{76,108},{1... | collective-permute-start | bytes 1769480 | tf_op jit(solution)/shard_map/ppermute | solution.py:43
  145.7 8.3 %convert_bitcast_fusion = bf16[1,2048,1024]{2,1,0:T(8,128)(2,1)} fusion(bf16[2048,1024]{1,0:T(8,128)(2,1)} %copy-done.12, bf16[1024,1024]{1,0:T(8,128)(2,1)S(1)} %copy-done), kind=kOutput, calls=%fused_computation.15 | convolution fusion | flops 4297064448 | bytes 10485760 | tf_op jit(solution)/shard_map/dot_general | solution.py:129
  154.0 2.8 %pad_maximum_fusion.1 = f32[4,288,512]{2,1,0:T(8,128)} fusion(f32[1,288,512]{2,1,0:T(8,128)} %bitcast.20, f32[1,288,512]{2,1,0:T(8,128)S(1)} %bitcast.82, f32[1,288,512]{2,1,0:T(8,128)S(1)} %bitcast.81, f32[1,288,512]{2,1,0:T(8,128)S(1)} %fusion.36), kind=kLoop, calls=%fused_computation.26 | loop fusion | flops 1769472 | bytes 4718592 | tf_op jit(solution)/shard_map/stack | solution.py:134
  156.8 3.8 %gather_fusion = f32[4,288,512]{2,1,0:T(8,128)} fusion(f32[4,288,512]{2,1,0:T(8,128)} %pad_maximum_fusion.1, s32[1024]{0:T(1024)S(1)} %pad_clamp_fusion.1), kind=kCustom, calls=%fused_computation.clone | custom fusion | bytes 4718608 | tf_op jit(solution)/shard_map/jit(_take)/gather | solution.py:134
  160.6 3.2 %pad_maximum_fusion.2 = f32[4,288,512]{2,1,0:T(8,128)} fusion(f32[1,288,512]{2,1,0:T(8,128)} %bitcast.24, f32[1,288,512]{2,1,0:T(8,128)} %bitcast.23, f32[1,288,512]{2,1,0:T(8,128)} %bitcast.22, f32[1,288,512]{2,1,0:T(8,128)} %bitcast.21), kind=kLoop, calls=%fused_computation.27 | loop fusion | flops 1769472 | bytes 4718592 | tf_op jit(solution)/shard_map/stack | solution.py:134
  163.8 3.8 %gather_fusion.1 = f32[4,288,512]{2,1,0:T(8,128)} fusion(f32[4,288,512]{2,1,0:T(8,128)} %pad_maximum_fusion.2, s32[1024]{0:T(1024)S(1)} %pad_clamp_fusion), kind=kCustom, calls=%fused_computation.1.clone | custom fusion | bytes 4718608 | tf_op jit(solution)/shard_map/jit(_take)/gather | solution.py:134
  167.6 3.0 %select_select_fusion.1 = (f32[4,288,512]{2,1,0:T(8,128)S(1)}, f32[4,288,512]{2,1,0:T(8,128)S(1)}) fusion(f32[4,288,512]{2,1,0:T(8,128)} %gather_fusion.1, f32[4,288,512]{2,1,0:T(8,128)} %gather_fusion, pred[4]{0:T(512)(128)(4,1)S(1)} %get-tuple-element.24, pred[4]{0:T(512)(128)(4,1)S(1)} %get-tuple-element.25, pred[]{:T(512)S(6)} %eq.16), kind=kLoop, calls=%fused_computation.29 | loop fusion | flops 2359296 | bytes 9437193 | tf_op jit(solution)/shard_map/jit(_where)/select_n | solution.py:137
  170.6 2.4 %pad_maximum_fusion = f32[4,256,1024]{2,1,0:T(8,128)} fusion(f32[4,288,512]{2,1,0:T(8,128)S(1)} %get-tuple-element.10, f32[4,288,512]{2,1,0:T(8,128)S(1)} %get-tuple-element.9), kind=kLoop, calls=%fused_computation.10 | loop fusion | flops 1048576 | bytes 8912896 | tf_op jit(solution)/shard_map/concatenate | solution.py:137
  (73 shorter events, 9.4 us)
Async XLA Ops:
  0.6 1.6 copy-start
  0.6 11.9 %copy-start.6 = (bf16[100,1024]{1,0:T(8,128)(2,1)S(1)}, bf16[100,1024]{1,0:T(8,128)(2,1)}, u32[]{:S(2)}) copy-start(bf16[100,1024]{1,0:T(8,128)(2,1)} %param.16) | copy-start | bytes 614404
  0.7 11.8 %copy-start.8 = (f32[100]{0:T(128)S(1)}, f32[100]{0:T(128)}, u32[]{:S(2)}) copy-start(f32[100]{0:T(128)} %param.17) | copy-start | bytes 1204
  12.5 2.0 %copy-start.1 = (bf16[2048,1024]{1,0:T(8,128)(2,1)}, bf16[2048,1024]{1,0:T(8,128)(2,1)S(1)}, u32[]{:S(2)}) copy-start(bf16[2048,1024]{1,0:T(8,128)(2,1)S(1)} %get-tuple-element.20) | copy-start | bytes 12582916
  12.5 26.5 %copy-start.7 = (f32[2048]{0:T(1024)S(1)}, f32[2048]{0:T(1024)}, u32[]{:S(2)}) copy-start(f32[2048]{0:T(1024)} %param.12) | copy-start | bytes 24580
  12.5 26.5 %copy-start.9 = (f32[100]{0:T(128)S(1)}, f32[100]{0:T(128)}, u32[]{:S(2)}) copy-start(f32[100]{0:T(128)} %param.13) | copy-start | bytes 1204
  14.5 20.5 %collective-permute-start.1 = (f32[100,2048]{1,0:T(8,128)S(1)}, f32[100,2048]{1,0:T(8,128)}, u32[]{:S(2)}, u32[]{:S(2)}) collective-permute-start(f32[100,2048]{1,0:T(8,128)S(1)} %fusion.4), channel_id=1, source_target_pairs={{0,64},{4,68},{8,72},{12,76},{64,0},{68,4},{72,8},{76,12},{16,80},... | collective-permute-start | bytes 2457608 | tf_op jit(solution)/shard_map/ppermute | solution.py:43
  16.6 20.1 %collective-permute-start = (f32[100,2048]{1,0:T(8,128)S(1)}, f32[100,2048]{1,0:T(8,128)}, u32[]{:S(2)}, u32[]{:S(2)}) collective-permute-start(f32[100,2048]{1,0:T(8,128)S(1)} %fusion.4), channel_id=1, source_target_pairs={{0,32},{4,36},{8,40},{12,44},{64,96},{68,100},{72,104},{76,108},{1... | collective-permute-start | bytes 2457608 | tf_op jit(solution)/shard_map/ppermute | solution.py:43
  35.0 4.0 %collective-permute-start.2 = (f32[100,2048]{1,0:T(8,128)}, f32[100,2048]{1,0:T(8,128)}, u32[]{:S(2)}, u32[]{:S(2)}) collective-permute-start(f32[100,2048]{1,0:T(8,128)} %collective-permute-done.1), channel_id=1, source_target_pairs={{0,32},{4,36},{8,40},{12,44},{64,96},{68,100},{72,104},{76,108},{1... | collective-permute-start | bytes 2457608 | tf_op jit(solution)/shard_map/ppermute | solution.py:43
  36.7 6.9 %copy-start.2 = (bf16[2048,1024]{1,0:T(8,128)(2,1)S(1)}, bf16[2048,1024]{1,0:T(8,128)(2,1)}, u32[]{:S(2)}) copy-start(bf16[2048,1024]{1,0:T(8,128)(2,1)} %copy-done.1) | copy-start | bytes 12582916
  43.6 0.8 copy-start.11
  44.4 6.3 %copy-start.10 = (bf16[1,2048,1024]{2,1,0:T(8,128)(2,1)S(1)}, bf16[1,2048,1024]{2,1,0:T(8,128)(2,1)}, u32[]{:S(2)}) copy-start(bf16[1,2048,1024]{2,1,0:T(8,128)(2,1)} %param.10) | copy-start | bytes 12582916
  50.7 6.2 %copy-start.12 = (bf16[2048,1024]{1,0:T(8,128)(2,1)}, bf16[2048,1024]{1,0:T(8,128)(2,1)S(1)}, u32[]{:S(2)}) copy-start(bf16[2048,1024]{1,0:T(8,128)(2,1)S(1)} %get-tuple-element.23) | copy-start | bytes 12582916
  64.3 4.9 %collective-permute-start.3 = (f32[4,288,512]{2,1,0:T(8,128)}, f32[4,288,512]{2,1,0:T(8,128)}, u32[]{:S(2)}, u32[]{:S(2)}) collective-permute-start(f32[4,288,512]{2,1,0:T(8,128)} %fusion.5), channel_id=1, source_target_pairs={{0,32},{4,36},{8,40},{12,44},{64,96},{68,100},{72,104},{76,108},{1... | collective-permute-start | bytes 7077896 | tf_op jit(solution)/shard_map/ppermute | solution.py:43
  64.7 2.2 %copy-start.3 = (f32[4,288,512]{2,1,0:T(8,128)S(1)}, f32[4,288,512]{2,1,0:T(8,128)}, u32[]{:S(2)}) copy-start(f32[4,288,512]{2,1,0:T(8,128)} %get-tuple-element.14) | copy-start | bytes 7077892
  67.4 4.5 %copy-start.4 = (f32[4,288,512]{2,1,0:T(8,128)}, f32[4,288,512]{2,1,0:T(8,128)S(1)}, u32[]{:S(2)}) copy-start(f32[4,288,512]{2,1,0:T(8,128)S(1)} %fusion.6) | copy-start | bytes 7077892
  71.9 10.4 %collective-permute-start.4 = (f32[288,512]{1,0:T(8,128)}, f32[288,512]{1,0:T(8,128)S(1)}, u32[]{:S(2)}, u32[]{:S(2)}) collective-permute-start(f32[288,512]{1,0:T(8,128)} %get-tuple-element.11), channel_id=1, source_target_pairs={{0,4},{4,8},{8,12},{12,0},{64,68},{68,72},{72,76},{76,64},{16,20},... | collective-permute-start | bytes 1769480 | tf_op jit(solution)/shard_map/ppermute | solution.py:43
  73.3 9.2 %collective-permute-start.5 = (f32[288,512]{1,0:T(8,128)}, f32[288,512]{1,0:T(8,128)S(1)}, u32[]{:S(2)}, u32[]{:S(2)}) collective-permute-start(f32[288,512]{1,0:T(8,128)} %get-tuple-element.13), channel_id=1, source_target_pairs={{0,12},{4,0},{8,4},{12,8},{64,76},{68,64},{72,68},{76,72},{16,28},... | collective-permute-start | bytes 1769480 | tf_op jit(solution)/shard_map/ppermute | solution.py:43
  74.6 15.3 %collective-permute-start.6 = (f32[288,512]{1,0:T(8,128)}, f32[288,512]{1,0:T(8,128)}, u32[]{:S(2)}, u32[]{:S(2)}) collective-permute-start(f32[288,512]{1,0:T(8,128)} %get-tuple-element.12), channel_id=1, source_target_pairs={{0,8},{4,12},{8,0},{12,4},{64,72},{68,76},{72,64},{76,68},{16,24},... | collective-permute-start | bytes 1769480 | tf_op jit(solution)/shard_map/ppermute | solution.py:43
  82.5 0.8 copy-start.5
  92.6 6.2 %collective-permute-start.7 = (f32[72,512]{1,0:T(8,128)}, f32[72,512]{1,0:T(8,128)S(1)}, u32[]{:S(2)}, u32[]{:S(2)}) collective-permute-start(f32[72,512]{1,0:T(8,128)} %get-tuple-element.17), channel_id=1, source_target_pairs={{0,1},{4,5},{8,9},{12,13},{64,65},{68,69},{72,73},{76,77},{16,17},... | collective-permute-start | bytes 442376 | tf_op jit(solution)/shard_map/ppermute | solution.py:43
  93.9 4.9 %collective-permute-start.8 = (f32[72,512]{1,0:T(8,128)S(1)}, f32[72,512]{1,0:T(8,128)S(1)}, u32[]{:S(2)}, u32[]{:S(2)}) collective-permute-start(f32[72,512]{1,0:T(8,128)S(1)} %get-tuple-element.19), channel_id=1, source_target_pairs={{0,3},{4,7},{8,11},{12,15},{64,67},{68,71},{72,75},{76,79},{16,19}... | collective-permute-start | bytes 442376 | tf_op jit(solution)/shard_map/ppermute | solution.py:43
  96.0 5.5 %collective-permute-start.9 = (f32[72,512]{1,0:T(8,128)S(1)}, f32[72,512]{1,0:T(8,128)S(1)}, u32[]{:S(2)}, u32[]{:S(2)}) collective-permute-start(f32[72,512]{1,0:T(8,128)S(1)} %get-tuple-element.18), channel_id=1, source_target_pairs={{0,2},{4,6},{8,10},{12,14},{64,66},{68,70},{72,74},{76,78},{16,18}... | collective-permute-start | bytes 442376 | tf_op jit(solution)/shard_map/ppermute | solution.py:43
  101.6 5.3 %collective-permute-start.10 = (f32[72,512]{1,0:T(8,128)S(1)}, f32[72,512]{1,0:T(8,128)S(1)}, u32[]{:S(2)}, u32[]{:S(2)}) collective-permute-start(f32[72,512]{1,0:T(8,128)S(1)} %fusion.22), channel_id=1, source_target_pairs={{0,64},{4,68},{8,72},{12,76},{64,16},{68,20},{72,24},{76,28},{16,8... | collective-permute-start | bytes 442376 | tf_op jit(solution)/shard_map/ppermute | solution.py:43
  103.0 4.0 %collective-permute-start.11 = (f32[72,512]{1,0:T(8,128)S(1)}, f32[72,512]{1,0:T(8,128)S(1)}, u32[]{:S(2)}, u32[]{:S(2)}) collective-permute-start(f32[72,512]{1,0:T(8,128)S(1)} %fusion.22), channel_id=1, source_target_pairs={{0,80},{4,84},{8,88},{12,92},{64,0},{68,4},{72,8},{76,12},{16,64},... | collective-permute-start | bytes 442376 | tf_op jit(solution)/shard_map/ppermute | solution.py:43
  104.5 5.6 %collective-permute-start.12 = (f32[72,512]{1,0:T(8,128)S(1)}, f32[72,512]{1,0:T(8,128)S(1)}, u32[]{:S(2)}, u32[]{:S(2)}) collective-permute-start(f32[72,512]{1,0:T(8,128)S(1)} %fusion.22), channel_id=1, source_target_pairs={{0,16},{4,20},{8,24},{12,28},{64,80},{68,84},{72,88},{76,92},{16,0... | collective-permute-start | bytes 442376 | tf_op jit(solution)/shard_map/ppermute | solution.py:43
  110.1 4.4 %collective-permute-start.13 = (f32[72,512]{1,0:T(8,128)S(1)}, f32[72,512]{1,0:T(8,128)S(1)}, u32[]{:S(2)}, u32[]{:S(2)}) collective-permute-start(f32[72,512]{1,0:T(8,128)S(1)} %add_add_fusion), channel_id=1, source_target_pairs={{0,3},{4,7},{8,11},{12,15},{64,67},{68,71},{72,75},{76,79},{16,19}... | collective-permute-start | bytes 442376 | tf_op jit(solution)/shard_map/ppermute | solution.py:43
  111.6 5.6 %collective-permute-start.14 = (f32[72,512]{1,0:T(8,128)S(1)}, f32[72,512]{1,0:T(8,128)S(1)}, u32[]{:S(2)}, u32[]{:S(2)}) collective-permute-start(f32[72,512]{1,0:T(8,128)S(1)} %add_add_fusion), channel_id=1, source_target_pairs={{0,2},{4,6},{8,10},{12,14},{64,66},{68,70},{72,74},{76,78},{16,18}... | collective-permute-start | bytes 442376 | tf_op jit(solution)/shard_map/ppermute | solution.py:43
  112.8 5.9 %collective-permute-start.15 = (f32[72,512]{1,0:T(8,128)S(1)}, f32[72,512]{1,0:T(8,128)S(1)}, u32[]{:S(2)}, u32[]{:S(2)}) collective-permute-start(f32[72,512]{1,0:T(8,128)S(1)} %add_add_fusion), channel_id=1, source_target_pairs={{0,1},{4,5},{8,9},{12,13},{64,65},{68,69},{72,73},{76,77},{16,17},... | collective-permute-start | bytes 442376 | tf_op jit(solution)/shard_map/ppermute | solution.py:43
  119.6 11.9 %collective-permute-start.16 = (f32[288,512]{1,0:T(8,128)}, f32[288,512]{1,0:T(8,128)S(1)}, u32[]{:S(2)}, u32[]{:S(2)}) collective-permute-start(f32[288,512]{1,0:T(8,128)} %constant_dynamic-slice_fusion), channel_id=1, source_target_pairs={{0,4},{4,8},{8,12},{12,0},{64,68},{68,72},{72,76},{76,64},{16,20},... | collective-permute-start | bytes 1769480 | tf_op jit(solution)/shard_map/ppermute | solution.py:43
  120.7 17.6 %collective-permute-start.17 = (f32[288,512]{1,0:T(8,128)}, f32[288,512]{1,0:T(8,128)S(1)}, u32[]{:S(2)}, u32[]{:S(2)}) collective-permute-start(f32[288,512]{1,0:T(8,128)} %constant_dynamic-slice_fusion), channel_id=1, source_target_pairs={{0,8},{4,12},{8,0},{12,4},{64,72},{68,76},{72,64},{76,68},{16,24},... | collective-permute-start | bytes 1769480 | tf_op jit(solution)/shard_map/ppermute | solution.py:43
  124.3 21.4 %collective-permute-start.18 = (f32[288,512]{1,0:T(8,128)}, f32[288,512]{1,0:T(8,128)}, u32[]{:S(2)}, u32[]{:S(2)}) collective-permute-start(f32[288,512]{1,0:T(8,128)} %constant_dynamic-slice_fusion), channel_id=1, source_target_pairs={{0,12},{4,0},{8,4},{12,8},{64,76},{68,64},{72,68},{76,72},{16,28},... | collective-permute-start | bytes 1769480 | tf_op jit(solution)/shard_map/ppermute | solution.py:43
  124.4 36.2 %collective-permute-start.19 = (f32[288,512]{1,0:T(8,128)}, f32[288,512]{1,0:T(8,128)}, u32[]{:S(2)}, u32[]{:S(2)}) collective-permute-start(f32[288,512]{1,0:T(8,128)} %constant_dynamic-slice_fusion), channel_id=1, source_target_pairs={{0,32},{4,36},{8,40},{12,44},{64,96},{68,100},{72,104},{76,108},{1... | collective-permute-start | bytes 1769480 | tf_op jit(solution)/shard_map/ppermute | solution.py:43
  131.4 29.1 %collective-permute-start.20 = (f32[288,512]{1,0:T(8,128)S(1)}, f32[288,512]{1,0:T(8,128)}, u32[]{:S(2)}, u32[]{:S(2)}) collective-permute-start(f32[288,512]{1,0:T(8,128)S(1)} %collective-permute-done.16), channel_id=1, source_target_pairs={{0,32},{4,36},{8,40},{12,44},{64,96},{68,100},{72,104},{76,108},{1... | collective-permute-start | bytes 1769480 | tf_op jit(solution)/shard_map/ppermute | solution.py:43
  138.3 22.3 %collective-permute-start.21 = (f32[288,512]{1,0:T(8,128)S(1)}, f32[288,512]{1,0:T(8,128)}, u32[]{:S(2)}, u32[]{:S(2)}) collective-permute-start(f32[288,512]{1,0:T(8,128)S(1)} %collective-permute-done.17), channel_id=1, source_target_pairs={{0,32},{4,36},{8,40},{12,44},{64,96},{68,100},{72,104},{76,108},{1... | collective-permute-start | bytes 1769480 | tf_op jit(solution)/shard_map/ppermute | solution.py:43
  145.7 14.9 %collective-permute-start.22 = (f32[288,512]{1,0:T(8,128)}, f32[288,512]{1,0:T(8,128)}, u32[]{:S(2)}, u32[]{:S(2)}) collective-permute-start(f32[288,512]{1,0:T(8,128)} %collective-permute-done.18), channel_id=1, source_target_pairs={{0,32},{4,36},{8,40},{12,44},{64,96},{68,100},{72,104},{76,108},{1... | collective-permute-start | bytes 1769480 | tf_op jit(solution)/shard_map/ppermute | solution.py:43

commit v2 on v1

v2 whole, which is shorter than its diff:
```python
import functools
import math

import jax
import jax.numpy as jnp
from jax import lax
from jax.experimental import pallas as pl
from jax.experimental.pallas import tpu as pltpu
from jax.sharding import Mesh, PartitionSpec as P

DELTA = 0.05
ALL = ("ylo", "core", "yhi", "z", "x")
MIB = 1 << 20
F32, BF16 = jnp.float32, jnp.bfloat16


def flat(core, x, y, z):
    return ((y % 2) * 2 + core) * 32 + (y // 2) * 16 + z * 4 + x


def moved(where):
    pairs = []
    for core in range(2):
        for x in range(4):
            for y in range(4):
                for z in range(4):
                    pairs.append((flat(core, x, y, z), flat(*where(core, x, y, z))))
    return pairs


SWAP = moved(lambda c, x, y, z: (1 - c, x, y, z))
NEAR = moved(lambda c, x, y, z: (c, x, y ^ 1, z))


def first(k):
    return moved(lambda c, x, y, z: (c, x, y, (z + k) % 4) if c == 0 else (c, (x + k) % 4, y, z))


def second(k):
    return moved(lambda c, x, y, z: (c, x, y, (z + k) % 4) if c == 1 else (c, (x + k) % 4, y, z))


def along_y(k):
    return moved(lambda c, x, y, z: (c, x, (y + k) % 4, z))


def send(array, pairs):
    return lax.ppermute(array, ALL, pairs)


def grad_sum(own, sibling):
    core, x, z = lax.axis_index("core"), lax.axis_index("x"), lax.axis_index("z")
    place = jnp.where(core == 0, x, z)
    got = send(sibling, SWAP)
    held = [own[k] + got[k] for k in range(4)]
    block = held[0]
    for k in (1, 3, 2):
        block = block + send(held[k], first(k))
    rows = block.shape[0] // 4
    quarters = block.reshape((4, rows) + block.shape[1:])
    pick = lambda k: lax.dynamic_index_in_dim(quarters, (place + k) % 4, 0, keepdims=False)
    quarter = pick(0)
    for k in (1, 3, 2):
        quarter = quarter + send(pick(k), second(k))
    quarter = quarter + send(quarter, along_y(1)) + send(quarter, along_y(3)) + send(quarter, along_y(2))
    came = [quarter] + [send(quarter, second(k)) for k in (1, 2, 3)]
    twice = jnp.concatenate([came[3], came[2], came[1], came[0], came[3], came[2], came[1]], 0)
    block = lax.dynamic_slice_in_dim(twice, ((3 - place) % 4) * rows, 4 * rows, 0)
    mine = [block] + [send(block, first(k)) for k in (1, 2, 3)]
    return mine, [send(m, SWAP) for m in mine]


def params(mib):
    return pltpu.CompilerParams(vmem_limit_bytes=mib * MIB)


def cost(flops, moved_bytes, trans=0):
    return pl.CostEstimate(flops=flops, bytes_accessed=moved_bytes, transcendentals=trans)


def forward_kernel(lat, w, b_hid, w_out, b_out, *refs):
    pred, hid, slope_out = refs[-3:]
    pre = jnp.dot(lat[...], w[...], preferred_element_type=F32) + b_hid[...]
    sig = jax.nn.sigmoid(pre)
    h = (pre * sig).astype(BF16)
    hid[...] = h
    slope_out[...] = sig * (1.0 + pre * (1.0 - sig))
    turned = lax.dot_general(h, w_out[...], (((1,), (1,)), ((), ())), preferred_element_type=F32)
    pred[...] = jnp.transpose(turned + b_out[...])


def forward(part, parts, tile, latent, w_hidden, b_hidden, w_output, b_output, held):
    points, depth = latent.shape
    width, n_vars = w_hidden.shape[1], w_output.shape[0]
    n = points // parts
    steps = n // tile
    whole = lambda shape: pl.BlockSpec(shape, lambda g: (0,) * len(shape))
    rows = lambda cols: pl.BlockSpec((tile, cols), lambda g: (part * steps + g, 0))
    return pl.pallas_call(
        forward_kernel,
        grid=(steps,),
        in_specs=[rows(depth), whole(w_hidden.shape), whole((1, width)), whole(w_output.shape), whole((1, n_vars))]
        + [pl.BlockSpec(memory_space=pl.ANY)] * len(held),
        out_specs=[pl.BlockSpec((n_vars, tile), lambda g: (0, g)), rows(width), rows(width)],
        out_shape=[
            jax.ShapeDtypeStruct((n_vars, n), F32),
            jax.ShapeDtypeStruct((points, width), BF16),
            jax.ShapeDtypeStruct((points, width), F32),
        ],
        input_output_aliases={5: 1, 6: 2} if held else {},
        compiler_params=params(40),
        cost_estimate=cost(2 * n * width * (depth + n_vars), n * (2 * depth + 6 * width) + 2 * depth * width, 2 * n * width),
    )(latent, w_hidden, b_hidden.reshape(1, width), w_output, b_output.reshape(1, n_vars), *held)


def turn_kernel(a, _, out):
    out[...] = jnp.transpose(a[...])


def turn(a, after):
    rows, cols = a.shape
    br, bc = 1024, 256
    return pl.pallas_call(
        turn_kernel,
        grid=(cols // bc, rows // br),
        in_specs=[pl.BlockSpec((br, bc), lambda i, j: (j, i)), pl.BlockSpec(memory_space=pl.ANY)],
        out_specs=pl.BlockSpec((bc, br), lambda i, j: (i, j)),
        out_shape=jax.ShapeDtypeStruct((cols, rows), a.dtype),
        compiler_params=params(40),
        cost_estimate=cost(0, 4 * rows * cols),
    )(a, after)


def cot_kernel(members, loss_scale, pair_coef, own, o1, o2, o3, target, area, var, *refs):
    cot, turned, misc, pad = refs[-4:]
    n_vars = own.shape[0]
    weights = var[...] * area[...]
    mine = own[...]

    def both(diff):
        u = diff * diff + DELTA * DELTA
        r = lax.rsqrt(u)
        return u * r - DELTA, diff * r

    mag, slo = both(mine - target[...])
    pair_mag, pair_slo = jnp.zeros_like(mine), jnp.zeros_like(mine)
    for other in (o1, o2, o3):
        m, s = both(mine - other[...])
        pair_mag, pair_slo = pair_mag + m, pair_slo + s
    term = weights * (mag * (1.0 / members) - (0.5 * pair_coef) * pair_mag)
    rounded = (weights * (slo * (1.0 / members) - pair_coef * pair_slo)).astype(BF16)
    cot[...] = rounded
    pad[...] = jnp.zeros_like(pad)
    pad[0:n_vars, :] = rounded.astype(F32)
    t = jnp.transpose(pad[...])
    turned[...] = t.astype(BF16)
    lane = lax.broadcasted_iota(jnp.int32, (1, 128), 1)
    sums = jnp.sum(t, axis=0, keepdims=True) + jnp.where(lane == n_vars, jnp.sum(term) * loss_scale, 0.0)

    @pl.when(pl.program_id(0) == 0)
    def _():
        misc[...] = jnp.zeros_like(misc)

    misc[...] += sums


def cotangent(part, parts, tile, own, others, target, area, var, held, members, loss_scale, pair_coef):
    n_vars, points = target.shape
    n = points // parts
    steps = n // tile
    local = pl.BlockSpec((n_vars, tile), lambda g: (0, g))
    placed = pl.BlockSpec((n_vars, tile), lambda g: (0, part * steps + g))
    return pl.pallas_call(
        functools.partial(cot_kernel, members, loss_scale, pair_coef),
        grid=(steps,),
        in_specs=[local] * 4
        + [placed, pl.BlockSpec((1, tile), lambda g: (0, part * steps + g)), pl.BlockSpec((n_vars, 1), lambda g: (0, 0))]
        + [pl.BlockSpec(memory_space=pl.ANY)] * len(held),
        out_specs=[
            placed,
            pl.BlockSpec((tile, 128), lambda g: (part * steps + g, 0)),
            pl.BlockSpec((1, 128), lambda g: (0, 0)),
        ],
        out_shape=[
            jax.ShapeDtypeStruct((n_vars, points), BF16),
            jax.ShapeDtypeStruct((points, 128), BF16),
            jax.ShapeDtypeStruct((1, 128), F32),
        ],
        scratch_shapes=[pltpu.VMEM((128, tile), F32)],
        input_output_aliases={7: 0, 8: 1} if held else {},
        compiler_params=params(40),
        cost_estimate=cost(60 * n * n_vars, n * n_vars * 24, 4 * n * n_vars),
    )(own, *others, target, area, var, *held)


def backward_kernel(scale, chunks, where, cot, turned, sp, hid, w_out, lat, misc0, misc1, dpre, out, dall, rest):
    g = pl.program_id(0)
    n_vars, tile = cot.shape
    row = lax.broadcasted_iota(jnp.int32, rest.shape, 0)

    @pl.when(g == 0)
    def _():
        m = jnp.concatenate([misc0[...] + misc1[...]] * (rest.shape[1] // 128), axis=1)
        kept = jnp.where(lax.broadcasted_iota(jnp.int32, m.shape, 1) == n_vars, m, m * scale)
        rest[...] = jnp.where(row == n_vars + 1, kept, 0.0)

    @pl.when(g < chunks)
    def _():
        back = jnp.dot(turned[...], w_out[...], preferred_element_type=F32)
        d = (back * sp[...]).astype(BF16)
        dall[pl.ds(pl.multiple_of(g * tile, tile), tile), :] = d
        dpre[...] = d
        rest[0:n_vars, :] += jnp.dot(cot[...], hid[...], preferred_element_type=F32) * scale
        rest[n_vars : n_vars + 1, :] += jnp.sum(d.astype(F32), axis=0, keepdims=True) * scale

    @pl.when(g >= chunks)
    def _():
        block = lax.rem(where[1] + g - chunks, 4)
        rows = lat.shape[0]
        out[0, 0:rows, :] = jnp.dot(lat[...], dall[...], preferred_element_type=F32) * scale
        out[0, rows : rows + 32, :] = rest[pl.ds(pl.multiple_of(block * 32, 32), 32), :]


def backward(which, place, cot, turned, sp, hid, w_out, lat_t, misc, scale, tile=512):
    n_vars, points = cot.shape
    depth, width = lat_t.shape[0], hid.shape[1]
    half, rows, chunks = width // 2, depth // 4, points // tile
    at = lambda g: jnp.minimum(g, chunks - 1)
    step = lambda g: jnp.maximum(g - chunks, 0)
    return pl.pallas_call(
        functools.partial(backward_kernel, scale, chunks),
        grid_spec=pltpu.PrefetchScalarGridSpec(
            num_scalar_prefetch=1,
            grid=(chunks + 4,),
            in_specs=[
                pl.BlockSpec((n_vars, tile), lambda g, s: (0, at(g))),
                pl.BlockSpec((tile, 128), lambda g, s: (at(g), 0)),
                pl.BlockSpec((tile, half), lambda g, s: (at(g), s[0])),
                pl.BlockSpec((tile, half), lambda g, s: (at(g), s[0])),
                pl.BlockSpec((128, half), lambda g, s: (0, s[0])),
                pl.BlockSpec((rows, points), lambda g, s: (lax.rem(s[1] + step(g), 4), 0)),
                pl.BlockSpec((1, 128), lambda g, s: (0, 0)),
                pl.BlockSpec((1, 128), lambda g, s: (0, 0)),
            ],
            out_specs=[
                pl.BlockSpec((tile, half), lambda g, s: (at(g), 0)),
                pl.BlockSpec((1, rows + 32, half), lambda g, s: (step(g), 0, 0)),
            ],
            scratch_shapes=[pltpu.VMEM((points, half), BF16), pltpu.VMEM((128, half), F32)],
        ),
        out_shape=[
            jax.ShapeDtypeStruct((points, half), BF16),
            jax.ShapeDtypeStruct((4, rows + 32, half), F32),
        ],
        compiler_params=params(40),
        cost_estimate=cost(2 * points * half * (depth + 2 * n_vars), points * (8 * half + 2 * depth), 0),
    )(jnp.stack([which, place]).astype(jnp.int32), cot, turned, sp, hid, w_out, lat_t, *misc)


def latent_kernel(where, d0, d1, w0, w1, out):
    dims = (((1,), (1,)), ((), ()))
    out[0] = (
        lax.dot_general(d0[...], w0[...], dims, preferred_element_type=F32)
        + lax.dot_general(d1[...], w1[...], dims, preferred_element_type=F32)
    ).astype(BF16)


def latent_gradient(core, dpre_own, dpre_sib, w_hidden, tile=512):
    points, half = dpre_own.shape
    depth = w_hidden.shape[0]
    rows = pl.BlockSpec((tile, half), lambda g, s: (g, 0))
    return pl.pallas_call(
        latent_kernel,
        grid_spec=pltpu.PrefetchScalarGridSpec(
            num_scalar_prefetch=1,
            grid=(points // tile,),
            in_specs=[
                rows,
                rows,
                pl.BlockSpec((depth, half), lambda g, s: (0, s[0])),
                pl.BlockSpec((depth, half), lambda g, s: (0, 1 - s[0])),
            ],
            out_specs=pl.BlockSpec((1, tile, depth), lambda g, s: (0, g, 0)),
        ),
        out_shape=jax.ShapeDtypeStruct((1, points, depth), BF16),
        compiler_params=params(40),
        cost_estimate=cost(4 * points * half * depth, points * (4 * half + 2 * depth) + 4 * depth * half, 0),
    )(core[None].astype(jnp.int32), dpre_own, dpre_sib, w_hidden, w_hidden)


def join_kernel(n_vars, where, *refs):
    ins, (grad_w, grad_o, grad_b, misc, rest) = refs[:8], refs[8:]
    rows, half = ins[0].shape[0] - 32, ins[0].shape[1]
    for which in range(2):
        col = where[0] if which == 0 else 1 - where[0]
        cols = pl.ds(pl.multiple_of(col * half, half), half)
        for k in range(4):
            block = lax.rem(where[1 + which] - k + 4, 4)
            grad_w[pl.ds(pl.multiple_of(block * rows, rows), rows), cols] = ins[4 * which + k][0:rows, :]
            rest[pl.ds(pl.multiple_of(block * 32, 32), 32), cols] = ins[4 * which + k][rows : rows + 32, :]
    grad_o[...] = rest[0:n_vars, :]
    grad_b[...] = rest[n_vars : n_vars + 1, :]
    misc[...] = rest[n_vars + 1 : n_vars + 2, 0:128]


def join(core, place_own, place_sib, own, sib, n_vars):
    rows, half = own[0].shape
    depth, width = 4 * (rows - 32), 2 * half
    vmem = pl.BlockSpec(memory_space=pltpu.VMEM)
    return pl.pallas_call(
        functools.partial(join_kernel, n_vars),
        in_specs=[pl.BlockSpec(memory_space=pltpu.SMEM)] + [vmem] * 8,
        out_specs=[vmem] * 4,
        out_shape=[
            jax.ShapeDtypeStruct((depth, width), F32),
            jax.ShapeDtypeStruct((n_vars, width), F32),
            jax.ShapeDtypeStruct((1, width), F32),
            jax.ShapeDtypeStruct((1, 128), F32),
        ],
        scratch_shapes=[pltpu.VMEM((128, width), F32)],
        compiler_params=params(40),
        cost_estimate=cost(0, 8 * depth * width, 0),
    )(jnp.stack([core, place_own, place_sib]).astype(jnp.int32), *own, *sib)


def shards(latent, target, area_weight, var_weight, w_hidden, b_hidden, w_output, b_output):
    members, parts, tile = 4, 2, 512
    n_vars, points = target.shape
    points_all = points * 32
    eps = 0.05 / members
    pair_coef = (1.0 - eps) / (members * (members - 1))
    scale = 1.0 / math.sqrt(members * points_all)
    core, x, z = lax.axis_index("core"), lax.axis_index("x"), lax.axis_index("z")
    place_own = jnp.where(core == 0, z, x)
    place_sib = jnp.where(core == 0, x, z)
    own_latent = latent[0]
    preds, held = [], ()
    for part in range(parts):
        pred, *held = forward(part, parts, tile, own_latent, w_hidden, b_hidden, w_output, b_output, held)
        preds.append(pred)
    hid, sp = held
    near = [send(p, NEAR) for p in preds]
    sibling = [send(p, SWAP) for p in preds]
    near_sibling = [send(p, SWAP) for p in near]
    lat_t = turn(own_latent, preds[-1])
    area, var = area_weight.reshape(1, points), var_weight.reshape(n_vars, 1)
    w_padded = jnp.pad(w_output, ((0, 128 - n_vars), (0, 0)))
    held, misc = (), []
    for part in range(parts):
        others = (sibling[part], near[part], near_sibling[part])
        *held, m = cotangent(
            part, parts, tile, preds[part], others, target, area, var, held, members, 1.0 / (points_all * n_vars), pair_coef
        )
        misc.append(m)
    cot, turned = held
    dpre_sib, blocks_sib = backward(1 - core, place_sib, cot, turned, sp, hid, w_padded, lat_t, misc, scale)
    dpre_own, blocks_own = backward(core, place_own, cot, turned, sp, hid, w_padded, lat_t, misc, scale)
    out_own, out_sib = grad_sum(blocks_own, blocks_sib)
    latent_grad = latent_gradient(core, dpre_own, dpre_sib, w_hidden)
    grad_w_hidden, grad_w_output, grad_b_hidden, last = join(core, place_own, place_sib, out_own, out_sib, n_vars)
    return (
        last[0, n_vars],
        grad_w_hidden,
        grad_b_hidden[0],
        grad_w_output,
        last[0, :n_vars],
        latent_grad,
    )


def solution(mesh):
    fine = Mesh(mesh.devices.reshape(2, 2, 2, 4, 4), ALL)
    member, space = ("ylo", "core"), ("yhi", "z", "x")
    return jax.shard_map(
        shards,
        mesh=fine,
        in_specs=(P(member, space, None), P(None, space), P(space), P(), P(), P(), P(), P()),
        out_specs=(P(), P(), P(), P(), P(), P(member, space, None)),
        check_vma=False,
    )
```

time: 176 us -> 150 us (0.85)
  Pallas kernels: 0 us -> 40.6 us
  matrix products: 33.3 us -> 0 us
  other arithmetic: 28 us -> 3.63 us
  waiting for transfers between devices: 48.2 us -> 35.2 us
  local copies, waits for them, and re-layouts: 17.1 us -> 19.9 us
  starting transfers between devices: 47.4 us -> 49.7 us
    pallas_call x0 -> x9, Pallas kernels: none -> 40.6 us  [the longest x2 15 us: backward(): pl.pallas_call(functools.partial(backward_kernel, scale, chunks), grid_sp...]
    dot_general x6 -> x0, matrix products: 33.3 us -> none  [the longest x1 10.3 us: shards(): jnp.dot(own_latent, w_hidden, preferred_element_type=jnp.float32) + b_hidden]
    unnamed x32 -> x48, local copies, waits for them, and re-layouts: 3.45 us -> 17.9 us
    ppermute x23 -> x26, waiting for transfers between devices: 48.2 us -> 35.2 us  [send(): return lax.ppermute(array, ALL, pairs)]
    concatenate x6 -> x0, other arithmetic: 9.55 us -> none  [the longest x1 4.36 us: shards(): jnp.concatenate([part_w_hidden.reshape(4, depth // 4, width), rest.reshap...]
    gather x2 -> x0, local copies, waits for them, and re-layouts: 7.57 us -> none  [in_place(): return jnp.take(jnp.stack(outs), (place - jnp.arange(4)) % 4, axis=0)]
    another operation x2, other arithmetic: 5.99 us -> 0.16 us  [the longest x1 0.08 us: backward(): jnp.stack([which, place]).astype(jnp.int32)]
    reduce_sum x1 -> x0, other arithmetic: 4.58 us -> none  [shards(): part_b_output = jnp.sum(cot.astype(jnp.float32), axis=1) * scale]
  transfers between devices with their start and end apart: 23 -> 26, of which waited for: 13 -> 13; matrix products, arithmetic and copies ran while one was open for 10% -> 0% of each run, Pallas kernels for 0% -> 15%
where the time goes in v2:
time: 150 us
  starting transfers between devices  49.7 us (33%)
  Pallas kernels  40.6 us (27%)
  waiting for transfers between devices  35.2 us (23%)
  local copies, waits for them, and re-layouts  19.9 us (13%)
  other arithmetic  3.63 us (2%)
    ppermute x26, starting transfers between devices, send(): return lax.ppermute(array, ALL, pairs)  49.7 us
    ppermute x26, waiting for transfers between devices, send(): return lax.ppermute(array, ALL, pairs)  35.2 us
    unnamed x48, local copies, waits for them, and re-layouts  17.9 us
    pallas_call x2, Pallas kernels, backward(): pl.pallas_call(functools.partial(backward_kernel, scale, chunks), grid_sp...  15 us
    pallas_call x2, Pallas kernels, forward(): pl.pallas_call(forward_kernel, grid=(steps,), in_specs=[rows(depth), whol...  10.3 us
    pallas_call x1, Pallas kernels, latent_gradient(): pl.pallas_call(latent_kernel, grid_spec=pltpu.PrefetchScalarGridSpec(num_...  6.31 us
    pallas_call x2, Pallas kernels, cotangent(): pl.pallas_call(functools.partial(cot_kernel, members, loss_scale, pair_co...  3.45 us
  transfers between devices with their start and end apart: 26, of which 13 were waited for; matrix products, arithmetic and copies ran while one was open for 0% of the time, Pallas kernels for 15%

profile of v2, /device:TPU:1, one launch (start us, length us, event | category | flops | bytes accessed | tf_op | source)
XLA Modules:
  0.0 150.0 jit_solution(1576170127101299878)
XLA Ops:
  0.6 2.2 %copy-done.4 = bf16[1,2048,1024]{2,1,0:T(8,128)(2,1)S(1)} copy-done((bf16[1,2048,1024]{2,1,0:T(8,128)(2,1)S(1)}, bf16[1,2048,1024]{2,1,0:T(8,128)(2,1)}, u32[]{:S(2)}) %copy-start.4) | copy-done | bytes 4194328
  2.8 1.6 %copy-done.7 = bf16[1024,1024]{1,0:T(8,128)(2,1)S(1)} copy-done((bf16[1024,1024]{1,0:T(8,128)(2,1)S(1)}, bf16[1024,1024]{1,0:T(8,128)(2,1)}, u32[]{:S(2)}) %copy-start.7) | copy-done | bytes 2097176
  4.4 0.9 copy-done.9
  6.7 5.1 %shard_map.127 = (f32[100,1024]{1,0:T(8,128)S(1)}, bf16[2048,1024]{1,0:T(8,128)(2,1)S(1)}, f32[2048,1024]{1,0:T(8,128)}) custom-call(bf16[2048,1024]{1,0:T(8,128)(2,1)S(1)} %bitcast.40, bf16[1024,1024]{1,0:T(8,128)(2,1)S(1)} %copy-done.7, f32[1,1024]{1,0:T(1,128)S(1)} %bitcast.45, bf16[100,1024]{1,0:T(8,128)(2,1)S(1)} %copy-done.9, f32[1,100]{1,0:T(1,128)S(1)} %bitcast.47), custom_call_target="tpu_custom_call" | custom-call | flops 2357198848 | bytes 10485760 | tf_op jit(solution)/shard_map/pallas_call | solution.py:99
  11.8 2.1 %collective-permute-start.4 = (f32[100,1024]{1,0:T(8,128)S(1)}, f32[100,1024]{1,0:T(8,128)S(1)}, u32[]{:S(2)}, u32[]{:S(2)}) collective-permute-start(f32[100,1024]{1,0:T(8,128)S(1)} %get-tuple-element.29.own), channel_id=1, source_target_pairs={{0,64},{4,68},{8,72},{12,76},{64,0},{68,4},{72,8},{76,12},{16,80},... | collective-permute-start | bytes 1228808 | tf_op jit(solution)/shard_map/ppermute | solution.py:48
  14.0 5.2 %shard_map.128 = (f32[100,1024]{1,0:T(8,128)S(1)}, bf16[2048,1024]{1,0:T(8,128)(2,1)S(1)}, f32[2048,1024]{1,0:T(8,128)}) custom-call(bf16[2048,1024]{1,0:T(8,128)(2,1)S(1)} %bitcast.41, bf16[1024,1024]{1,0:T(8,128)(2,1)S(1)} %copy-done.7, f32[1,1024]{1,0:T(1,128)S(1)} %bitcast.46, ...), custom_call_target="tpu_custom_call", output_to_operand_aliasing={{1}: (5, {}), {2}: (6, {})} | custom-call | flops 2357198848 | bytes 10485760 | tf_op jit(solution)/shard_map/pallas_call | solution.py:99
  19.1 2.0 %copy-done.2 = bf16[2048,1024]{1,0:T(8,128)(2,1)} copy-done((bf16[2048,1024]{1,0:T(8,128)(2,1)}, bf16[2048,1024]{1,0:T(8,128)(2,1)S(1)}, u32[]{:S(2)}) %copy-start.2) | copy-done | bytes 4194328
  21.1 1.3 collective-permute-start.3
  23.1 2.1 %collective-permute-start.5 = (f32[100,1024]{1,0:T(8,128)S(1)}, f32[100,1024]{1,0:T(8,128)S(1)}, u32[]{:S(2)}, u32[]{:S(2)}) collective-permute-start(f32[100,1024]{1,0:T(8,128)S(1)} %collective-permute-done.4.o2), channel_id=1, source_target_pairs={{0,32},{4,36},{8,40},{12,44},{64,96},{68,100},{72,104},{76,108},{1... | collective-permute-start | bytes 1228808 | tf_op jit(solution)/shard_map/ppermute | solution.py:48
  25.1 7.4 %collective-permute-done.1.o2 = f32[100,1024]{1,0:T(8,128)} collective-permute-done((f32[100,1024]{1,0:T(8,128)S(1)}, f32[100,1024]{1,0:T(8,128)}, u32[]{:S(2)}, u32[]{:S(2)}) %collective-permute-start.1) | collective-permute-done | bytes 409632 | tf_op jit(solution)/shard_map/ppermute | solution.py:48
  32.6 1.4 collective-permute-start.2
  34.0 2.2 %copy-done.5 = bf16[1,2048,1024]{2,1,0:T(8,128)(2,1)S(1)} copy-done((bf16[1,2048,1024]{2,1,0:T(8,128)(2,1)S(1)}, bf16[1,2048,1024]{2,1,0:T(8,128)(2,1)}, u32[]{:S(2)}) %copy-start.5) | copy-done | bytes 4194328
  36.2 2.6 %shard_map.131.lat = bf16[1024,2048]{1,0:T(8,128)(2,1)S(1)} custom-call(bf16[2048,1024]{1,0:T(8,128)(2,1)S(1)} %bitcast.42, f32[100,1024]{1,0:T(8,128)S(1)} %get-tuple-element.28.own._), custom_call_target="tpu_custom_call" | custom-call | bytes 8388608 | tf_op jit(solution)/shard_map/pallas_call | solution.py:123
  38.8 2.0 %copy-done = bf16[1024,2048]{1,0:T(8,128)(2,1)} copy-done((bf16[1024,2048]{1,0:T(8,128)(2,1)}, bf16[1024,2048]{1,0:T(8,128)(2,1)S(1)}, u32[]{:S(2)}) %copy-start) | copy-done | bytes 4194328
  41.0 1.2 shard_map.129
  42.3 2.2 %shard_map.130 = (bf16[100,2048]{1,0:T(8,128)(2,1)S(1)}, bf16[2048,128]{1,0:T(8,128)(2,1)S(1)}, f32[1,128]{1,0:T(1,128)S(1)}) custom-call(f32[100,1024]{1,0:T(8,128)S(1)} %get-tuple-element.28.own._, f32[100,1024]{1,0:T(8,128)} %collective-permute-done.o1, f32[100,1024]{1,0:T(8,128)} %collective-permute-done.1.o2, ...), custom_call_target="tpu_custom_call", output_to_operand_aliasing={{0}: (7, {}), {1}: (8, {})} | custom-call | flops 6144000 | bytes 2457600 | tf_op jit(solution)/shard_map/pallas_call | solution.py:173
  44.5 2.2 %copy-done.3 = bf16[2048,1024]{1,0:T(8,128)(2,1)S(1)} copy-done((bf16[2048,1024]{1,0:T(8,128)(2,1)S(1)}, bf16[2048,1024]{1,0:T(8,128)(2,1)}, u32[]{:S(2)}) %copy-start.3) | copy-done | bytes 4194328
  46.7 7.5 %shard_map.133 = (bf16[2048,512]{1,0:T(8,128)(2,1)S(1)}, f32[4,288,512]{2,1,0:T(8,128)S(1)}) custom-call(s32[2]{0:T(128)S(1)} %get-tuple-element.53.where, bf16[100,2048]{1,0:T(8,128)(2,1)S(1)} %get-tuple-element.32.cot, bf16[2048,128]{1,0:T(8,128)(2,1)S(1)} %get-tuple-element.33.turned, f32[2048,1024]{1,0:T(8,128)} %get-tuple-element.34.sp, ...), custom_call_target="tpu_custom_call" | custom-call | flops 2566914048 | bytes 12582912 | tf_op jit(solution)/shard_map/pallas_call | solution.py:230
  54.3 7.5 %shard_map.132 = (bf16[2048,512]{1,0:T(8,128)(2,1)S(1)}, f32[4,288,512]{2,1,0:T(8,128)S(1)}) custom-call(s32[2]{0:T(128)S(1)} %get-tuple-element.52.where, bf16[100,2048]{1,0:T(8,128)(2,1)S(1)} %get-tuple-element.32.cot, bf16[2048,128]{1,0:T(8,128)(2,1)S(1)} %get-tuple-element.33.turned, f32[2048,1024]{1,0:T(8,128)} %get-tuple-element.34.sp, ...), custom_call_target="tpu_custom_call" | custom-call | flops 2566914048 | bytes 12582912 | tf_op jit(solution)/shard_map/pallas_call | solution.py:230
  61.9 1.6 %fusion.2 = (f32[288,512]{1,0:T(8,128)}, f32[288,512]{1,0:T(8,128)}, f32[288,512]{1,0:T(8,128)}) fusion(f32[4,288,512]{2,1,0:T(8,128)S(1)} %collective-permute-done.6, f32[4,288,512]{2,1,0:T(8,128)S(1)} %get-tuple-element.38), kind=kLoop, calls=%fused_computation.5 | loop fusion | flops 442368 | bytes 5308416 | tf_op jit(solution)/shard_map/add | solution.py:55
  64.5 1.4 collective-permute-start.7
  65.9 1.3 collective-permute-start.8
  67.2 1.7 %collective-permute-start.9 = (f32[288,512]{1,0:T(8,128)}, f32[288,512]{1,0:T(8,128)}, u32[]{:S(2)}, u32[]{:S(2)}) collective-permute-start(f32[288,512]{1,0:T(8,128)} %get-tuple-element.47), channel_id=1, source_target_pairs={{0,8},{4,12},{8,0},{12,4},{64,72},{68,76},{72,64},{76,68},{16,24},... | collective-permute-start | bytes 1769480 | tf_op jit(solution)/shard_map/ppermute | solution.py:48
  68.9 6.1 %collective-permute-done.7 = f32[288,512]{1,0:T(8,128)S(1)} collective-permute-done((f32[288,512]{1,0:T(8,128)}, f32[288,512]{1,0:T(8,128)S(1)}, u32[]{:S(2)}, u32[]{:S(2)}) %collective-permute-start.7) | collective-permute-done | bytes 589856 | tf_op jit(solution)/shard_map/ppermute | solution.py:48
  75.9 6.6 %collective-permute-done.9 = f32[288,512]{1,0:T(8,128)} collective-permute-done((f32[288,512]{1,0:T(8,128)}, f32[288,512]{1,0:T(8,128)}, u32[]{:S(2)}, u32[]{:S(2)}) %collective-permute-start.9) | collective-permute-done | bytes 589856 | tf_op jit(solution)/shard_map/ppermute | solution.py:48
  82.5 1.7 %fusion.6 = f32[288,512]{1,0:T(8,128)S(1)} fusion(f32[288,512]{1,0:T(8,128)} %collective-permute-done.9, f32[288,512]{1,0:T(8,128)} %copy-done.19, f32[288,512]{1,0:T(8,128)S(1)} %collective-permute-done.7, f32[4,288,512]{2,1,0:T(8,128)} %copy-done.18, f32[4,288,512]{2,1,0:T(8,128)S(1)} %get-tuple-element.38), kind=kLoop, calls=%fused_computation.10 | loop fusion | flops 589824 | bytes 3538944 | tf_op jit(solution)/shard_map/add | solution.py:58
  85.0 1.3 collective-permute-start.10
  86.3 2.1 %collective-permute-start.11 = (f32[72,512]{1,0:T(8,128)S(1)}, f32[72,512]{1,0:T(8,128)S(1)}, u32[]{:S(2)}, u32[]{:S(2)}) collective-permute-start(f32[72,512]{1,0:T(8,128)S(1)} %get-tuple-element.51), channel_id=1, source_target_pairs={{0,3},{4,7},{8,11},{12,15},{64,67},{68,71},{72,75},{76,79},{16,19}... | collective-permute-start | bytes 442376 | tf_op jit(solution)/shard_map/ppermute | solution.py:48
  88.4 1.3 collective-permute-start.12
  89.8 1.4 collective-permute-done.10
  91.2 2.8 %collective-permute-done.12 = f32[72,512]{1,0:T(8,128)S(1)} collective-permute-done((f32[72,512]{1,0:T(8,128)S(1)}, f32[72,512]{1,0:T(8,128)S(1)}, u32[]{:S(2)}, u32[]{:S(2)}) %collective-permute-start.12) | collective-permute-done | bytes 147488 | tf_op jit(solution)/shard_map/ppermute | solution.py:48
  94.0 1.4 collective-permute-start.13
  95.3 1.7 %collective-permute-start.14 = (f32[72,512]{1,0:T(8,128)S(1)}, f32[72,512]{1,0:T(8,128)S(1)}, u32[]{:S(2)}, u32[]{:S(2)}) collective-permute-start(f32[72,512]{1,0:T(8,128)S(1)} %fusion.8), channel_id=1, source_target_pairs={{0,80},{4,84},{8,88},{12,92},{64,0},{68,4},{72,8},{76,12},{16,64},... | collective-permute-start | bytes 442376 | tf_op jit(solution)/shard_map/ppermute | solution.py:48
  97.1 1.4 collective-permute-start.15
  99.3 3.3 %collective-permute-done.15 = f32[72,512]{1,0:T(8,128)S(1)} collective-permute-done((f32[72,512]{1,0:T(8,128)S(1)}, f32[72,512]{1,0:T(8,128)S(1)}, u32[]{:S(2)}, u32[]{:S(2)}) %collective-permute-start.15) | collective-permute-done | bytes 147488 | tf_op jit(solution)/shard_map/ppermute | solution.py:48
  102.7 1.4 collective-permute-start.16
  104.1 1.3 collective-permute-start.17
  105.5 1.6 %collective-permute-done.16 = f32[72,512]{1,0:T(8,128)S(1)} collective-permute-done((f32[72,512]{1,0:T(8,128)S(1)}, f32[72,512]{1,0:T(8,128)S(1)}, u32[]{:S(2)}, u32[]{:S(2)}) %collective-permute-start.16) | collective-permute-done | bytes 147488 | tf_op jit(solution)/shard_map/ppermute | solution.py:48
  107.1 2.6 %collective-permute-done.17 = f32[72,512]{1,0:T(8,128)S(1)} collective-permute-done((f32[72,512]{1,0:T(8,128)S(1)}, f32[72,512]{1,0:T(8,128)S(1)}, u32[]{:S(2)}, u32[]{:S(2)}) %collective-permute-start.17) | collective-permute-done | bytes 147488 | tf_op jit(solution)/shard_map/ppermute | solution.py:48
  109.7 1.5 %collective-permute-done.18 = f32[72,512]{1,0:T(8,128)S(1)} collective-permute-done((f32[72,512]{1,0:T(8,128)S(1)}, f32[72,512]{1,0:T(8,128)S(1)}, u32[]{:S(2)}, u32[]{:S(2)}) %collective-permute-start.18) | collective-permute-done | bytes 147488 | tf_op jit(solution)/shard_map/ppermute | solution.py:48
  111.4 1.2 collective-permute-start.19
  112.6 3.6 %collective-permute-start.20 = (f32[288,512]{1,0:T(8,128)S(1)}, f32[288,512]{1,0:T(8,128)S(1)}, u32[]{:S(2)}, u32[]{:S(2)}) collective-permute-start(f32[288,512]{1,0:T(8,128)S(1)} %constant_dynamic-slice_fusion.refs_0_), channel_id=1, source_target_pairs={{0,8},{4,12},{8,0},{12,4},{64,72},{68,76},{72,64},{76,68},{16,24},... | collective-permute-start | bytes 1769480 | tf_op jit(solution)/shard_map/ppermute | solution.py:48
  116.2 7.2 %collective-permute-start.22 = (f32[288,512]{1,0:T(8,128)S(1)}, f32[288,512]{1,0:T(8,128)S(1)}, u32[]{:S(2)}, u32[]{:S(2)}) collective-permute-start(f32[288,512]{1,0:T(8,128)S(1)} %constant_dynamic-slice_fusion.refs_0_), channel_id=1, source_target_pairs={{0,32},{4,36},{8,40},{12,44},{64,96},{68,100},{72,104},{76,108},{1... | collective-permute-start | bytes 1769480 | tf_op jit(solution)/shard_map/ppermute | solution.py:48
  123.7 7.1 %collective-permute-start.23 = (f32[288,512]{1,0:T(8,128)S(1)}, f32[288,512]{1,0:T(8,128)S(1)}, u32[]{:S(2)}, u32[]{:S(2)}) collective-permute-start(f32[288,512]{1,0:T(8,128)S(1)} %collective-permute-done.19.refs_1_), channel_id=1, source_target_pairs={{0,32},{4,36},{8,40},{12,44},{64,96},{68,100},{72,104},{76,108},{1... | collective-permute-start | bytes 1769480 | tf_op jit(solution)/shard_map/ppermute | solution.py:48
  130.8 6.6 %collective-permute-start.24 = (f32[288,512]{1,0:T(8,128)S(1)}, f32[288,512]{1,0:T(8,128)S(1)}, u32[]{:S(2)}, u32[]{:S(2)}) collective-permute-start(f32[288,512]{1,0:T(8,128)S(1)} %collective-permute-done.20.refs_2_), channel_id=1, source_target_pairs={{0,32},{4,36},{8,40},{12,44},{64,96},{68,100},{72,104},{76,108},{1... | collective-permute-start | bytes 1769480 | tf_op jit(solution)/shard_map/ppermute | solution.py:48
  138.1 1.6 %copy-done.17 = bf16[2048,512]{1,0:T(8,128)(2,1)S(1)} copy-done((bf16[2048,512]{1,0:T(8,128)(2,1)S(1)}, bf16[2048,512]{1,0:T(8,128)(2,1)}, u32[]{:S(2)}) %copy-start.17) | copy-done | bytes 2097176
  139.6 6.3 %shard_map.135 = bf16[1,2048,1024]{2,1,0:T(8,128)(2,1)} custom-call(s32[1]{0:T(128)} %bitcast.where, bf16[2048,512]{1,0:T(8,128)(2,1)S(1)} %copy-done.17, bf16[2048,512]{1,0:T(8,128)(2,1)S(1)} %copy-done.15, bf16[1024,1024]{1,0:T(8,128)(2,1)S(1)} %copy-done.8, bf16[1024,1024]{1,0:T(8,128)(2,1)S(1)} %copy-done.8), custom_call_target="tpu_custom_call" | custom-call | flops 4294967296 | bytes 10485760 | tf_op jit(solution)/shard_map/pallas_call | solution.py:272
  146.0 2.9 %shard_map.134 = (f32[1024,1024]{1,0:T(8,128)}, f32[100,1024]{1,0:T(8,128)}, f32[1,1024]{1,0:T(1,128)}, f32[1,128]{1,0:T(1,128)S(1)}) custom-call(s32[3]{0:T(128)S(1)} %pad_add_fusion.where, f32[288,512]{1,0:T(8,128)S(1)} %constant_dynamic-slice_fusion.refs_0_, f32[288,512]{1,0:T(8,128)S(1)} %collective-permute-done.19.refs_1_, ...), custom_call_target="tpu_custom_call" | custom-call | bytes 8388608 | tf_op jit(solution)/shard_map/pallas_call | solution.py:310
  (74 shorter events, 8.2 us)
Async XLA Ops:
  0.6 2.2 %copy-start.4 = (bf16[1,2048,1024]{2,1,0:T(8,128)(2,1)S(1)}, bf16[1,2048,1024]{2,1,0:T(8,128)(2,1)}, u32[]{:S(2)}) copy-start(bf16[1,2048,1024]{2,1,0:T(8,128)(2,1)} %param.8) | copy-start | bytes 12582916
  2.8 1.6 %copy-start.7 = (bf16[1024,1024]{1,0:T(8,128)(2,1)S(1)}, bf16[1024,1024]{1,0:T(8,128)(2,1)}, u32[]{:S(2)}) copy-start(bf16[1024,1024]{1,0:T(8,128)(2,1)} %w1.1) | copy-start | bytes 6291460
  4.4 0.9 copy-start.9
  5.3 0.7 copy-start.12
  6.0 0.7 copy-start.13
  11.8 11.2 %collective-permute-start.4 = (f32[100,1024]{1,0:T(8,128)S(1)}, f32[100,1024]{1,0:T(8,128)S(1)}, u32[]{:S(2)}, u32[]{:S(2)}) collective-permute-start(f32[100,1024]{1,0:T(8,128)S(1)} %get-tuple-element.29.own), channel_id=1, source_target_pairs={{0,64},{4,68},{8,72},{12,76},{64,0},{68,4},{72,8},{76,12},{16,80},... | collective-permute-start | bytes 1228808 | tf_op jit(solution)/shard_map/ppermute | solution.py:48
  19.1 2.0 %copy-start.2 = (bf16[2048,1024]{1,0:T(8,128)(2,1)}, bf16[2048,1024]{1,0:T(8,128)(2,1)S(1)}, u32[]{:S(2)}) copy-start(bf16[2048,1024]{1,0:T(8,128)(2,1)S(1)} %get-tuple-element.35.hid) | copy-start | bytes 12582916
  21.1 11.4 %collective-permute-start.1 = (f32[100,1024]{1,0:T(8,128)S(1)}, f32[100,1024]{1,0:T(8,128)}, u32[]{:S(2)}, u32[]{:S(2)}) collective-permute-start(f32[100,1024]{1,0:T(8,128)S(1)} %get-tuple-element.28.own._), channel_id=1, source_target_pairs={{0,64},{4,68},{8,72},{12,76},{64,0},{68,4},{72,8},{76,12},{16,80},... | collective-permute-start | bytes 1228808 | tf_op jit(solution)/shard_map/ppermute | solution.py:48
  21.1 19.9 %collective-permute-start.3 = (f32[100,1024]{1,0:T(8,128)S(1)}, f32[100,1024]{1,0:T(8,128)S(1)}, u32[]{:S(2)}, u32[]{:S(2)}) collective-permute-start(f32[100,1024]{1,0:T(8,128)S(1)} %get-tuple-element.29.own), channel_id=1, source_target_pairs={{0,32},{4,36},{8,40},{12,44},{64,96},{68,100},{72,104},{76,108},{1... | collective-permute-start | bytes 1228808 | tf_op jit(solution)/shard_map/ppermute | solution.py:48
  23.1 17.9 %collective-permute-start.5 = (f32[100,1024]{1,0:T(8,128)S(1)}, f32[100,1024]{1,0:T(8,128)S(1)}, u32[]{:S(2)}, u32[]{:S(2)}) collective-permute-start(f32[100,1024]{1,0:T(8,128)S(1)} %collective-permute-done.4.o2), channel_id=1, source_target_pairs={{0,32},{4,36},{8,40},{12,44},{64,96},{68,100},{72,104},{76,108},{1... | collective-permute-start | bytes 1228808 | tf_op jit(solution)/shard_map/ppermute | solution.py:48
  25.1 17.1 %collective-permute-start = (f32[100,1024]{1,0:T(8,128)S(1)}, f32[100,1024]{1,0:T(8,128)}, u32[]{:S(2)}, u32[]{:S(2)}) collective-permute-start(f32[100,1024]{1,0:T(8,128)S(1)} %get-tuple-element.28.own._), channel_id=1, source_target_pairs={{0,32},{4,36},{8,40},{12,44},{64,96},{68,100},{72,104},{76,108},{1... | collective-permute-start | bytes 1228808 | tf_op jit(solution)/shard_map/ppermute | solution.py:48
  32.6 9.7 %collective-permute-start.2 = (f32[100,1024]{1,0:T(8,128)}, f32[100,1024]{1,0:T(8,128)}, u32[]{:S(2)}, u32[]{:S(2)}) collective-permute-start(f32[100,1024]{1,0:T(8,128)} %collective-permute-done.1.o2), channel_id=1, source_target_pairs={{0,32},{4,36},{8,40},{12,44},{64,96},{68,100},{72,104},{76,108},{1... | collective-permute-start | bytes 1228808 | tf_op jit(solution)/shard_map/ppermute | solution.py:48
  34.0 2.2 %copy-start.5 = (bf16[1,2048,1024]{2,1,0:T(8,128)(2,1)S(1)}, bf16[1,2048,1024]{2,1,0:T(8,128)(2,1)}, u32[]{:S(2)}) copy-start(bf16[1,2048,1024]{2,1,0:T(8,128)(2,1)} %param.8) | copy-start | bytes 12582916
  36.1 4.6 %copy-start.20 = (f32[100]{0:T(128)S(1)}, f32[100]{0:T(128)}, u32[]{:S(2)}) copy-start(f32[100]{0:T(128)} %param.11) | copy-start | bytes 1204
  36.2 4.7 %copy-start.10 = (bf16[100,1024]{1,0:T(8,128)(2,1)S(1)}, bf16[100,1024]{1,0:T(8,128)(2,1)}, u32[]{:S(2)}) copy-start(bf16[100,1024]{1,0:T(8,128)(2,1)} %w_out.3) | copy-start | bytes 614404
  36.2 4.9 %copy-start.6 = (f32[100,2048]{1,0:T(8,128)S(1)}, f32[100,2048]{1,0:T(8,128)}, u32[]{:S(2)}) copy-start(f32[100,2048]{1,0:T(8,128)} %target.3) | copy-start | bytes 2457604
  36.2 4.9 %copy-start.11 = (f32[2048]{0:T(1024)S(1)}, f32[2048]{0:T(1024)}, u32[]{:S(2)}) copy-start(f32[2048]{0:T(1024)} %param.10) | copy-start | bytes 24580
  38.8 2.0 %copy-start = (bf16[1024,2048]{1,0:T(8,128)(2,1)}, bf16[1024,2048]{1,0:T(8,128)(2,1)S(1)}, u32[]{:S(2)}) copy-start(bf16[1024,2048]{1,0:T(8,128)(2,1)S(1)} %shard_map.131.lat) | copy-start | bytes 12582916
  41.0 3.5 %copy-start.1 = (bf16[1024,2048]{1,0:T(8,128)(2,1)S(1)}, bf16[1024,2048]{1,0:T(8,128)(2,1)}, u32[]{:S(2)}) copy-start(bf16[1024,2048]{1,0:T(8,128)(2,1)} %copy-done) | copy-start | bytes 12582916
  44.5 2.2 %copy-start.3 = (bf16[2048,1024]{1,0:T(8,128)(2,1)S(1)}, bf16[2048,1024]{1,0:T(8,128)(2,1)}, u32[]{:S(2)}) copy-start(bf16[2048,1024]{1,0:T(8,128)(2,1)} %copy-done.2) | copy-start | bytes 12582916
  54.2 7.6 %copy-start.14 = (bf16[2048,512]{1,0:T(8,128)(2,1)}, bf16[2048,512]{1,0:T(8,128)(2,1)S(1)}, u32[]{:S(2)}) copy-start(bf16[2048,512]{1,0:T(8,128)(2,1)S(1)} %get-tuple-element.45.d1) | copy-start | bytes 6291460
  54.2 7.6 %collective-permute-start.6 = (f32[4,288,512]{2,1,0:T(8,128)S(1)}, f32[4,288,512]{2,1,0:T(8,128)S(1)}, u32[]{:S(2)}, u32[]{:S(2)}) collective-permute-start(f32[4,288,512]{2,1,0:T(8,128)S(1)} %get-tuple-element.39), channel_id=1, source_target_pairs={{0,32},{4,36},{8,40},{12,44},{64,96},{68,100},{72,104},{76,108},{1... | collective-permute-start | bytes 7077896 | tf_op jit(solution)/shard_map/ppermute | solution.py:48
  61.9 1.9 %copy-start.16 = (bf16[2048,512]{1,0:T(8,128)(2,1)}, bf16[2048,512]{1,0:T(8,128)(2,1)S(1)}, u32[]{:S(2)}) copy-start(bf16[2048,512]{1,0:T(8,128)(2,1)S(1)} %get-tuple-element.44.d0) | copy-start | bytes 6291460
  61.9 2.6 %copy-start.18 = (f32[4,288,512]{2,1,0:T(8,128)}, f32[4,288,512]{2,1,0:T(8,128)S(1)}, u32[]{:S(2)}) copy-start(f32[4,288,512]{2,1,0:T(8,128)S(1)} %collective-permute-done.6) | copy-start | bytes 7077892
  64.5 10.4 %collective-permute-start.7 = (f32[288,512]{1,0:T(8,128)}, f32[288,512]{1,0:T(8,128)S(1)}, u32[]{:S(2)}, u32[]{:S(2)}) collective-permute-start(f32[288,512]{1,0:T(8,128)} %get-tuple-element.46), channel_id=1, source_target_pairs={{0,4},{4,8},{8,12},{12,0},{64,68},{68,72},{72,76},{76,64},{16,20},... | collective-permute-start | bytes 1769480 | tf_op jit(solution)/shard_map/ppermute | solution.py:48
  65.9 9.2 %collective-permute-start.8 = (f32[288,512]{1,0:T(8,128)}, f32[288,512]{1,0:T(8,128)S(1)}, u32[]{:S(2)}, u32[]{:S(2)}) collective-permute-start(f32[288,512]{1,0:T(8,128)} %get-tuple-element.48), channel_id=1, source_target_pairs={{0,12},{4,0},{8,4},{12,8},{64,76},{68,64},{72,68},{76,72},{16,28},... | collective-permute-start | bytes 1769480 | tf_op jit(solution)/shard_map/ppermute | solution.py:48
  67.2 15.4 %collective-permute-start.9 = (f32[288,512]{1,0:T(8,128)}, f32[288,512]{1,0:T(8,128)}, u32[]{:S(2)}, u32[]{:S(2)}) collective-permute-start(f32[288,512]{1,0:T(8,128)} %get-tuple-element.47), channel_id=1, source_target_pairs={{0,8},{4,12},{8,0},{12,4},{64,72},{68,76},{72,64},{76,68},{16,24},... | collective-permute-start | bytes 1769480 | tf_op jit(solution)/shard_map/ppermute | solution.py:48
  75.1 0.8 copy-start.19
  85.0 6.2 %collective-permute-start.10 = (f32[72,512]{1,0:T(8,128)}, f32[72,512]{1,0:T(8,128)S(1)}, u32[]{:S(2)}, u32[]{:S(2)}) collective-permute-start(f32[72,512]{1,0:T(8,128)} %get-tuple-element.49), channel_id=1, source_target_pairs={{0,1},{4,5},{8,9},{12,13},{64,65},{68,69},{72,73},{76,77},{16,17},... | collective-permute-start | bytes 442376 | tf_op jit(solution)/shard_map/ppermute | solution.py:48
  86.3 4.8 %collective-permute-start.11 = (f32[72,512]{1,0:T(8,128)S(1)}, f32[72,512]{1,0:T(8,128)S(1)}, u32[]{:S(2)}, u32[]{:S(2)}) collective-permute-start(f32[72,512]{1,0:T(8,128)S(1)} %get-tuple-element.51), channel_id=1, source_target_pairs={{0,3},{4,7},{8,11},{12,15},{64,67},{68,71},{72,75},{76,79},{16,19}... | collective-permute-start | bytes 442376 | tf_op jit(solution)/shard_map/ppermute | solution.py:48
  88.4 5.5 %collective-permute-start.12 = (f32[72,512]{1,0:T(8,128)S(1)}, f32[72,512]{1,0:T(8,128)S(1)}, u32[]{:S(2)}, u32[]{:S(2)}) collective-permute-start(f32[72,512]{1,0:T(8,128)S(1)} %get-tuple-element.50), channel_id=1, source_target_pairs={{0,2},{4,6},{8,10},{12,14},{64,66},{68,70},{72,74},{76,78},{16,18}... | collective-permute-start | bytes 442376 | tf_op jit(solution)/shard_map/ppermute | solution.py:48
  89.8 48.3 %copy-start.8 = (bf16[1024,1024]{1,0:T(8,128)(2,1)S(1)}, bf16[1024,1024]{1,0:T(8,128)(2,1)}, u32[]{:S(2)}) copy-start(bf16[1024,1024]{1,0:T(8,128)(2,1)} %w1.1) | copy-start | bytes 6291460
  94.0 5.4 %collective-permute-start.13 = (f32[72,512]{1,0:T(8,128)S(1)}, f32[72,512]{1,0:T(8,128)S(1)}, u32[]{:S(2)}, u32[]{:S(2)}) collective-permute-start(f32[72,512]{1,0:T(8,128)S(1)} %fusion.8), channel_id=1, source_target_pairs={{0,64},{4,68},{8,72},{12,76},{64,16},{68,20},{72,24},{76,28},{16,8... | collective-permute-start | bytes 442376 | tf_op jit(solution)/shard_map/ppermute | solution.py:48
  95.3 4.0 %collective-permute-start.14 = (f32[72,512]{1,0:T(8,128)S(1)}, f32[72,512]{1,0:T(8,128)S(1)}, u32[]{:S(2)}, u32[]{:S(2)}) collective-permute-start(f32[72,512]{1,0:T(8,128)S(1)} %fusion.8), channel_id=1, source_target_pairs={{0,80},{4,84},{8,88},{12,92},{64,0},{68,4},{72,8},{76,12},{16,64},... | collective-permute-start | bytes 442376 | tf_op jit(solution)/shard_map/ppermute | solution.py:48
  97.1 5.6 %collective-permute-start.15 = (f32[72,512]{1,0:T(8,128)S(1)}, f32[72,512]{1,0:T(8,128)S(1)}, u32[]{:S(2)}, u32[]{:S(2)}) collective-permute-start(f32[72,512]{1,0:T(8,128)S(1)} %fusion.8), channel_id=1, source_target_pairs={{0,16},{4,20},{8,24},{12,28},{64,80},{68,84},{72,88},{76,92},{16,0... | collective-permute-start | bytes 442376 | tf_op jit(solution)/shard_map/ppermute | solution.py:48
  102.7 4.4 %collective-permute-start.16 = (f32[72,512]{1,0:T(8,128)S(1)}, f32[72,512]{1,0:T(8,128)S(1)}, u32[]{:S(2)}, u32[]{:S(2)}) collective-permute-start(f32[72,512]{1,0:T(8,128)S(1)} %add_add_fusion), channel_id=1, source_target_pairs={{0,3},{4,7},{8,11},{12,15},{64,67},{68,71},{72,75},{76,79},{16,19}... | collective-permute-start | bytes 442376 | tf_op jit(solution)/shard_map/ppermute | solution.py:48
  104.1 5.6 %collective-permute-start.17 = (f32[72,512]{1,0:T(8,128)S(1)}, f32[72,512]{1,0:T(8,128)S(1)}, u32[]{:S(2)}, u32[]{:S(2)}) collective-permute-start(f32[72,512]{1,0:T(8,128)S(1)} %add_add_fusion), channel_id=1, source_target_pairs={{0,2},{4,6},{8,10},{12,14},{64,66},{68,70},{72,74},{76,78},{16,18}... | collective-permute-start | bytes 442376 | tf_op jit(solution)/shard_map/ppermute | solution.py:48
  105.5 32.6 %copy-start.15 = (bf16[2048,512]{1,0:T(8,128)(2,1)S(1)}, bf16[2048,512]{1,0:T(8,128)(2,1)}, u32[]{:S(2)}) copy-start(bf16[2048,512]{1,0:T(8,128)(2,1)} %copy-done.14) | copy-start | bytes 6291460
  105.5 5.8 %collective-permute-start.18 = (f32[72,512]{1,0:T(8,128)S(1)}, f32[72,512]{1,0:T(8,128)S(1)}, u32[]{:S(2)}, u32[]{:S(2)}) collective-permute-start(f32[72,512]{1,0:T(8,128)S(1)} %add_add_fusion), channel_id=1, source_target_pairs={{0,1},{4,5},{8,9},{12,13},{64,65},{68,69},{72,73},{76,77},{16,17},... | collective-permute-start | bytes 442376 | tf_op jit(solution)/shard_map/ppermute | solution.py:48
  111.4 12.3 %collective-permute-start.19 = (f32[288,512]{1,0:T(8,128)S(1)}, f32[288,512]{1,0:T(8,128)S(1)}, u32[]{:S(2)}, u32[]{:S(2)}) collective-permute-start(f32[288,512]{1,0:T(8,128)S(1)} %constant_dynamic-slice_fusion.refs_0_), channel_id=1, source_target_pairs={{0,4},{4,8},{8,12},{12,0},{64,68},{68,72},{72,76},{76,64},{16,20},... | collective-permute-start | bytes 1769480 | tf_op jit(solution)/shard_map/ppermute | solution.py:48
  112.6 18.2 %collective-permute-start.20 = (f32[288,512]{1,0:T(8,128)S(1)}, f32[288,512]{1,0:T(8,128)S(1)}, u32[]{:S(2)}, u32[]{:S(2)}) collective-permute-start(f32[288,512]{1,0:T(8,128)S(1)} %constant_dynamic-slice_fusion.refs_0_), channel_id=1, source_target_pairs={{0,8},{4,12},{8,0},{12,4},{64,72},{68,76},{72,64},{76,68},{16,24},... | collective-permute-start | bytes 1769480 | tf_op jit(solution)/shard_map/ppermute | solution.py:48
  116.2 21.1 %collective-permute-start.21 = (f32[288,512]{1,0:T(8,128)S(1)}, f32[288,512]{1,0:T(8,128)S(1)}, u32[]{:S(2)}, u32[]{:S(2)}) collective-permute-start(f32[288,512]{1,0:T(8,128)S(1)} %constant_dynamic-slice_fusion.refs_0_), channel_id=1, source_target_pairs={{0,12},{4,0},{8,4},{12,8},{64,76},{68,64},{72,68},{76,72},{16,28},... | collective-permute-start | bytes 1769480 | tf_op jit(solution)/shard_map/ppermute | solution.py:48
  116.2 29.7 %collective-permute-start.22 = (f32[288,512]{1,0:T(8,128)S(1)}, f32[288,512]{1,0:T(8,128)S(1)}, u32[]{:S(2)}, u32[]{:S(2)}) collective-permute-start(f32[288,512]{1,0:T(8,128)S(1)} %constant_dynamic-slice_fusion.refs_0_), channel_id=1, source_target_pairs={{0,32},{4,36},{8,40},{12,44},{64,96},{68,100},{72,104},{76,108},{1... | collective-permute-start | bytes 1769480 | tf_op jit(solution)/shard_map/ppermute | solution.py:48
  123.7 22.3 %collective-permute-start.23 = (f32[288,512]{1,0:T(8,128)S(1)}, f32[288,512]{1,0:T(8,128)S(1)}, u32[]{:S(2)}, u32[]{:S(2)}) collective-permute-start(f32[288,512]{1,0:T(8,128)S(1)} %collective-permute-done.19.refs_1_), channel_id=1, source_target_pairs={{0,32},{4,36},{8,40},{12,44},{64,96},{68,100},{72,104},{76,108},{1... | collective-permute-start | bytes 1769480 | tf_op jit(solution)/shard_map/ppermute | solution.py:48
  130.8 15.2 %collective-permute-start.24 = (f32[288,512]{1,0:T(8,128)S(1)}, f32[288,512]{1,0:T(8,128)S(1)}, u32[]{:S(2)}, u32[]{:S(2)}) collective-permute-start(f32[288,512]{1,0:T(8,128)S(1)} %collective-permute-done.20.refs_2_), channel_id=1, source_target_pairs={{0,32},{4,36},{8,40},{12,44},{64,96},{68,100},{72,104},{76,108},{1... | collective-permute-start | bytes 1769480 | tf_op jit(solution)/shard_map/ppermute | solution.py:48
  137.3 8.7 %collective-permute-start.25 = (f32[288,512]{1,0:T(8,128)S(1)}, f32[288,512]{1,0:T(8,128)S(1)}, u32[]{:S(2)}, u32[]{:S(2)}) collective-permute-start(f32[288,512]{1,0:T(8,128)S(1)} %collective-permute-done.21.refs_3_), channel_id=1, source_target_pairs={{0,32},{4,36},{8,40},{12,44},{64,96},{68,100},{72,104},{76,108},{1... | collective-permute-start | bytes 1769480 | tf_op jit(solution)/shard_map/ppermute | solution.py:48
  138.1 1.6 %copy-start.17 = (bf16[2048,512]{1,0:T(8,128)(2,1)S(1)}, bf16[2048,512]{1,0:T(8,128)(2,1)}, u32[]{:S(2)}) copy-start(bf16[2048,512]{1,0:T(8,128)(2,1)} %copy-done.16) | copy-start | bytes 6291460

commit v3 on v1

v3 whole, which is shorter than its diff:
```python
import functools
import math

import jax
import jax.numpy as jnp
from jax import lax
from jax.experimental import pallas as pl
from jax.experimental.pallas import tpu as pltpu
from jax.sharding import Mesh, PartitionSpec as P

DELTA = 0.05
ALL = ("ylo", "core", "yhi", "z", "x")
MIB = 1 << 20
F32, BF16 = jnp.float32, jnp.bfloat16


def flat(core, x, y, z):
    return ((y % 2) * 2 + core) * 32 + (y // 2) * 16 + z * 4 + x


def moved(where):
    pairs = []
    for core in range(2):
        for x in range(4):
            for y in range(4):
                for z in range(4):
                    pairs.append((flat(core, x, y, z), flat(*where(core, x, y, z))))
    return pairs


SWAP = moved(lambda c, x, y, z: (1 - c, x, y, z))
NEAR = moved(lambda c, x, y, z: (c, x, y ^ 1, z))


def first(k):
    return moved(lambda c, x, y, z: (c, x, y, (z + k) % 4) if c == 0 else (c, (x + k) % 4, y, z))


def second(k):
    return moved(lambda c, x, y, z: (c, x, y, (z + k) % 4) if c == 1 else (c, (x + k) % 4, y, z))


def along_y(k):
    return moved(lambda c, x, y, z: (c, x, (y + k) % 4, z))


def send(array, pairs):
    return lax.ppermute(array, ALL, pairs)


def grad_sum(own, sibling, beside, dpre):
    core, x, z = lax.axis_index("core"), lax.axis_index("x"), lax.axis_index("z")
    place = jnp.where(core == 0, x, z)
    got = send(sibling, SWAP)
    held = [own[k] + got[k] for k in range(4)]
    held, dpre = lax.optimization_barrier((held, dpre))
    aside = beside(dpre)
    came = [send(held[k], first(k)) for k in (1, 3, 2)]
    *came, aside = lax.optimization_barrier((*came, aside))
    block = held[0] + came[0] + came[1] + came[2]
    rows = block.shape[0] // 4
    quarters = block.reshape((4, rows) + block.shape[1:])
    pick = lambda k: lax.dynamic_index_in_dim(quarters, (place + k) % 4, 0, keepdims=False)
    quarter = pick(0)
    for k in (1, 3, 2):
        quarter = quarter + send(pick(k), second(k))
    quarter = quarter + send(quarter, along_y(1)) + send(quarter, along_y(3)) + send(quarter, along_y(2))
    came = [quarter] + [send(quarter, second(k)) for k in (1, 2, 3)]
    twice = jnp.concatenate([came[3], came[2], came[1], came[0], came[3], came[2], came[1]], 0)
    block = lax.dynamic_slice_in_dim(twice, ((3 - place) % 4) * rows, 4 * rows, 0)
    mine = [block] + [send(block, first(k)) for k in (1, 2, 3)]
    return mine, [send(m, SWAP) for m in mine], aside


def params(mib=56):
    return pltpu.CompilerParams(vmem_limit_bytes=mib * MIB)


def cost(flops, moved_bytes, trans=0):
    return pl.CostEstimate(flops=flops, bytes_accessed=moved_bytes, transcendentals=trans)


def forward_kernel(lat, w, b_hid, w_out, b_out, *refs):
    pred, hid, slope_out = refs[-3:]
    cols = 256
    turned = b_out[...]
    for j in range(0, w.shape[1], cols):
        at = slice(j, j + cols)
        pre = jnp.dot(lat[...], w[:, at], preferred_element_type=F32) + b_hid[:, at]
        sig = jax.nn.sigmoid(pre)
        h = (pre * sig).astype(BF16)
        hid[:, at] = h
        slope_out[:, at] = sig * (1.0 + pre * (1.0 - sig))
        turned = turned + lax.dot_general(h, w_out[:, at], (((1,), (1,)), ((), ())), preferred_element_type=F32)
    pred[...] = jnp.transpose(turned)


def forward(part, n, latent, w_hidden, b_hidden, w_output, b_output, tile=512):
    depth = latent.shape[1]
    width, n_vars = w_hidden.shape[1], w_output.shape[0]
    steps = n // tile
    whole = lambda shape: pl.BlockSpec(shape, lambda g: (0, 0))
    rows = pl.BlockSpec((tile, width), lambda g: (g, 0))
    return pl.pallas_call(
        forward_kernel,
        grid=(steps,),
        in_specs=[
            pl.BlockSpec((tile, depth), lambda g: (part * steps + g, 0)),
            whole(w_hidden.shape),
            whole((1, width)),
            whole(w_output.shape),
            whole((1, n_vars)),
        ],
        out_specs=[pl.BlockSpec((n_vars, tile), lambda g: (0, g)), rows, rows],
        out_shape=[
            jax.ShapeDtypeStruct((n_vars, n), F32),
            jax.ShapeDtypeStruct((n, width), BF16),
            jax.ShapeDtypeStruct((n, width), F32),
        ],
        compiler_params=params(),
        cost_estimate=cost(2 * n * width * (depth + n_vars), n * (2 * depth + 6 * width) + 2 * depth * width, 2 * n * width),
    )(latent, w_hidden, b_hidden.reshape(1, width), w_output, b_output.reshape(1, n_vars))


def cot_kernel(members, scale, loss_scale, pair_coef, own, o1, o2, o3, target, area, var, sp, hid, w_out, *refs):
    dpre, rest, cot_held = refs[-3:]
    n_vars, n = own.shape
    j = pl.program_id(0)
    rest[...] = refs[0][...] if len(refs) > 3 else jnp.zeros_like(rest)

    @pl.when(j == 0)
    def _():
        weights = var[...] * area[...]
        mine = own[...]

        def both(diff):
            u = diff * diff + DELTA * DELTA
            r = lax.rsqrt(u)
            return u * r - DELTA, diff * r

        mag, slo = both(mine - target[...])
        pair_mag, pair_slo = jnp.zeros_like(mine), jnp.zeros_like(mine)
        for other in (o1, o2, o3):
            m, s = both(mine - other[...])
            pair_mag, pair_slo = pair_mag + m, pair_slo + s
        term = weights * (mag * (1.0 / members) - (0.5 * pair_coef) * pair_mag)
        cot = (weights * (slo * (1.0 / members) - pair_coef * pair_slo)).astype(BF16)
        cot_held[...] = cot
        sums = lax.dot_general(
            jnp.ones((16, n), BF16), cot, (((1,), (1,)), ((), ())), preferred_element_type=F32
        )[0:1]
        rest[n_vars + 1 : n_vars + 2, 0:n_vars] += sums * scale
        rest[n_vars + 2 : n_vars + 3, 0:128] += jnp.full((1, 128), jnp.sum(term) * loss_scale, F32)

    cot = cot_held[...]
    back = lax.dot_general(cot, w_out[...], (((0,), (0,)), ((), ())), preferred_element_type=F32)
    d = (back * sp[...]).astype(BF16)
    dpre[...] = d
    rest[0:n_vars, :] += jnp.dot(cot, hid[...], preferred_element_type=F32) * scale
    rest[n_vars : n_vars + 1, :] += jnp.sum(d.astype(F32), axis=0, keepdims=True) * scale


def cotangent(part, n, own, others, target, area, var, sp, hid, w_output, held, members, scale, loss_scale, pair_coef, cols=256):
    n_vars, width = target.shape[0], sp.shape[1]
    local = pl.BlockSpec((n_vars, n), lambda j: (0, 0))
    block = pl.BlockSpec((n, cols), lambda j: (0, j))
    rest = pl.BlockSpec((128, cols), lambda j: (0, j))
    return pl.pallas_call(
        functools.partial(cot_kernel, members, scale, loss_scale, pair_coef),
        grid=(width // cols,),
        in_specs=[local] * 4
        + [
            pl.BlockSpec((n_vars, n), lambda j: (0, part)),
            pl.BlockSpec((1, n), lambda j: (0, part)),
            pl.BlockSpec((n_vars, 1), lambda j: (0, 0)),
            block,
            block,
            pl.BlockSpec((n_vars, cols), lambda j: (0, j)),
        ]
        + [rest] * len(held),
        out_specs=[block, rest],
        out_shape=[
            jax.ShapeDtypeStruct((n, width), BF16),
            jax.ShapeDtypeStruct((128, width), F32),
        ],
        scratch_shapes=[pltpu.VMEM((n_vars, n), BF16)],
        compiler_params=params(),
        cost_estimate=cost(4 * n * n_vars * width, n * (n_vars * 20 + 8 * width), 4 * n * n_vars),
    )(own, *others, target, area, var, sp, hid, w_output, *held)


def weight_kernel(scale, where, lat0, lat1, dpre0, dpre1, rest, out):
    rows, n = lat0.shape[1], dpre0.shape[0]
    dims = (((0,), (0,)), ((), ()))
    for j, lat in enumerate((lat0, lat1)):
        block = lax.rem(where[1] + 2 * pl.program_id(0) + j, 4)
        out[j, 0:rows, :] = (
            lax.dot_general(lat[0:n, :], dpre0[...], dims, preferred_element_type=F32)
            + lax.dot_general(lat[n : 2 * n, :], dpre1[...], dims, preferred_element_type=F32)
        ) * scale
        out[j, rows : rows + 32, :] = rest[pl.ds(pl.multiple_of(block * 32, 32), 32), :]


def weight_grad(which, place, latent, dpre, rest, scale):
    (points, depth), width = latent.shape, dpre[0].shape[1]
    half, rows = width // 2, depth // 4
    halves = pl.BlockSpec((points // 2, half), lambda g, s: (0, s[0]))
    lat = lambda j: pl.BlockSpec((points, rows), lambda g, s: (0, lax.rem(s[1] + 2 * g + j, 4)))
    return pl.pallas_call(
        functools.partial(weight_kernel, scale),
        grid_spec=pltpu.PrefetchScalarGridSpec(
            num_scalar_prefetch=1,
            grid=(2,),
            in_specs=[
                lat(0),
                lat(1),
                halves,
                halves,
                pl.BlockSpec((128, half), lambda g, s: (0, s[0])),
            ],
            out_specs=pl.BlockSpec((2, rows + 32, half), lambda g, s: (g, 0, 0)),
        ),
        out_shape=jax.ShapeDtypeStruct((4, rows + 32, half), F32),
        compiler_params=params(),
        cost_estimate=cost(2 * points * half * depth, points * (2 * half + 2 * depth) + 4 * depth * half),
    )(jnp.stack([which, place]).astype(jnp.int32), latent, latent, *dpre, rest)


def latent_kernel(steps, dpre0, dpre1, w, out):
    g = pl.program_id(0)
    for part, dpre in enumerate((dpre0, dpre1)):

        @pl.when(g // steps == part)
        def _():
            out[0] = lax.dot_general(
                dpre[...], w[...], (((1,), (1,)), ((), ())), preferred_element_type=F32
            ).astype(BF16)


def latent_gradient(dpre, w_hidden, tile=512):
    n, width = dpre[0].shape
    depth, points, steps = w_hidden.shape[0], 2 * n, n // tile
    return pl.pallas_call(
        functools.partial(latent_kernel, steps),
        grid=(2 * steps,),
        in_specs=[
            pl.BlockSpec((tile, width), lambda g: (jnp.minimum(g, steps - 1), 0)),
            pl.BlockSpec((tile, width), lambda g: (jnp.maximum(g - steps, 0), 0)),
            pl.BlockSpec((depth, width), lambda g: (0, 0)),
        ],
        out_specs=pl.BlockSpec((1, tile, depth), lambda g: (0, g, 0)),
        out_shape=jax.ShapeDtypeStruct((1, points, depth), BF16),
        compiler_params=params(),
        cost_estimate=cost(2 * points * width * depth, points * (2 * width + 2 * depth) + 2 * depth * width),
    )(*dpre, w_hidden)


def join_kernel(n_vars, where, *refs):
    ins, (grad_w, grad_o, grad_b, grad_b_out, loss, rest) = refs[:8], refs[8:]
    rows, half = ins[0].shape[0] - 32, ins[0].shape[1]
    for which in range(2):
        col = where[0] if which == 0 else 1 - where[0]
        cols = pl.ds(pl.multiple_of(col * half, half), half)
        for k in range(4):
            block = lax.rem(where[1 + which] - k + 4, 4)
            grad_w[pl.ds(pl.multiple_of(block * rows, rows), rows), cols] = ins[4 * which + k][0:rows, :]
            rest[pl.ds(pl.multiple_of(block * 32, 32), 32), cols] = ins[4 * which + k][rows : rows + 32, :]
    grad_o[...] = rest[0:n_vars, :]
    grad_b[...] = rest[n_vars : n_vars + 1, :]
    grad_b_out[...] = rest[n_vars + 1 : n_vars + 2, 0:n_vars]
    loss[...] = rest[n_vars + 2 : n_vars + 3, 0:1]


def join(where, own, sib, n_vars):
    rows, half = own[0].shape
    depth, width = 4 * (rows - 32), 2 * half
    vmem = pl.BlockSpec(memory_space=pltpu.VMEM)
    return pl.pallas_call(
        functools.partial(join_kernel, n_vars),
        in_specs=[pl.BlockSpec(memory_space=pltpu.SMEM)] + [vmem] * 8,
        out_specs=[vmem] * 5,
        out_shape=[
            jax.ShapeDtypeStruct((depth, width), F32),
            jax.ShapeDtypeStruct((n_vars, width), F32),
            jax.ShapeDtypeStruct((1, width), F32),
            jax.ShapeDtypeStruct((1, n_vars), F32),
            jax.ShapeDtypeStruct((1, 1), F32),
        ],
        scratch_shapes=[pltpu.VMEM((128, width), F32)],
        compiler_params=params(16),
        cost_estimate=cost(0, 8 * depth * width),
    )(where, *own, *sib)


def shards(latent, target, area_weight, var_weight, w_hidden, b_hidden, w_output, b_output):
    members = 4
    parts = [(0, 1024), (1, 1024)]
    n_vars, points = target.shape
    points_all = points * 32
    eps = 0.05 / members
    pair_coef = (1.0 - eps) / (members * (members - 1))
    scale = 1.0 / math.sqrt(members * points_all)
    loss_scale = 1.0 / (points_all * n_vars)
    core, x, z = lax.axis_index("core"), lax.axis_index("x"), lax.axis_index("z")
    place_own = jnp.where(core == 0, z, x)
    place_sib = jnp.where(core == 0, x, z)
    own_latent = latent[0]
    made = [forward(part, n, own_latent, w_hidden, b_hidden, w_output, b_output) for part, n in parts]
    area, var = area_weight.reshape(1, points), var_weight.reshape(n_vars, 1)
    dpre, rest, after = [], (), made[-1][0]
    for (part, n), (pred, hid, sp) in zip(parts, made):
        near = send(pred, NEAR)
        near, after = lax.optimization_barrier((near, after))
        others = (send(pred, SWAP), near, send(near, SWAP))
        d, total = cotangent(
            part, n, pred, others, target, area, var, sp, hid, w_output, rest, members, scale, loss_scale, pair_coef
        )
        dpre.append(d)
        rest, after = (total,), total
    rest = after
    blocks_sib = weight_grad(1 - core, place_sib, own_latent, dpre, rest, scale)
    blocks_own = weight_grad(core, place_own, own_latent, dpre, rest, scale)
    out_own, out_sib, latent_grad = grad_sum(blocks_own, blocks_sib, lambda d: latent_gradient(d, w_hidden), dpre)
    where = jnp.stack([core, place_own, place_sib]).astype(jnp.int32)
    grad_w_hidden, grad_w_output, grad_b_hidden, grad_b_output, loss = join(where, out_own, out_sib, n_vars)
    return (
        loss.reshape(()),
        grad_w_hidden,
        grad_b_hidden.reshape(-1),
        grad_w_output,
        grad_b_output.reshape(-1),
        latent_grad,
    )


def solution(mesh):
    fine = Mesh(mesh.devices.reshape(2, 2, 2, 4, 4), ALL)
    member, space = ("ylo", "core"), ("yhi", "z", "x")
    return jax.shard_map(
        shards,
        mesh=fine,
        in_specs=(P(member, space, None), P(None, space), P(space), P(), P(), P(), P(), P()),
        out_specs=(P(), P(), P(), P(), P(), P(member, space, None)),
        check_vma=False,
    )
```

time: 176 us -> 137 us (0.78)
  Pallas kernels: 0 us -> 56.4 us
  matrix products: 33.3 us -> 0 us
  waiting for transfers between devices: 48.2 us -> 21.6 us
  other arithmetic: 28 us -> 4.84 us
  local copies, waits for them, and re-layouts: 17.1 us -> 2.65 us
  starting transfers between devices: 47.4 us -> 50.4 us
    pallas_call x0 -> x8, Pallas kernels: none -> 56.4 us  [the longest x2 17.2 us: forward(): pl.pallas_call(forward_kernel, grid=(steps,), in_specs=[pl.BlockSpec((til...]
    dot_general x6 -> x0, matrix products: 33.3 us -> none  [the longest x1 10.3 us: shards(): jnp.dot(own_latent, w_hidden, preferred_element_type=jnp.float32) + b_hidden]
    ppermute x23 -> x26, waiting for transfers between devices: 48.2 us -> 21.6 us  [send(): return lax.ppermute(array, ALL, pairs)]
    concatenate x6 -> x0, other arithmetic: 9.55 us -> none  [the longest x1 4.36 us: shards(): jnp.concatenate([part_w_hidden.reshape(4, depth // 4, width), rest.reshap...]
    gather x2 -> x0, local copies, waits for them, and re-layouts: 7.57 us -> none  [in_place(): return jnp.take(jnp.stack(outs), (place - jnp.arange(4)) % 4, axis=0)]
    another operation x2 -> x3, other arithmetic: 5.99 us -> 1.33 us  [the longest x2 1.25 us: weight_grad(): jnp.stack([which, place]).astype(jnp.int32)]
    reduce_sum x1 -> x0, other arithmetic: 4.58 us -> none  [shards(): part_b_output = jnp.sum(cot.astype(jnp.float32), axis=1) * scale]
    slice x5 -> x0, local copies, waits for them, and re-layouts: 3.87 us -> none  [the longest x2 1.9 us: ordered(): twice = jnp.concatenate([mine, mine[:3]], 0)]
  transfers between devices with their start and end apart: 23 -> 26, of which waited for: 13 -> 12; matrix products, arithmetic and copies ran while one was open for 10% -> 2% of each run, Pallas kernels for 0% -> 23%
where the time goes in v3:
time: 137 us
  Pallas kernels  56.4 us (41%)
  starting transfers between devices  50.4 us (37%)
  waiting for transfers between devices  21.6 us (16%)
  other arithmetic  4.84 us (4%)
  local copies, waits for them, and re-layouts  2.65 us (2%)
    ppermute x26, starting transfers between devices, send(): return lax.ppermute(array, ALL, pairs)  50.4 us
    ppermute x26, waiting for transfers between devices, send(): return lax.ppermute(array, ALL, pairs)  21.6 us
    pallas_call x2, Pallas kernels, forward(): pl.pallas_call(forward_kernel, grid=(steps,), in_specs=[pl.BlockSpec((til...  17.2 us
    pallas_call x2, Pallas kernels, cotangent(): pl.pallas_call(functools.partial(cot_kernel, members, scale, loss_scale,...  14.4 us
    pallas_call x2, Pallas kernels, weight_grad(): pl.pallas_call(functools.partial(weight_kernel, scale), grid_spec=pltpu.P...  13.1 us
    pallas_call x1, Pallas kernels, latent_gradient(): pl.pallas_call(functools.partial(latent_kernel, steps), grid=(2 * steps,)...  8.73 us
    add x1, other arithmetic, grad_sum(): held = [own[k] + got[k] for k in range(4)]  3.18 us
    pallas_call x1, Pallas kernels, join(): pl.pallas_call(functools.partial(join_kernel, n_vars), in_specs=[pl.Block...  2.9 us
  transfers between devices with their start and end apart: 26, of which 12 were waited for; matrix products, arithmetic and copies ran while one was open for 2% of the time, Pallas kernels for 23%

profile of v3, /device:TPU:1, one launch (start us, length us, event | category | flops | bytes accessed | tf_op | source)
XLA Modules:
  0.0 136.6 jit_solution(3911362679296850973)
XLA Ops:
  0.6 8.6 %shard_map.127 = (f32[100,1024]{1,0:T(8,128)}, bf16[1024,1024]{1,0:T(8,128)(2,1)}, f32[1024,1024]{1,0:T(8,128)}) custom-call(bf16[2048,1024]{1,0:T(8,128)(2,1)} %bitcast.33, bf16[1024,1024]{1,0:T(8,128)(2,1)} %w.5, f32[1,1024]{1,0:T(1,128)} %bitcast.44, bf16[100,1024]{1,0:T(8,128)(2,1)} %w_out.7, f32[1,100]{1,0:T(1,128)} %bitcast.47), custom_call_target="tpu_custom_call" | custom-call | flops 2357198848 | bytes 10485760 | tf_op jit(solution)/shard_map/pallas_call | solution.py:104
  9.3 2.2 %collective-permute-start.1 = (f32[100,1024]{1,0:T(8,128)}, f32[100,1024]{1,0:T(8,128)S(1)}, u32[]{:S(2)}, u32[]{:S(2)}) collective-permute-start(f32[100,1024]{1,0:T(8,128)} %get-tuple-element.33.own), channel_id=1, source_target_pairs={{0,64},{4,68},{8,72},{12,76},{64,0},{68,4},{72,8},{76,12},{16,80},... | collective-permute-start | bytes 1228808 | tf_op jit(solution)/shard_map/ppermute | solution.py:48
  11.5 1.0 collective-permute-start
  12.4 8.5 %shard_map.128 = (f32[100,1024]{1,0:T(8,128)}, bf16[1024,1024]{1,0:T(8,128)(2,1)}, f32[1024,1024]{1,0:T(8,128)}) custom-call(bf16[2048,1024]{1,0:T(8,128)(2,1)} %bitcast.34, bf16[1024,1024]{1,0:T(8,128)(2,1)} %w.5, f32[1,1024]{1,0:T(1,128)} %bitcast.45, bf16[100,1024]{1,0:T(8,128)(2,1)} %w_out.7, f32[1,100]{1,0:T(1,128)} %bitcast.48), custom_call_target="tpu_custom_call" | custom-call | flops 2357198848 | bytes 10485760 | tf_op jit(solution)/shard_map/pallas_call | solution.py:104
  21.0 1.5 %collective-permute-start.2 = (f32[100,1024]{1,0:T(8,128)S(1)}, f32[100,1024]{1,0:T(8,128)S(1)}, u32[]{:S(2)}, u32[]{:S(2)}) collective-permute-start(f32[100,1024]{1,0:T(8,128)S(1)} %collective-permute-done.1.o2), channel_id=1, source_target_pairs={{0,32},{4,36},{8,40},{12,44},{64,96},{68,100},{72,104},{76,108},{1... | collective-permute-start | bytes 1228808 | tf_op jit(solution)/shard_map/ppermute | solution.py:48
  22.5 1.5 %collective-permute-start.4 = (f32[100,1024]{1,0:T(8,128)}, f32[100,1024]{1,0:T(8,128)S(1)}, u32[]{:S(2)}, u32[]{:S(2)}) collective-permute-start(f32[100,1024]{1,0:T(8,128)} %get-tuple-element.34.own), channel_id=1, source_target_pairs={{0,64},{4,68},{8,72},{12,76},{64,0},{68,4},{72,8},{76,12},{16,80},... | collective-permute-start | bytes 1228808 | tf_op jit(solution)/shard_map/ppermute | solution.py:48
  24.2 0.7 copy.14.var
  25.0 0.8 copy-done.4
  25.9 7.1 %shard_map.129 = (bf16[1024,1024]{1,0:T(8,128)(2,1)}, f32[128,1024]{1,0:T(8,128)}) custom-call(f32[100,1024]{1,0:T(8,128)} %get-tuple-element.33.own, f32[100,1024]{1,0:T(8,128)} %copy-done.4, f32[100,1024]{1,0:T(8,128)} %copy-done.3, f32[100,1024]{1,0:T(8,128)} %copy-done.5, f32[100,2048]{1,0:T(8,128)} %target.3, f32[1,2048]{1,0:T(1,128)} %bitcast.41, ...), custom_call_target="tpu_custom_call" | custom-call | flops 419430400 | bytes 10436608 | tf_op jit(solution)/shard_map/pallas_call | solution.py:168
  33.1 1.1 collective-permute-done.4.o2
  34.1 0.8 collective-permute-start.5
  34.9 0.7 pad_add_fusion.2.where
  35.6 0.7 collective-permute-done.5.o3
  36.3 0.8 copy-done.2
  37.1 7.3 %shard_map.130 = (bf16[1024,1024]{1,0:T(8,128)(2,1)}, f32[128,1024]{1,0:T(8,128)}) custom-call(f32[100,1024]{1,0:T(8,128)} %get-tuple-element.34.own, f32[100,1024]{1,0:T(8,128)} %copy-done.1, f32[100,1024]{1,0:T(8,128)} %copy-done, f32[100,1024]{1,0:T(8,128)} %copy-done.2, f32[100,2048]{1,0:T(8,128)} %target.3, f32[1,2048]{1,0:T(1,128)} %bitcast.42, ...), custom_call_target="tpu_custom_call" | custom-call | flops 419430400 | bytes 10436608 | tf_op jit(solution)/shard_map/pallas_call | solution.py:168
  44.4 6.6 %shard_map.132 = f32[4,288,512]{2,1,0:T(8,128)} custom-call(s32[2]{0:T(128)} %pad_add_fusion.2.where, bf16[2048,1024]{1,0:T(8,128)(2,1)} %bitcast.35, bf16[2048,1024]{1,0:T(8,128)(2,1)} %bitcast.36, bf16[1024,1024]{1,0:T(8,128)(2,1)} %get-tuple-element.49.dpre0, bf16[1024,1024]{1,0:T(8,128)(2,1)} %get-tuple-element.50.dpre1, f32[128,1024]{1,0:T(8,128)} %get-tuple-element.44.rest), custom_call_target="tpu_custom_call" | custom-call | flops 2147483648 | bytes 8388608 | tf_op jit(solution)/shard_map/pallas_call | solution.py:209
  51.9 6.6 %shard_map.131 = f32[4,288,512]{2,1,0:T(8,128)} custom-call(s32[2]{0:T(128)} %pad_add_fusion.1.where, bf16[2048,1024]{1,0:T(8,128)(2,1)} %bitcast.37, bf16[2048,1024]{1,0:T(8,128)(2,1)} %bitcast.38, bf16[1024,1024]{1,0:T(8,128)(2,1)} %get-tuple-element.49.dpre0, bf16[1024,1024]{1,0:T(8,128)(2,1)} %get-tuple-element.50.dpre1, f32[128,1024]{1,0:T(8,128)} %get-tuple-element.44.rest), custom_call_target="tpu_custom_call" | custom-call | flops 2147483648 | bytes 8388608 | tf_op jit(solution)/shard_map/pallas_call | solution.py:209
  58.5 3.2 %fusion = (f32[288,512]{1,0:T(8,128)}, f32[288,512]{1,0:T(8,128)S(1)}, f32[288,512]{1,0:T(8,128)}, f32[288,512]{1,0:T(8,128)S(1)}) fusion(f32[4,288,512]{2,1,0:T(8,128)S(1)} %collective-permute-done.6, f32[4,288,512]{2,1,0:T(8,128)} %shard_map.131), kind=kLoop, calls=%fused_computation.1 | loop fusion | flops 589824 | bytes 7077888 | tf_op jit(solution)/shard_map/add | solution.py:55
  61.7 1.4 %collective-permute-start.7 = (f32[288,512]{1,0:T(8,128)}, f32[288,512]{1,0:T(8,128)S(1)}, u32[]{:S(2)}, u32[]{:S(2)}) collective-permute-start(f32[288,512]{1,0:T(8,128)} %get-tuple-element.46), channel_id=1, source_target_pairs={{0,4},{4,8},{8,12},{12,0},{64,68},{68,72},{72,76},{76,64},{16,20},... | collective-permute-start | bytes 1769480 | tf_op jit(solution)/shard_map/ppermute | solution.py:48
  63.0 1.3 collective-permute-start.8
  64.3 1.7 %collective-permute-start.9 = (f32[288,512]{1,0:T(8,128)S(1)}, f32[288,512]{1,0:T(8,128)S(1)}, u32[]{:S(2)}, u32[]{:S(2)}) collective-permute-start(f32[288,512]{1,0:T(8,128)S(1)} %get-tuple-element.48), channel_id=1, source_target_pairs={{0,8},{4,12},{8,0},{12,4},{64,72},{68,76},{72,64},{76,68},{16,24},... | collective-permute-start | bytes 1769480 | tf_op jit(solution)/shard_map/ppermute | solution.py:48
  66.0 8.7 %shard_map.133 = bf16[1,2048,1024]{2,1,0:T(8,128)(2,1)} custom-call(bf16[1024,1024]{1,0:T(8,128)(2,1)} %get-tuple-element.49.dpre0, bf16[1024,1024]{1,0:T(8,128)(2,1)} %get-tuple-element.50.dpre1, bf16[1024,1024]{1,0:T(8,128)(2,1)} %w.5), custom_call_target="tpu_custom_call" | custom-call | flops 4294967296 | bytes 10485760 | tf_op jit(solution)/shard_map/pallas_call | solution.py:243
  74.8 4.8 %collective-permute-done.9 = f32[288,512]{1,0:T(8,128)S(1)} collective-permute-done((f32[288,512]{1,0:T(8,128)S(1)}, f32[288,512]{1,0:T(8,128)S(1)}, u32[]{:S(2)}, u32[]{:S(2)}) %collective-permute-start.9) | collective-permute-done | bytes 589856 | tf_op jit(solution)/shard_map/ppermute | solution.py:48
  79.9 1.4 %collective-permute-start.10 = (f32[72,512]{1,0:T(8,128)S(1)}, f32[72,512]{1,0:T(8,128)S(1)}, u32[]{:S(2)}, u32[]{:S(2)}) collective-permute-start(f32[72,512]{1,0:T(8,128)S(1)} %get-tuple-element.64), channel_id=1, source_target_pairs={{0,1},{4,5},{8,9},{12,13},{64,65},{68,69},{72,73},{76,77},{16,17},... | collective-permute-start | bytes 442376 | tf_op jit(solution)/shard_map/ppermute | solution.py:48
  81.3 2.2 %collective-permute-start.11 = (f32[72,512]{1,0:T(8,128)S(1)}, f32[72,512]{1,0:T(8,128)S(1)}, u32[]{:S(2)}, u32[]{:S(2)}) collective-permute-start(f32[72,512]{1,0:T(8,128)S(1)} %get-tuple-element.66), channel_id=1, source_target_pairs={{0,3},{4,7},{8,11},{12,15},{64,67},{68,71},{72,75},{76,79},{16,19}... | collective-permute-start | bytes 442376 | tf_op jit(solution)/shard_map/ppermute | solution.py:48
  83.5 1.2 collective-permute-start.12
  84.7 1.2 collective-permute-done.10
  85.9 3.0 %collective-permute-done.12 = f32[72,512]{1,0:T(8,128)S(1)} collective-permute-done((f32[72,512]{1,0:T(8,128)S(1)}, f32[72,512]{1,0:T(8,128)S(1)}, u32[]{:S(2)}, u32[]{:S(2)}) %collective-permute-start.12) | collective-permute-done | bytes 147488 | tf_op jit(solution)/shard_map/ppermute | solution.py:48
  89.0 1.4 collective-permute-start.13
  90.4 1.5 %collective-permute-start.14 = (f32[72,512]{1,0:T(8,128)S(1)}, f32[72,512]{1,0:T(8,128)S(1)}, u32[]{:S(2)}, u32[]{:S(2)}) collective-permute-start(f32[72,512]{1,0:T(8,128)S(1)} %fusion.5), channel_id=1, source_target_pairs={{0,80},{4,84},{8,88},{12,92},{64,0},{68,4},{72,8},{76,12},{16,64},... | collective-permute-start | bytes 442376 | tf_op jit(solution)/shard_map/ppermute | solution.py:48
  91.9 1.6 %collective-permute-start.15 = (f32[72,512]{1,0:T(8,128)S(1)}, f32[72,512]{1,0:T(8,128)S(1)}, u32[]{:S(2)}, u32[]{:S(2)}) collective-permute-start(f32[72,512]{1,0:T(8,128)S(1)} %fusion.5), channel_id=1, source_target_pairs={{0,16},{4,20},{8,24},{12,28},{64,80},{68,84},{72,88},{76,92},{16,0... | collective-permute-start | bytes 442376 | tf_op jit(solution)/shard_map/ppermute | solution.py:48
  93.5 0.9 collective-permute-done.13
  94.4 3.1 %collective-permute-done.15 = f32[72,512]{1,0:T(8,128)S(1)} collective-permute-done((f32[72,512]{1,0:T(8,128)S(1)}, f32[72,512]{1,0:T(8,128)S(1)}, u32[]{:S(2)}, u32[]{:S(2)}) %collective-permute-start.15) | collective-permute-done | bytes 147488 | tf_op jit(solution)/shard_map/ppermute | solution.py:48
  97.6 1.5 %collective-permute-start.16 = (f32[72,512]{1,0:T(8,128)S(1)}, f32[72,512]{1,0:T(8,128)S(1)}, u32[]{:S(2)}, u32[]{:S(2)}) collective-permute-start(f32[72,512]{1,0:T(8,128)S(1)} %add_add_fusion.1), channel_id=1, source_target_pairs={{0,3},{4,7},{8,11},{12,15},{64,67},{68,71},{72,75},{76,79},{16,19}... | collective-permute-start | bytes 442376 | tf_op jit(solution)/shard_map/ppermute | solution.py:48
  99.0 1.4 collective-permute-start.17
  100.4 0.8 collective-permute-start.18
  101.1 0.6 collective-permute-done.16
  101.8 2.8 %collective-permute-done.17 = f32[72,512]{1,0:T(8,128)S(1)} collective-permute-done((f32[72,512]{1,0:T(8,128)S(1)}, f32[72,512]{1,0:T(8,128)S(1)}, u32[]{:S(2)}, u32[]{:S(2)}) %collective-permute-start.17) | collective-permute-done | bytes 147488 | tf_op jit(solution)/shard_map/ppermute | solution.py:48
  104.6 1.5 %collective-permute-done.18 = f32[72,512]{1,0:T(8,128)S(1)} collective-permute-done((f32[72,512]{1,0:T(8,128)S(1)}, f32[72,512]{1,0:T(8,128)S(1)}, u32[]{:S(2)}, u32[]{:S(2)}) %collective-permute-start.18) | collective-permute-done | bytes 147488 | tf_op jit(solution)/shard_map/ppermute | solution.py:48
  106.2 1.8 %collective-permute-start.19 = (f32[288,512]{1,0:T(8,128)S(1)}, f32[288,512]{1,0:T(8,128)S(1)}, u32[]{:S(2)}, u32[]{:S(2)}) collective-permute-start(f32[288,512]{1,0:T(8,128)S(1)} %constant_dynamic-slice_fusion.refs_0_), channel_id=1, source_target_pairs={{0,4},{4,8},{8,12},{12,0},{64,68},{68,72},{72,76},{76,64},{16,20},... | collective-permute-start | bytes 1769480 | tf_op jit(solution)/shard_map/ppermute | solution.py:48
  108.1 2.1 %collective-permute-start.20 = (f32[288,512]{1,0:T(8,128)S(1)}, f32[288,512]{1,0:T(8,128)S(1)}, u32[]{:S(2)}, u32[]{:S(2)}) collective-permute-start(f32[288,512]{1,0:T(8,128)S(1)} %constant_dynamic-slice_fusion.refs_0_), channel_id=1, source_target_pairs={{0,8},{4,12},{8,0},{12,4},{64,72},{68,76},{72,64},{76,68},{16,24},... | collective-permute-start | bytes 1769480 | tf_op jit(solution)/shard_map/ppermute | solution.py:48
  110.6 7.4 %collective-permute-start.22 = (f32[288,512]{1,0:T(8,128)S(1)}, f32[288,512]{1,0:T(8,128)S(1)}, u32[]{:S(2)}, u32[]{:S(2)}) collective-permute-start(f32[288,512]{1,0:T(8,128)S(1)} %constant_dynamic-slice_fusion.refs_0_), channel_id=1, source_target_pairs={{0,32},{4,36},{8,40},{12,44},{64,96},{68,100},{72,104},{76,108},{1... | collective-permute-start | bytes 1769480 | tf_op jit(solution)/shard_map/ppermute | solution.py:48
  118.0 6.7 %collective-permute-start.23 = (f32[288,512]{1,0:T(8,128)S(1)}, f32[288,512]{1,0:T(8,128)S(1)}, u32[]{:S(2)}, u32[]{:S(2)}) collective-permute-start(f32[288,512]{1,0:T(8,128)S(1)} %collective-permute-done.19.refs_1_), channel_id=1, source_target_pairs={{0,32},{4,36},{8,40},{12,44},{64,96},{68,100},{72,104},{76,108},{1... | collective-permute-start | bytes 1769480 | tf_op jit(solution)/shard_map/ppermute | solution.py:48
  124.7 6.5 %collective-permute-start.24 = (f32[288,512]{1,0:T(8,128)S(1)}, f32[288,512]{1,0:T(8,128)S(1)}, u32[]{:S(2)}, u32[]{:S(2)}) collective-permute-start(f32[288,512]{1,0:T(8,128)S(1)} %collective-permute-done.20.refs_2_), channel_id=1, source_target_pairs={{0,32},{4,36},{8,40},{12,44},{64,96},{68,100},{72,104},{76,108},{1... | collective-permute-start | bytes 1769480 | tf_op jit(solution)/shard_map/ppermute | solution.py:48
  131.3 0.7 collective-permute-start.25
  132.0 0.9 collective-permute-done.24.refs_6_
  132.9 0.8 collective-permute-done.25.refs_7_
  133.7 2.9 %shard_map.134 = (f32[1024,1024]{1,0:T(8,128)}, f32[100,1024]{1,0:T(8,128)}, f32[1,1024]{1,0:T(1,128)}, f32[1,100]{1,0:T(1,128)}, f32[1,1]{1,0:T(1,128)}) custom-call(s32[3]{0:T(128)S(1)} %pad_add_fusion.where, f32[288,512]{1,0:T(8,128)S(1)} %constant_dynamic-slice_fusion.refs_0_, f32[288,512]{1,0:T(8,128)S(1)} %collective-permute-done.19.refs_1_, ...), custom_call_target="tpu_custom_call" | custom-call | bytes 8388608 | tf_op jit(solution)/shard_map/pallas_call | solution.py:278
  (43 shorter events, 2.5 us)
Async XLA Ops:
  9.3 14.9 %copy-start.6 = (f32[100]{0:T(128)S(1)}, f32[100]{0:T(128)}, u32[]{:S(2)}) copy-start(f32[100]{0:T(128)} %param.11) | copy-start | bytes 1204
  9.3 11.7 %collective-permute-start.1 = (f32[100,1024]{1,0:T(8,128)}, f32[100,1024]{1,0:T(8,128)S(1)}, u32[]{:S(2)}, u32[]{:S(2)}) collective-permute-start(f32[100,1024]{1,0:T(8,128)} %get-tuple-element.33.own), channel_id=1, source_target_pairs={{0,64},{4,68},{8,72},{12,76},{64,0},{68,4},{72,8},{76,12},{16,80},... | collective-permute-start | bytes 1228808 | tf_op jit(solution)/shard_map/ppermute | solution.py:48
  11.5 13.5 %collective-permute-start = (f32[100,1024]{1,0:T(8,128)}, f32[100,1024]{1,0:T(8,128)S(1)}, u32[]{:S(2)}, u32[]{:S(2)}) collective-permute-start(f32[100,1024]{1,0:T(8,128)} %get-tuple-element.33.own), channel_id=1, source_target_pairs={{0,32},{4,36},{8,40},{12,44},{64,96},{68,100},{72,104},{76,108},{1... | collective-permute-start | bytes 1228808 | tf_op jit(solution)/shard_map/ppermute | solution.py:48
  21.0 4.0 %copy-start.3 = (f32[100,1024]{1,0:T(8,128)}, f32[100,1024]{1,0:T(8,128)S(1)}, u32[]{:S(2)}) copy-start(f32[100,1024]{1,0:T(8,128)S(1)} %collective-permute-done.1.o2) | copy-start | bytes 1228804
  21.0 4.0 %collective-permute-start.2 = (f32[100,1024]{1,0:T(8,128)S(1)}, f32[100,1024]{1,0:T(8,128)S(1)}, u32[]{:S(2)}, u32[]{:S(2)}) collective-permute-start(f32[100,1024]{1,0:T(8,128)S(1)} %collective-permute-done.1.o2), channel_id=1, source_target_pairs={{0,32},{4,36},{8,40},{12,44},{64,96},{68,100},{72,104},{76,108},{1... | collective-permute-start | bytes 1228808 | tf_op jit(solution)/shard_map/ppermute | solution.py:48
  22.5 11.7 %collective-permute-start.4 = (f32[100,1024]{1,0:T(8,128)}, f32[100,1024]{1,0:T(8,128)S(1)}, u32[]{:S(2)}, u32[]{:S(2)}) collective-permute-start(f32[100,1024]{1,0:T(8,128)} %get-tuple-element.34.own), channel_id=1, source_target_pairs={{0,64},{4,68},{8,72},{12,76},{64,0},{68,4},{72,8},{76,12},{16,80},... | collective-permute-start | bytes 1228808 | tf_op jit(solution)/shard_map/ppermute | solution.py:48
  23.9 11.7 %collective-permute-start.3 = (f32[100,1024]{1,0:T(8,128)}, f32[100,1024]{1,0:T(8,128)S(1)}, u32[]{:S(2)}, u32[]{:S(2)}) collective-permute-start(f32[100,1024]{1,0:T(8,128)} %get-tuple-element.34.own), channel_id=1, source_target_pairs={{0,32},{4,36},{8,40},{12,44},{64,96},{68,100},{72,104},{76,108},{1... | collective-permute-start | bytes 1228808 | tf_op jit(solution)/shard_map/ppermute | solution.py:48
  24.9 0.8 copy-start.4
  25.0 1.0 copy-start.5
  34.1 2.2 %copy-start = (f32[100,1024]{1,0:T(8,128)}, f32[100,1024]{1,0:T(8,128)S(1)}, u32[]{:S(2)}) copy-start(f32[100,1024]{1,0:T(8,128)S(1)} %collective-permute-done.4.o2) | copy-start | bytes 1228804
  34.1 2.2 %collective-permute-start.5 = (f32[100,1024]{1,0:T(8,128)S(1)}, f32[100,1024]{1,0:T(8,128)S(1)}, u32[]{:S(2)}, u32[]{:S(2)}) collective-permute-start(f32[100,1024]{1,0:T(8,128)S(1)} %collective-permute-done.4.o2), channel_id=1, source_target_pairs={{0,32},{4,36},{8,40},{12,44},{64,96},{68,100},{72,104},{76,108},{1... | collective-permute-start | bytes 1228808 | tf_op jit(solution)/shard_map/ppermute | solution.py:48
  35.6 0.8 copy-start.1
  36.3 0.8 copy-start.2
  50.9 7.5 %collective-permute-start.6 = (f32[4,288,512]{2,1,0:T(8,128)}, f32[4,288,512]{2,1,0:T(8,128)S(1)}, u32[]{:S(2)}, u32[]{:S(2)}) collective-permute-start(f32[4,288,512]{2,1,0:T(8,128)} %shard_map.132), channel_id=1, source_target_pairs={{0,32},{4,36},{8,40},{12,44},{64,96},{68,100},{72,104},{76,108},{1... | collective-permute-start | bytes 7077896 | tf_op jit(solution)/shard_map/ppermute | solution.py:48
  61.7 13.1 %collective-permute-start.7 = (f32[288,512]{1,0:T(8,128)}, f32[288,512]{1,0:T(8,128)S(1)}, u32[]{:S(2)}, u32[]{:S(2)}) collective-permute-start(f32[288,512]{1,0:T(8,128)} %get-tuple-element.46), channel_id=1, source_target_pairs={{0,4},{4,8},{8,12},{12,0},{64,68},{68,72},{72,76},{76,64},{16,20},... | collective-permute-start | bytes 1769480 | tf_op jit(solution)/shard_map/ppermute | solution.py:48
  63.0 11.7 %collective-permute-start.8 = (f32[288,512]{1,0:T(8,128)}, f32[288,512]{1,0:T(8,128)S(1)}, u32[]{:S(2)}, u32[]{:S(2)}) collective-permute-start(f32[288,512]{1,0:T(8,128)} %get-tuple-element.47), channel_id=1, source_target_pairs={{0,12},{4,0},{8,4},{12,8},{64,76},{68,64},{72,68},{76,72},{16,28},... | collective-permute-start | bytes 1769480 | tf_op jit(solution)/shard_map/ppermute | solution.py:48
  64.3 15.2 %collective-permute-start.9 = (f32[288,512]{1,0:T(8,128)S(1)}, f32[288,512]{1,0:T(8,128)S(1)}, u32[]{:S(2)}, u32[]{:S(2)}) collective-permute-start(f32[288,512]{1,0:T(8,128)S(1)} %get-tuple-element.48), channel_id=1, source_target_pairs={{0,8},{4,12},{8,0},{12,4},{64,72},{68,76},{72,64},{76,68},{16,24},... | collective-permute-start | bytes 1769480 | tf_op jit(solution)/shard_map/ppermute | solution.py:48
  79.9 6.1 %collective-permute-start.10 = (f32[72,512]{1,0:T(8,128)S(1)}, f32[72,512]{1,0:T(8,128)S(1)}, u32[]{:S(2)}, u32[]{:S(2)}) collective-permute-start(f32[72,512]{1,0:T(8,128)S(1)} %get-tuple-element.64), channel_id=1, source_target_pairs={{0,1},{4,5},{8,9},{12,13},{64,65},{68,69},{72,73},{76,77},{16,17},... | collective-permute-start | bytes 442376 | tf_op jit(solution)/shard_map/ppermute | solution.py:48
  81.3 4.7 %collective-permute-start.11 = (f32[72,512]{1,0:T(8,128)S(1)}, f32[72,512]{1,0:T(8,128)S(1)}, u32[]{:S(2)}, u32[]{:S(2)}) collective-permute-start(f32[72,512]{1,0:T(8,128)S(1)} %get-tuple-element.66), channel_id=1, source_target_pairs={{0,3},{4,7},{8,11},{12,15},{64,67},{68,71},{72,75},{76,79},{16,19}... | collective-permute-start | bytes 442376 | tf_op jit(solution)/shard_map/ppermute | solution.py:48
  83.5 5.5 %collective-permute-start.12 = (f32[72,512]{1,0:T(8,128)S(1)}, f32[72,512]{1,0:T(8,128)S(1)}, u32[]{:S(2)}, u32[]{:S(2)}) collective-permute-start(f32[72,512]{1,0:T(8,128)S(1)} %get-tuple-element.65), channel_id=1, source_target_pairs={{0,2},{4,6},{8,10},{12,14},{64,66},{68,70},{72,74},{76,78},{16,18}... | collective-permute-start | bytes 442376 | tf_op jit(solution)/shard_map/ppermute | solution.py:48
  89.0 5.3 %collective-permute-start.13 = (f32[72,512]{1,0:T(8,128)S(1)}, f32[72,512]{1,0:T(8,128)S(1)}, u32[]{:S(2)}, u32[]{:S(2)}) collective-permute-start(f32[72,512]{1,0:T(8,128)S(1)} %fusion.5), channel_id=1, source_target_pairs={{0,64},{4,68},{8,72},{12,76},{64,16},{68,20},{72,24},{76,28},{16,8... | collective-permute-start | bytes 442376 | tf_op jit(solution)/shard_map/ppermute | solution.py:48
  90.4 4.0 %collective-permute-start.14 = (f32[72,512]{1,0:T(8,128)S(1)}, f32[72,512]{1,0:T(8,128)S(1)}, u32[]{:S(2)}, u32[]{:S(2)}) collective-permute-start(f32[72,512]{1,0:T(8,128)S(1)} %fusion.5), channel_id=1, source_target_pairs={{0,80},{4,84},{8,88},{12,92},{64,0},{68,4},{72,8},{76,12},{16,64},... | collective-permute-start | bytes 442376 | tf_op jit(solution)/shard_map/ppermute | solution.py:48
  91.9 5.6 %collective-permute-start.15 = (f32[72,512]{1,0:T(8,128)S(1)}, f32[72,512]{1,0:T(8,128)S(1)}, u32[]{:S(2)}, u32[]{:S(2)}) collective-permute-start(f32[72,512]{1,0:T(8,128)S(1)} %fusion.5), channel_id=1, source_target_pairs={{0,16},{4,20},{8,24},{12,28},{64,80},{68,84},{72,88},{76,92},{16,0... | collective-permute-start | bytes 442376 | tf_op jit(solution)/shard_map/ppermute | solution.py:48
  97.6 4.2 %collective-permute-start.16 = (f32[72,512]{1,0:T(8,128)S(1)}, f32[72,512]{1,0:T(8,128)S(1)}, u32[]{:S(2)}, u32[]{:S(2)}) collective-permute-start(f32[72,512]{1,0:T(8,128)S(1)} %add_add_fusion.1), channel_id=1, source_target_pairs={{0,3},{4,7},{8,11},{12,15},{64,67},{68,71},{72,75},{76,79},{16,19}... | collective-permute-start | bytes 442376 | tf_op jit(solution)/shard_map/ppermute | solution.py:48
  99.0 5.6 %collective-permute-start.17 = (f32[72,512]{1,0:T(8,128)S(1)}, f32[72,512]{1,0:T(8,128)S(1)}, u32[]{:S(2)}, u32[]{:S(2)}) collective-permute-start(f32[72,512]{1,0:T(8,128)S(1)} %add_add_fusion.1), channel_id=1, source_target_pairs={{0,2},{4,6},{8,10},{12,14},{64,66},{68,70},{72,74},{76,78},{16,18}... | collective-permute-start | bytes 442376 | tf_op jit(solution)/shard_map/ppermute | solution.py:48
  100.4 5.7 %collective-permute-start.18 = (f32[72,512]{1,0:T(8,128)S(1)}, f32[72,512]{1,0:T(8,128)S(1)}, u32[]{:S(2)}, u32[]{:S(2)}) collective-permute-start(f32[72,512]{1,0:T(8,128)S(1)} %add_add_fusion.1), channel_id=1, source_target_pairs={{0,1},{4,5},{8,9},{12,13},{64,65},{68,69},{72,73},{76,77},{16,17},... | collective-permute-start | bytes 442376 | tf_op jit(solution)/shard_map/ppermute | solution.py:48
  106.2 11.8 %collective-permute-start.19 = (f32[288,512]{1,0:T(8,128)S(1)}, f32[288,512]{1,0:T(8,128)S(1)}, u32[]{:S(2)}, u32[]{:S(2)}) collective-permute-start(f32[288,512]{1,0:T(8,128)S(1)} %constant_dynamic-slice_fusion.refs_0_), channel_id=1, source_target_pairs={{0,4},{4,8},{8,12},{12,0},{64,68},{68,72},{72,76},{76,64},{16,20},... | collective-permute-start | bytes 1769480 | tf_op jit(solution)/shard_map/ppermute | solution.py:48
  108.1 16.6 %collective-permute-start.20 = (f32[288,512]{1,0:T(8,128)S(1)}, f32[288,512]{1,0:T(8,128)S(1)}, u32[]{:S(2)}, u32[]{:S(2)}) collective-permute-start(f32[288,512]{1,0:T(8,128)S(1)} %constant_dynamic-slice_fusion.refs_0_), channel_id=1, source_target_pairs={{0,8},{4,12},{8,0},{12,4},{64,72},{68,76},{72,64},{76,68},{16,24},... | collective-permute-start | bytes 1769480 | tf_op jit(solution)/shard_map/ppermute | solution.py:48
  110.2 21.1 %collective-permute-start.21 = (f32[288,512]{1,0:T(8,128)S(1)}, f32[288,512]{1,0:T(8,128)S(1)}, u32[]{:S(2)}, u32[]{:S(2)}) collective-permute-start(f32[288,512]{1,0:T(8,128)S(1)} %constant_dynamic-slice_fusion.refs_0_), channel_id=1, source_target_pairs={{0,12},{4,0},{8,4},{12,8},{64,76},{68,64},{72,68},{76,72},{16,28},... | collective-permute-start | bytes 1769480 | tf_op jit(solution)/shard_map/ppermute | solution.py:48
  110.6 21.4 %collective-permute-start.22 = (f32[288,512]{1,0:T(8,128)S(1)}, f32[288,512]{1,0:T(8,128)S(1)}, u32[]{:S(2)}, u32[]{:S(2)}) collective-permute-start(f32[288,512]{1,0:T(8,128)S(1)} %constant_dynamic-slice_fusion.refs_0_), channel_id=1, source_target_pairs={{0,32},{4,36},{8,40},{12,44},{64,96},{68,100},{72,104},{76,108},{1... | collective-permute-start | bytes 1769480 | tf_op jit(solution)/shard_map/ppermute | solution.py:48
  118.0 14.0 %collective-permute-start.23 = (f32[288,512]{1,0:T(8,128)S(1)}, f32[288,512]{1,0:T(8,128)S(1)}, u32[]{:S(2)}, u32[]{:S(2)}) collective-permute-start(f32[288,512]{1,0:T(8,128)S(1)} %collective-permute-done.19.refs_1_), channel_id=1, source_target_pairs={{0,32},{4,36},{8,40},{12,44},{64,96},{68,100},{72,104},{76,108},{1... | collective-permute-start | bytes 1769480 | tf_op jit(solution)/shard_map/ppermute | solution.py:48
  124.7 8.2 %collective-permute-start.24 = (f32[288,512]{1,0:T(8,128)S(1)}, f32[288,512]{1,0:T(8,128)S(1)}, u32[]{:S(2)}, u32[]{:S(2)}) collective-permute-start(f32[288,512]{1,0:T(8,128)S(1)} %collective-permute-done.20.refs_2_), channel_id=1, source_target_pairs={{0,32},{4,36},{8,40},{12,44},{64,96},{68,100},{72,104},{76,108},{1... | collective-permute-start | bytes 1769480 | tf_op jit(solution)/shard_map/ppermute | solution.py:48
  131.3 2.5 %collective-permute-start.25 = (f32[288,512]{1,0:T(8,128)S(1)}, f32[288,512]{1,0:T(8,128)S(1)}, u32[]{:S(2)}, u32[]{:S(2)}) collective-permute-start(f32[288,512]{1,0:T(8,128)S(1)} %collective-permute-done.21.refs_3_), channel_id=1, source_target_pairs={{0,32},{4,36},{8,40},{12,44},{64,96},{68,100},{72,104},{76,108},{1... | collective-permute-start | bytes 1769480 | tf_op jit(solution)/shard_map/ppermute | solution.py:48

commit v4 on v3

--- a/solution.py
+++ b/solution.py
@@ -52,12 +52,14 @@
     core, x, z = lax.axis_index("core"), lax.axis_index("x"), lax.axis_index("z")
     place = jnp.where(core == 0, x, z)
     got = send(sibling, SWAP)
-    held = [own[k] + got[k] for k in range(4)]
-    held, dpre = lax.optimization_barrier((held, dpre))
+    held = {}
+    for k in (2, 1, 3, 0):
+        held[k], own, got = lax.optimization_barrier((own[k] + got[k], own, got))
+    kept, dpre = lax.optimization_barrier((held[0], dpre))
     aside = beside(dpre)
-    came = [send(held[k], first(k)) for k in (1, 3, 2)]
-    *came, aside = lax.optimization_barrier((*came, aside))
-    block = held[0] + came[0] + came[1] + came[2]
+    came = [send(held[k], first(k)) for k in (2, 1, 3)]
+    came, aside = lax.optimization_barrier((came, aside))
+    block = kept + came[0] + came[1] + came[2]
     rows = block.shape[0] // 4
     quarters = block.reshape((4, rows) + block.shape[1:])
     pick = lambda k: lax.dynamic_index_in_dim(quarters, (place + k) % 4, 0, keepdims=False)
@@ -80,19 +82,17 @@
     return pl.CostEstimate(flops=flops, bytes_accessed=moved_bytes, transcendentals=trans)
 
 
-def forward_kernel(lat, w, b_hid, w_out, b_out, *refs):
-    pred, hid, slope_out = refs[-3:]
+def forward_kernel(lat, w, b_hid, w_out, b_out, pred, hid, slope_out):
     cols = 256
-    turned = b_out[...]
     for j in range(0, w.shape[1], cols):
         at = slice(j, j + cols)
         pre = jnp.dot(lat[...], w[:, at], preferred_element_type=F32) + b_hid[:, at]
         sig = jax.nn.sigmoid(pre)
-        h = (pre * sig).astype(BF16)
-        hid[:, at] = h
+        hid[:, at] = (pre * sig).astype(BF16)
         slope_out[:, at] = sig * (1.0 + pre * (1.0 - sig))
-        turned = turned + lax.dot_general(h, w_out[:, at], (((1,), (1,)), ((), ())), preferred_element_type=F32)
-    pred[...] = jnp.transpose(turned)
+    n_vars = w_out.shape[0]
+    bias = jnp.transpose(jnp.broadcast_to(b_out[...], (128, n_vars)))[:, 0:1]
+    pred[...] = bias + lax.dot_general(w_out[...], hid[...], (((1,), (1,)), ((), ())), preferred_element_type=F32)
 
 
 def forward(part, n, latent, w_hidden, b_hidden, w_output, b_output, tile=512):
@@ -122,92 +122,165 @@
     )(latent, w_hidden, b_hidden.reshape(1, width), w_output, b_output.reshape(1, n_vars))
 
 
-def cot_kernel(members, scale, loss_scale, pair_coef, own, o1, o2, o3, target, area, var, sp, hid, w_out, *refs):
-    dpre, rest, cot_held = refs[-3:]
+def cot_tile(members, scale, loss_scale, pair_coef, own, o1, o2, o3, target, area, var, sp, hid, w_out, rest):
     n_vars, n = own.shape
-    j = pl.program_id(0)
-    rest[...] = refs[0][...] if len(refs) > 3 else jnp.zeros_like(rest)
-
-    @pl.when(j == 0)
-    def _():
-        weights = var[...] * area[...]
-        mine = own[...]
-
-        def both(diff):
-            u = diff * diff + DELTA * DELTA
-            r = lax.rsqrt(u)
-            return u * r - DELTA, diff * r
-
-        mag, slo = both(mine - target[...])
-        pair_mag, pair_slo = jnp.zeros_like(mine), jnp.zeros_like(mine)
-        for other in (o1, o2, o3):
-            m, s = both(mine - other[...])
-            pair_mag, pair_slo = pair_mag + m, pair_slo + s
-        term = weights * (mag * (1.0 / members) - (0.5 * pair_coef) * pair_mag)
-        cot = (weights * (slo * (1.0 / members) - pair_coef * pair_slo)).astype(BF16)
-        cot_held[...] = cot
-        sums = lax.dot_general(
-            jnp.ones((16, n), BF16), cot, (((1,), (1,)), ((), ())), preferred_element_type=F32
-        )[0:1]
-        rest[n_vars + 1 : n_vars + 2, 0:n_vars] += sums * scale
-        rest[n_vars + 2 : n_vars + 3, 0:128] += jnp.full((1, 128), jnp.sum(term) * loss_scale, F32)
-
-    cot = cot_held[...]
+    weights = var[...] * area[...]
+    mine = own[...]
+
+    def both(diff):
+        u = diff * diff + DELTA * DELTA
+        r = lax.rsqrt(u)
+        return u * r - DELTA, diff * r
+
+    mag, slo = both(mine - target[...])
+    pair_mag, pair_slo = jnp.zeros_like(mine), jnp.zeros_like(mine)
+    for other in (o1, o2, o3):
+        m, s = both(mine - other[...])
+        pair_mag, pair_slo = pair_mag + m, pair_slo + s
+    term = weights * (mag * (1.0 / members) - (0.5 * pair_coef) * pair_mag)
+    cot = (weights * (slo * (1.0 / members) - pair_coef * pair_slo)).astype(BF16)
+    sums = lax.dot_general(
+        jnp.ones((16, n), BF16), cot, (((1,), (1,)), ((), ())), preferred_element_type=F32
+    )[0:1]
+    rest[n_vars + 1 : n_vars + 2, 0:n_vars] += sums * scale
+    rest[n_vars + 2 : n_vars + 3, 0:128] += jnp.full((1, 128), jnp.sum(term) * loss_scale, F32)
+
     back = lax.dot_general(cot, w_out[...], (((0,), (0,)), ((), ())), preferred_element_type=F32)
     d = (back * sp[...]).astype(BF16)
-    dpre[...] = d
     rest[0:n_vars, :] += jnp.dot(cot, hid[...], preferred_element_type=F32) * scale
     rest[n_vars : n_vars + 1, :] += jnp.sum(d.astype(F32), axis=0, keepdims=True) * scale
-
-
-def cotangent(part, n, own, others, target, area, var, sp, hid, w_output, held, members, scale, loss_scale, pair_coef, cols=256):
-    n_vars, width = target.shape[0], sp.shape[1]
-    local = pl.BlockSpec((n_vars, n), lambda j: (0, 0))
-    block = pl.BlockSpec((n, cols), lambda j: (0, j))
-    rest = pl.BlockSpec((128, cols), lambda j: (0, j))
-    return pl.pallas_call(
-        functools.partial(cot_kernel, members, scale, loss_scale, pair_coef),
-        grid=(width // cols,),
+    return d
+
+
+def cot_kernel(numbers, *refs):
+    dpre, rest = refs[-2:]
+
+    @pl.when(pl.program_id(0) == 0)
+    def _():
+        rest[...] = jnp.zeros_like(rest)
+
+    dpre[...] = cot_tile(*numbers, *refs[:10], rest)
+
+
+def weight_blocks(scale, which, where, step, lats, dpres, rest, out):
+    rows, half = lats[0].shape[1], out.shape[2]
+    for j, lat in enumerate(lats):
+        total, start = 0.0, 0
+        for d in dpres:
+            n = d.shape[0]
+            total += lax.dot_general(
+                lat[start : start + n, :], d, (((0,), (0,)), ((), ())), preferred_element_type=F32
+            )
+            start += n
+        block = lax.rem(where[2 + which] + 2 * step + j, 4)
+        out[j, 0:rows, :] = total * scale
+        cols = pl.ds(pl.multiple_of(where[which] * half, half), half)
+        out[j, rows : rows + 32, :] = rest[pl.ds(pl.multiple_of(block * 32, 32), 32), cols]
+
+
+def cot_weight_kernel(numbers, steps, which, where, *refs):
+    ins, (rest_in, lat0, lat1, dpre0), (dpre, rest, out, held) = refs[:10], refs[10:14], refs[14:]
+    g = pl.program_id(0)
+    tile, half = dpre.shape[0], out.shape[2]
+
+    @pl.when(g == 0)
+    def _():
+        rest[...] = rest_in[...]
+
+    @pl.when(g < steps)
+    def _():
+        d = cot_tile(*numbers, *ins, rest)
+        dpre[...] = d
+        held[pl.ds(pl.multiple_of(g * tile, tile), tile), :] = d
+
+    @pl.when(g >= steps)
+    def _():
+        cols = pl.ds(pl.multiple_of(where[which] * half, half), half)
+        weight_blocks(numbers[1], which, where, g - steps, (lat0, lat1), (dpre0[...], held[:, cols]), rest, out)
+
+
+def cotangent(numbers, part, own, others, target, area, var, sp, hid, w_output, tile=512):
+    n, width = sp.shape
+    n_vars, steps = target.shape[0], n // tile
+    whole = lambda shape: pl.BlockSpec(shape, lambda g: (0, 0))
+    local = pl.BlockSpec((n_vars, tile), lambda g: (0, g))
+    rows = pl.BlockSpec((tile, width), lambda g: (g, 0))
+    return pl.pallas_call(
+        functools.partial(cot_kernel, numbers),
+        grid=(steps,),
         in_specs=[local] * 4
         + [
-            pl.BlockSpec((n_vars, n), lambda j: (0, part)),
-            pl.BlockSpec((1, n), lambda j: (0, part)),
-            pl.BlockSpec((n_vars, 1), lambda j: (0, 0)),
-            block,
-            block,
-            pl.BlockSpec((n_vars, cols), lambda j: (0, j)),
-        ]
-        + [rest] * len(held),
-        out_specs=[block, rest],
+            pl.BlockSpec((n_vars, tile), lambda g: (0, part * steps + g)),
+            pl.BlockSpec((1, tile), lambda g: (0, part * steps + g)),
+            whole((n_vars, 1)),
+            rows,
+            rows,
+            whole(w_output.shape),
+        ],
+        out_specs=[rows, whole((128, width))],
         out_shape=[
             jax.ShapeDtypeStruct((n, width), BF16),
             jax.ShapeDtypeStruct((128, width), F32),
         ],
-        scratch_shapes=[pltpu.VMEM((n_vars, n), BF16)],
         compiler_params=params(),
-        cost_estimate=cost(4 * n * n_vars * width, n * (n_vars * 20 + 8 * width), 4 * n * n_vars),
-    )(own, *others, target, area, var, sp, hid, w_output, *held)
-
-
-def weight_kernel(scale, where, lat0, lat1, dpre0, dpre1, rest, out):
-    rows, n = lat0.shape[1], dpre0.shape[0]
-    dims = (((0,), (0,)), ((), ()))
-    for j, lat in enumerate((lat0, lat1)):
-        block = lax.rem(where[1] + 2 * pl.program_id(0) + j, 4)
-        out[j, 0:rows, :] = (
-            lax.dot_general(lat[0:n, :], dpre0[...], dims, preferred_element_type=F32)
-            + lax.dot_general(lat[n : 2 * n, :], dpre1[...], dims, preferred_element_type=F32)
-        ) * scale
-        out[j, rows : rows + 32, :] = rest[pl.ds(pl.multiple_of(block * 32, 32), 32), :]
-
-
-def weight_grad(which, place, latent, dpre, rest, scale):
+        cost_estimate=cost(1, 1),
+    )(own, *others, target, area, var, sp, hid, w_output)
+
+
+def cotangent_weight(
+    numbers, part, which, where, own, others, target, area, var, sp, hid, w_output, rest, latent, dpre0, tile=512
+):
+    n, width = sp.shape
+    points, depth = latent.shape
+    n_vars, steps, half, block = target.shape[0], n // tile, width // 2, depth // 4
+    at = lambda g: jnp.minimum(g, steps - 1)
+    step = lambda g: jnp.maximum(g - steps, 0)
+    whole = lambda shape: pl.BlockSpec(shape, lambda g, s: (0, 0))
+    local = pl.BlockSpec((n_vars, tile), lambda g, s: (0, at(g)))
+    rows = pl.BlockSpec((tile, width), lambda g, s: (at(g), 0))
+    lat = lambda j: pl.BlockSpec((points, block), lambda g, s: (0, lax.rem(s[2 + which] + 2 * step(g) + j, 4)))
+    return pl.pallas_call(
+        functools.partial(cot_weight_kernel, numbers, steps, which),
+        grid_spec=pltpu.PrefetchScalarGridSpec(
+            num_scalar_prefetch=1,
+            grid=(steps + 2,),
+            in_specs=[local] * 4
+            + [
+                pl.BlockSpec((n_vars, tile), lambda g, s: (0, part * steps + at(g))),
+                pl.BlockSpec((1, tile), lambda g, s: (0, part * steps + at(g))),
+                whole((n_vars, 1)),
+                rows,
+                rows,
+                whole(w_output.shape),
+                whole((128, width)),
+                lat(0),
+                lat(1),
+                pl.BlockSpec((n, half), lambda g, s: (0, s[which])),
+            ],
+            out_specs=[rows, whole((128, width)), pl.BlockSpec((2, block + 32, half), lambda g, s: (step(g), 0, 0))],
+            scratch_shapes=[pltpu.VMEM((n, width), BF16)],
+        ),
+        out_shape=[
+            jax.ShapeDtypeStruct((n, width), BF16),
+            jax.ShapeDtypeStruct((128, width), F32),
+            jax.ShapeDtypeStruct((4, block + 32, half), F32),
+        ],
+        compiler_params=params(),
+        cost_estimate=cost(2 * points * half * depth, points * 2 * depth + n * (n_vars * 20 + 8 * width) + 4 * depth * half),
+    )(where, own, *others, target, area, var, sp, hid, w_output, rest, latent, latent, dpre0)
+
+
+def weight_kernel(scale, which, where, lat0, lat1, dpre0, dpre1, rest, out):
+    weight_blocks(scale, which, where, pl.program_id(0), (lat0, lat1), (dpre0[...], dpre1[...]), rest, out)
+
+
+def weight_grad(which, where, latent, dpre, rest, scale):
     (points, depth), width = latent.shape, dpre[0].shape[1]
     half, rows = width // 2, depth // 4
-    halves = pl.BlockSpec((points // 2, half), lambda g, s: (0, s[0]))
-    lat = lambda j: pl.BlockSpec((points, rows), lambda g, s: (0, lax.rem(s[1] + 2 * g + j, 4)))
-    return pl.pallas_call(
-        functools.partial(weight_kernel, scale),
+    halves = pl.BlockSpec((points // 2, half), lambda g, s: (0, s[which]))
+    lat = lambda j: pl.BlockSpec((points, rows), lambda g, s: (0, lax.rem(s[2 + which] + 2 * g + j, 4)))
+    return pl.pallas_call(
+        functools.partial(weight_kernel, scale, which),
         grid_spec=pltpu.PrefetchScalarGridSpec(
             num_scalar_prefetch=1,
             grid=(2,),
@@ -216,14 +289,14 @@
                 lat(1),
                 halves,
                 halves,
-                pl.BlockSpec((128, half), lambda g, s: (0, s[0])),
+                pl.BlockSpec((128, width), lambda g, s: (0, 0)),
             ],
             out_specs=pl.BlockSpec((2, rows + 32, half), lambda g, s: (g, 0, 0)),
         ),
         out_shape=jax.ShapeDtypeStruct((4, rows + 32, half), F32),
         compiler_params=params(),
         cost_estimate=cost(2 * points * half * depth, points * (2 * half + 2 * depth) + 4 * depth * half),
-    )(jnp.stack([which, place]).astype(jnp.int32), latent, latent, *dpre, rest)
+    )(where, latent, latent, *dpre, rest)
 
 
 def latent_kernel(steps, dpre0, dpre1, w, out):
@@ -259,10 +332,9 @@
     ins, (grad_w, grad_o, grad_b, grad_b_out, loss, rest) = refs[:8], refs[8:]
     rows, half = ins[0].shape[0] - 32, ins[0].shape[1]
     for which in range(2):
-        col = where[0] if which == 0 else 1 - where[0]
-        cols = pl.ds(pl.multiple_of(col * half, half), half)
+        cols = pl.ds(pl.multiple_of(where[which] * half, half), half)
         for k in range(4):
-            block = lax.rem(where[1 + which] - k + 4, 4)
+            block = lax.rem(where[2 + which] - k + 4, 4)
             grad_w[pl.ds(pl.multiple_of(block * rows, rows), rows), cols] = ins[4 * which + k][0:rows, :]
             rest[pl.ds(pl.multiple_of(block * 32, 32), 32), cols] = ins[4 * which + k][rows : rows + 32, :]
     grad_o[...] = rest[0:n_vars, :]
@@ -304,24 +376,26 @@
     core, x, z = lax.axis_index("core"), lax.axis_index("x"), lax.axis_index("z")
     place_own = jnp.where(core == 0, z, x)
     place_sib = jnp.where(core == 0, x, z)
+    where = jnp.stack([core, 1 - core, place_own, place_sib]).astype(jnp.int32)
     own_latent = latent[0]
     made = [forward(part, n, own_latent, w_hidden, b_hidden, w_output, b_output) for part, n in parts]
     area, var = area_weight.reshape(1, points), var_weight.reshape(n_vars, 1)
-    dpre, rest, after = [], (), made[-1][0]
-    for (part, n), (pred, hid, sp) in zip(parts, made):
-        near = send(pred, NEAR)
-        near, after = lax.optimization_barrier((near, after))
-        others = (send(pred, SWAP), near, send(near, SWAP))
-        d, total = cotangent(
-            part, n, pred, others, target, area, var, sp, hid, w_output, rest, members, scale, loss_scale, pair_coef
-        )
-        dpre.append(d)
-        rest, after = (total,), total
-    rest = after
-    blocks_sib = weight_grad(1 - core, place_sib, own_latent, dpre, rest, scale)
-    blocks_own = weight_grad(core, place_own, own_latent, dpre, rest, scale)
+    numbers = (members, scale, loss_scale, pair_coef)
+
+    (pred0, hid0, sp0), (pred1, hid1, sp1) = made
+    near0, near1 = send(pred0, NEAR), send(pred1, NEAR)
+    sib0, sib1 = send(pred0, SWAP), send(pred1, SWAP)
+    near0, sib0, sib1, where = lax.optimization_barrier((near0, sib0, sib1, where))
+    others = (sib0, near0, send(near0, SWAP))
+    dpre0, rest = cotangent(numbers, 0, pred0, others, target, area, var, sp0, hid0, w_output)
+    near1, rest = lax.optimization_barrier((near1, rest))
+    others = (sib1, near1, send(near1, SWAP))
+    dpre1, rest, blocks_sib = cotangent_weight(
+        numbers, 1, 1, where, pred1, others, target, area, var, sp1, hid1, w_output, rest, own_latent, dpre0
+    )
+    dpre = (dpre0, dpre1)
+    blocks_own = weight_grad(0, where, own_latent, dpre, rest, scale)
     out_own, out_sib, latent_grad = grad_sum(blocks_own, blocks_sib, lambda d: latent_gradient(d, w_hidden), dpre)
-    where = jnp.stack([core, place_own, place_sib]).astype(jnp.int32)
     grad_w_hidden, grad_w_output, grad_b_hidden, grad_b_output, loss = join(where, out_own, out_sib, n_vars)
     return (
         loss.reshape(()),

time: 137 us -> 133 us (0.971)
  waiting for transfers between devices: 21.6 us -> 36.6 us
  starting transfers between devices: 50.4 us -> 39.5 us
  Pallas kernels: 56.4 us -> 49.7 us
    ppermute x26, waiting for transfers between devices: 21.6 us -> 36.6 us  [send(): return lax.ppermute(array, ALL, pairs)]
    ppermute x26, starting transfers between devices: 50.4 us -> 39.5 us  [send(): return lax.ppermute(array, ALL, pairs)]
    pallas_call x4 -> x3, Pallas kernels: 27.6 us -> 23.6 us  [the longest x1 11.3 us: cotangent_weight(): pl.pallas_call(functools.partial(cot_weight_kernel, numbers, steps, which...]
    pallas_call x2, Pallas kernels: 17.2 us -> 14.4 us  [forward(): pl.pallas_call(forward_kernel, grid=(steps,), in_specs=[pl.BlockSpec((til...]
    add x2 -> x5, other arithmetic: 3.43 us -> 2.91 us  [the longest x4 2.66 us: grad_sum(): held[k], own, got = lax.optimization_barrier((own[k] + got[k], own, got))]
  transfers between devices with their start and end apart: 26 -> 26, of which waited for: 12 -> 17; matrix products, arithmetic and copies ran while one was open for 2% -> 1% of each run, Pallas kernels for 23% -> 21%
where the time goes in v4:
time: 133 us
  Pallas kernels  49.7 us (37%)
  starting transfers between devices  39.5 us (30%)
  waiting for transfers between devices  36.6 us (28%)
  other arithmetic  3.64 us (3%)
  local copies, waits for them, and re-layouts  2.5 us (2%)
    ppermute x26, starting transfers between devices, send(): return lax.ppermute(array, ALL, pairs)  39.5 us
    ppermute x26, waiting for transfers between devices, send(): return lax.ppermute(array, ALL, pairs)  36.6 us
    pallas_call x2, Pallas kernels, forward(): pl.pallas_call(forward_kernel, grid=(steps,), in_specs=[pl.BlockSpec((til...  14.4 us
    pallas_call x1, Pallas kernels, cotangent_weight(): pl.pallas_call(functools.partial(cot_weight_kernel, numbers, steps, which...  11.3 us
    pallas_call x1, Pallas kernels, latent_gradient(): pl.pallas_call(functools.partial(latent_kernel, steps), grid=(2 * steps,)...  8.76 us
    pallas_call x1, Pallas kernels, weight_grad(): pl.pallas_call(functools.partial(weight_kernel, scale, which), grid_spec=...  6.66 us
    pallas_call x1, Pallas kernels, cotangent(): pl.pallas_call(functools.partial(cot_kernel, numbers), grid=(steps,), in_...  5.66 us
    pallas_call x1, Pallas kernels, join(): pl.pallas_call(functools.partial(join_kernel, n_vars), in_specs=[pl.Block...  2.9 us
  transfers between devices with their start and end apart: 26, of which 17 were waited for; matrix products, arithmetic and copies ran while one was open for 1% of the time, Pallas kernels for 21%

profile of v4, /device:TPU:1, one launch (start us, length us, event | category | flops | bytes accessed | tf_op | source)
XLA Modules:
  0.0 132.7 jit_solution(2100943016743306456)
XLA Ops:
  0.6 7.3 %shard_map.127 = (f32[100,1024]{1,0:T(8,128)}, bf16[1024,1024]{1,0:T(8,128)(2,1)}, f32[1024,1024]{1,0:T(8,128)}) custom-call(bf16[2048,1024]{1,0:T(8,128)(2,1)} %bitcast.33, bf16[1024,1024]{1,0:T(8,128)(2,1)} %w.5, f32[1,1024]{1,0:T(1,128)} %bitcast.44, bf16[100,1024]{1,0:T(8,128)(2,1)} %refs_9_.3, f32[1,100]{1,0:T(1,128)} %bitcast.47), custom_call_target="tpu_custom_call" | custom-call | flops 2357198848 | bytes 10485760 | tf_op jit(solution)/shard_map/pallas_call | solution.py:104
  7.9 2.2 %collective-permute-start = (f32[100,1024]{1,0:T(8,128)}, f32[100,1024]{1,0:T(8,128)S(1)}, u32[]{:S(2)}, u32[]{:S(2)}) collective-permute-start(f32[100,1024]{1,0:T(8,128)} %get-tuple-element.45.refs_0_), channel_id=1, source_target_pairs={{0,64},{4,68},{8,72},{12,76},{64,0},{68,4},{72,8},{76,12},{16,80},... | collective-permute-start | bytes 1228808 | tf_op jit(solution)/shard_map/ppermute | solution.py:48
  10.1 1.0 collective-permute-start.1
  11.1 7.1 %shard_map.128 = (f32[100,1024]{1,0:T(8,128)}, bf16[1024,1024]{1,0:T(8,128)(2,1)}, f32[1024,1024]{1,0:T(8,128)}) custom-call(bf16[2048,1024]{1,0:T(8,128)(2,1)} %bitcast.34, bf16[1024,1024]{1,0:T(8,128)(2,1)} %w.5, f32[1,1024]{1,0:T(1,128)} %bitcast.45, bf16[100,1024]{1,0:T(8,128)(2,1)} %refs_9_.3, f32[1,100]{1,0:T(1,128)} %bitcast.48), custom_call_target="tpu_custom_call" | custom-call | flops 2357198848 | bytes 10485760 | tf_op jit(solution)/shard_map/pallas_call | solution.py:104
  19.5 0.7 collective-permute-done.2.refs_1_
  20.2 1.0 collective-permute-start.3
  21.2 1.5 %collective-permute-start.4 = (f32[100,1024]{1,0:T(8,128)}, f32[100,1024]{1,0:T(8,128)S(1)}, u32[]{:S(2)}, u32[]{:S(2)}) collective-permute-start(f32[100,1024]{1,0:T(8,128)} %get-tuple-element.46.refs_0_), channel_id=1, source_target_pairs={{0,64},{4,68},{8,72},{12,76},{64,0},{68,4},{72,8},{76,12},{16,80},... | collective-permute-start | bytes 1228808 | tf_op jit(solution)/shard_map/ppermute | solution.py:48
  22.7 0.7 copy.14.refs_6_
  23.4 0.8 copy-done.6
  24.2 5.7 %shard_map.129 = (bf16[1024,1024]{1,0:T(8,128)(2,1)}, f32[128,1024]{1,0:T(8,128)}) custom-call(f32[100,1024]{1,0:T(8,128)} %get-tuple-element.45.refs_0_, f32[100,1024]{1,0:T(8,128)} %copy-done.4, f32[100,1024]{1,0:T(8,128)} %copy-done.3, f32[100,1024]{1,0:T(8,128)} %copy-done.6, f32[100,2048]{1,0:T(8,128)} %refs_4_.3, f32[1,2048]{1,0:T(1,128)} %bitcast.41, ...), custom_call_target="tpu_custom_call" | custom-call | flops 1 | bytes 1 | tf_op jit(solution)/shard_map/pallas_call | solution.py:208
  29.9 2.9 %collective-permute-done.4.refs_2_ = f32[100,1024]{1,0:T(8,128)S(1)} collective-permute-done((f32[100,1024]{1,0:T(8,128)}, f32[100,1024]{1,0:T(8,128)S(1)}, u32[]{:S(2)}, u32[]{:S(2)}) %collective-permute-start.4) | collective-permute-done | bytes 409632 | tf_op jit(solution)/shard_map/ppermute | solution.py:48
  32.8 0.9 collective-permute-start.5
  33.7 1.4 %collective-permute-done.5.refs_3_ = f32[100,1024]{1,0:T(8,128)S(1)} collective-permute-done((f32[100,1024]{1,0:T(8,128)S(1)}, f32[100,1024]{1,0:T(8,128)S(1)}, u32[]{:S(2)}, u32[]{:S(2)}) %collective-permute-start.5) | collective-permute-done | bytes 409632 | tf_op jit(solution)/shard_map/ppermute | solution.py:48
  35.1 0.8 copy-done.7
  35.9 11.3 %shard_map.130 = (bf16[1024,1024]{1,0:T(8,128)(2,1)}, f32[128,1024]{1,0:T(8,128)}, f32[4,288,512]{2,1,0:T(8,128)}) custom-call(s32[4]{0:T(128)} %pad_add_fusion.where, f32[100,1024]{1,0:T(8,128)} %get-tuple-element.46.refs_0_, f32[100,1024]{1,0:T(8,128)} %copy-done.2, f32[100,1024]{1,0:T(8,128)} %copy-done.5, f32[100,1024]{1,0:T(8,128)} %copy-done.7, ...), custom_call_target="tpu_custom_call" | custom-call | flops 2147483648 | bytes 16728064 | tf_op jit(solution)/shard_map/pallas_call | solution.py:242
  47.6 6.7 %shard_map.131 = f32[4,288,512]{2,1,0:T(8,128)} custom-call(s32[4]{0:T(128)} %pad_add_fusion.where, bf16[2048,1024]{1,0:T(8,128)(2,1)} %bitcast.37, bf16[2048,1024]{1,0:T(8,128)(2,1)} %bitcast.38, bf16[1024,1024]{1,0:T(8,128)(2,1)} %get-tuple-element.73.refs_13_.dpre0, bf16[1024,1024]{1,0:T(8,128)(2,1)} %get-tuple-element.74.dpre1, ...), custom_call_target="tpu_custom_call" | custom-call | flops 2147483648 | bytes 8388608 | tf_op jit(solution)/shard_map/pallas_call | solution.py:282
  54.3 1.3 fusion
  55.6 1.2 add_bitcast_fusion.2
  56.9 2.7 %collective-permute-start.9 = (f32[288,512]{1,0:T(8,128)S(1)}, f32[288,512]{1,0:T(8,128)S(1)}, u32[]{:S(2)}, u32[]{:S(2)}) collective-permute-start(f32[288,512]{1,0:T(8,128)S(1)} %add_bitcast_fusion.1), channel_id=1, source_target_pairs={{0,12},{4,0},{8,4},{12,8},{64,76},{68,64},{72,68},{76,72},{16,28},... | collective-permute-start | bytes 1769480 | tf_op jit(solution)/shard_map/ppermute | solution.py:48
  59.6 1.7 %collective-permute-start.7 = (f32[288,512]{1,0:T(8,128)S(1)}, f32[288,512]{1,0:T(8,128)S(1)}, u32[]{:S(2)}, u32[]{:S(2)}) collective-permute-start(f32[288,512]{1,0:T(8,128)S(1)} %fusion), channel_id=1, source_target_pairs={{0,8},{4,12},{8,0},{12,4},{64,72},{68,76},{72,64},{76,68},{16,24},... | collective-permute-start | bytes 1769480 | tf_op jit(solution)/shard_map/ppermute | solution.py:48
  61.4 8.8 %shard_map.132 = bf16[1,2048,1024]{2,1,0:T(8,128)(2,1)} custom-call(bf16[1024,1024]{1,0:T(8,128)(2,1)} %get-tuple-element.73.refs_13_.dpre0, bf16[1024,1024]{1,0:T(8,128)(2,1)} %get-tuple-element.74.dpre1, bf16[1024,1024]{1,0:T(8,128)(2,1)} %w.5), custom_call_target="tpu_custom_call" | custom-call | flops 4294967296 | bytes 10485760 | tf_op jit(solution)/shard_map/pallas_call | solution.py:316
  70.2 2.5 %collective-permute-done.9 = f32[288,512]{1,0:T(8,128)S(1)} collective-permute-done((f32[288,512]{1,0:T(8,128)S(1)}, f32[288,512]{1,0:T(8,128)S(1)}, u32[]{:S(2)}, u32[]{:S(2)}) %collective-permute-start.9) | collective-permute-done | bytes 589856 | tf_op jit(solution)/shard_map/ppermute | solution.py:48
  72.7 3.4 %collective-permute-done.8 = f32[288,512]{1,0:T(8,128)S(1)} collective-permute-done((f32[288,512]{1,0:T(8,128)S(1)}, f32[288,512]{1,0:T(8,128)S(1)}, u32[]{:S(2)}, u32[]{:S(2)}) %collective-permute-start.8) | collective-permute-done | bytes 589856 | tf_op jit(solution)/shard_map/ppermute | solution.py:48
  76.4 1.4 %collective-permute-start.10 = (f32[72,512]{1,0:T(8,128)S(1)}, f32[72,512]{1,0:T(8,128)S(1)}, u32[]{:S(2)}, u32[]{:S(2)}) collective-permute-start(f32[72,512]{1,0:T(8,128)S(1)} %get-tuple-element.84), channel_id=1, source_target_pairs={{0,1},{4,5},{8,9},{12,13},{64,65},{68,69},{72,73},{76,77},{16,17},... | collective-permute-start | bytes 442376 | tf_op jit(solution)/shard_map/ppermute | solution.py:48
  77.9 2.2 %collective-permute-start.11 = (f32[72,512]{1,0:T(8,128)S(1)}, f32[72,512]{1,0:T(8,128)S(1)}, u32[]{:S(2)}, u32[]{:S(2)}) collective-permute-start(f32[72,512]{1,0:T(8,128)S(1)} %get-tuple-element.86), channel_id=1, source_target_pairs={{0,3},{4,7},{8,11},{12,15},{64,67},{68,71},{72,75},{76,79},{16,19}... | collective-permute-start | bytes 442376 | tf_op jit(solution)/shard_map/ppermute | solution.py:48
  80.1 1.2 collective-permute-start.12
  81.3 1.2 collective-permute-done.10
  82.5 3.0 %collective-permute-done.12 = f32[72,512]{1,0:T(8,128)S(1)} collective-permute-done((f32[72,512]{1,0:T(8,128)S(1)}, f32[72,512]{1,0:T(8,128)S(1)}, u32[]{:S(2)}, u32[]{:S(2)}) %collective-permute-start.12) | collective-permute-done | bytes 147488 | tf_op jit(solution)/shard_map/ppermute | solution.py:48
  85.6 1.4 %collective-permute-start.13 = (f32[72,512]{1,0:T(8,128)S(1)}, f32[72,512]{1,0:T(8,128)S(1)}, u32[]{:S(2)}, u32[]{:S(2)}) collective-permute-start(f32[72,512]{1,0:T(8,128)S(1)} %fusion.2), channel_id=1, source_target_pairs={{0,64},{4,68},{8,72},{12,76},{64,16},{68,20},{72,24},{76,28},{16,8... | collective-permute-start | bytes 442376 | tf_op jit(solution)/shard_map/ppermute | solution.py:48
  87.0 1.5 %collective-permute-start.14 = (f32[72,512]{1,0:T(8,128)S(1)}, f32[72,512]{1,0:T(8,128)S(1)}, u32[]{:S(2)}, u32[]{:S(2)}) collective-permute-start(f32[72,512]{1,0:T(8,128)S(1)} %fusion.2), channel_id=1, source_target_pairs={{0,80},{4,84},{8,88},{12,92},{64,0},{68,4},{72,8},{76,12},{16,64},... | collective-permute-start | bytes 442376 | tf_op jit(solution)/shard_map/ppermute | solution.py:48
  88.5 1.6 %collective-permute-start.15 = (f32[72,512]{1,0:T(8,128)S(1)}, f32[72,512]{1,0:T(8,128)S(1)}, u32[]{:S(2)}, u32[]{:S(2)}) collective-permute-start(f32[72,512]{1,0:T(8,128)S(1)} %fusion.2), channel_id=1, source_target_pairs={{0,16},{4,20},{8,24},{12,28},{64,80},{68,84},{72,88},{76,92},{16,0... | collective-permute-start | bytes 442376 | tf_op jit(solution)/shard_map/ppermute | solution.py:48
  90.0 0.9 collective-permute-done.13
  91.0 3.1 %collective-permute-done.15 = f32[72,512]{1,0:T(8,128)S(1)} collective-permute-done((f32[72,512]{1,0:T(8,128)S(1)}, f32[72,512]{1,0:T(8,128)S(1)}, u32[]{:S(2)}, u32[]{:S(2)}) %collective-permute-start.15) | collective-permute-done | bytes 147488 | tf_op jit(solution)/shard_map/ppermute | solution.py:48
  94.1 3.2 %collective-permute-start.16 = (f32[72,512]{1,0:T(8,128)S(1)}, f32[72,512]{1,0:T(8,128)S(1)}, u32[]{:S(2)}, u32[]{:S(2)}) collective-permute-start(f32[72,512]{1,0:T(8,128)S(1)} %add_add_fusion.1), channel_id=1, source_target_pairs={{0,3},{4,7},{8,11},{12,15},{64,67},{68,71},{72,75},{76,79},{16,19}... | collective-permute-start | bytes 442376 | tf_op jit(solution)/shard_map/ppermute | solution.py:48
  97.3 1.6 %collective-permute-start.17 = (f32[72,512]{1,0:T(8,128)S(1)}, f32[72,512]{1,0:T(8,128)S(1)}, u32[]{:S(2)}, u32[]{:S(2)}) collective-permute-start(f32[72,512]{1,0:T(8,128)S(1)} %add_add_fusion.1), channel_id=1, source_target_pairs={{0,2},{4,6},{8,10},{12,14},{64,66},{68,70},{72,74},{76,78},{16,18}... | collective-permute-start | bytes 442376 | tf_op jit(solution)/shard_map/ppermute | solution.py:48
  98.9 2.1 %collective-permute-done.16 = f32[72,512]{1,0:T(8,128)S(1)} collective-permute-done((f32[72,512]{1,0:T(8,128)S(1)}, f32[72,512]{1,0:T(8,128)S(1)}, u32[]{:S(2)}, u32[]{:S(2)}) %collective-permute-start.16) | collective-permute-done | bytes 147488 | tf_op jit(solution)/shard_map/ppermute | solution.py:48
  101.0 1.8 %collective-permute-done.17 = f32[72,512]{1,0:T(8,128)S(1)} collective-permute-done((f32[72,512]{1,0:T(8,128)S(1)}, f32[72,512]{1,0:T(8,128)S(1)}, u32[]{:S(2)}, u32[]{:S(2)}) %collective-permute-start.17) | collective-permute-done | bytes 147488 | tf_op jit(solution)/shard_map/ppermute | solution.py:48
  102.9 1.5 %collective-permute-done.18 = f32[72,512]{1,0:T(8,128)S(1)} collective-permute-done((f32[72,512]{1,0:T(8,128)S(1)}, f32[72,512]{1,0:T(8,128)S(1)}, u32[]{:S(2)}, u32[]{:S(2)}) %collective-permute-start.18) | collective-permute-done | bytes 147488 | tf_op jit(solution)/shard_map/ppermute | solution.py:48
  104.6 0.9 collective-permute-start.20
  105.5 1.8 %collective-permute-start.21 = (f32[288,512]{1,0:T(8,128)S(1)}, f32[288,512]{1,0:T(8,128)S(1)}, u32[]{:S(2)}, u32[]{:S(2)}) collective-permute-start(f32[288,512]{1,0:T(8,128)S(1)} %constant_dynamic-slice_fusion.refs_0_), channel_id=1, source_target_pairs={{0,12},{4,0},{8,4},{12,8},{64,76},{68,64},{72,68},{76,72},{16,28},... | collective-permute-start | bytes 1769480 | tf_op jit(solution)/shard_map/ppermute | solution.py:48
  107.3 5.0 %collective-permute-start.22 = (f32[288,512]{1,0:T(8,128)S(1)}, f32[288,512]{1,0:T(8,128)S(1)}, u32[]{:S(2)}, u32[]{:S(2)}) collective-permute-start(f32[288,512]{1,0:T(8,128)S(1)} %constant_dynamic-slice_fusion.refs_0_), channel_id=1, source_target_pairs={{0,32},{4,36},{8,40},{12,44},{64,96},{68,100},{72,104},{76,108},{1... | collective-permute-start | bytes 1769480 | tf_op jit(solution)/shard_map/ppermute | solution.py:48
  112.3 8.9 %collective-permute-done.19.refs_1_ = f32[288,512]{1,0:T(8,128)S(1)} collective-permute-done((f32[288,512]{1,0:T(8,128)S(1)}, f32[288,512]{1,0:T(8,128)S(1)}, u32[]{:S(2)}, u32[]{:S(2)}) %collective-permute-start.19) | collective-permute-done | bytes 589856 | tf_op jit(solution)/shard_map/ppermute | solution.py:48
  121.2 5.3 %collective-permute-start.23 = (f32[288,512]{1,0:T(8,128)S(1)}, f32[288,512]{1,0:T(8,128)S(1)}, u32[]{:S(2)}, u32[]{:S(2)}) collective-permute-start(f32[288,512]{1,0:T(8,128)S(1)} %collective-permute-done.19.refs_1_), channel_id=1, source_target_pairs={{0,32},{4,36},{8,40},{12,44},{64,96},{68,100},{72,104},{76,108},{1... | collective-permute-start | bytes 1769480 | tf_op jit(solution)/shard_map/ppermute | solution.py:48
  126.5 0.9 collective-permute-start.25
  127.4 0.7 collective-permute-done.23.refs_5_
  128.1 0.8 collective-permute-done.24.refs_6_
  128.9 0.8 collective-permute-done.25.refs_7_
  129.8 2.9 %shard_map.133 = (f32[1024,1024]{1,0:T(8,128)}, f32[100,1024]{1,0:T(8,128)}, f32[1,1024]{1,0:T(1,128)}, f32[1,100]{1,0:T(1,128)}, f32[1,1]{1,0:T(1,128)}) custom-call(s32[4]{0:T(128)S(1)} %copy-done, f32[288,512]{1,0:T(8,128)S(1)} %constant_dynamic-slice_fusion.refs_0_, f32[288,512]{1,0:T(8,128)S(1)} %collective-permute-done.19.refs_1_, ...), custom_call_target="tpu_custom_call" | custom-call | bytes 8388608 | tf_op jit(solution)/shard_map/pallas_call | solution.py:350
  (47 shorter events, 2.5 us)
Async XLA Ops:
  7.9 14.8 %copy-start.8 = (f32[100]{0:T(128)S(1)}, f32[100]{0:T(128)}, u32[]{:S(2)}) copy-start(f32[100]{0:T(128)} %param.11) | copy-start | bytes 1204
  7.9 11.5 %collective-permute-start = (f32[100,1024]{1,0:T(8,128)}, f32[100,1024]{1,0:T(8,128)S(1)}, u32[]{:S(2)}, u32[]{:S(2)}) collective-permute-start(f32[100,1024]{1,0:T(8,128)} %get-tuple-element.45.refs_0_), channel_id=1, source_target_pairs={{0,64},{4,68},{8,72},{12,76},{64,0},{68,4},{72,8},{76,12},{16,80},... | collective-permute-start | bytes 1228808 | tf_op jit(solution)/shard_map/ppermute | solution.py:48
  10.1 9.3 %collective-permute-start.1 = (f32[100,1024]{1,0:T(8,128)}, f32[100,1024]{1,0:T(8,128)S(1)}, u32[]{:S(2)}, u32[]{:S(2)}) collective-permute-start(f32[100,1024]{1,0:T(8,128)} %get-tuple-element.45.refs_0_), channel_id=1, source_target_pairs={{0,32},{4,36},{8,40},{12,44},{64,96},{68,100},{72,104},{76,108},{1... | collective-permute-start | bytes 1228808 | tf_op jit(solution)/shard_map/ppermute | solution.py:48
  18.2 2.0 %collective-permute-start.2 = (f32[100,1024]{1,0:T(8,128)}, f32[100,1024]{1,0:T(8,128)S(1)}, u32[]{:S(2)}, u32[]{:S(2)}) collective-permute-start(f32[100,1024]{1,0:T(8,128)} %get-tuple-element.46.refs_0_), channel_id=1, source_target_pairs={{0,32},{4,36},{8,40},{12,44},{64,96},{68,100},{72,104},{76,108},{1... | collective-permute-start | bytes 1228808 | tf_op jit(solution)/shard_map/ppermute | solution.py:48
  19.5 4.0 %copy-start.3 = (f32[100,1024]{1,0:T(8,128)}, f32[100,1024]{1,0:T(8,128)S(1)}, u32[]{:S(2)}) copy-start(f32[100,1024]{1,0:T(8,128)S(1)} %collective-permute-done.refs_2_) | copy-start | bytes 1228804
  19.5 4.0 %copy-start.4 = (f32[100,1024]{1,0:T(8,128)}, f32[100,1024]{1,0:T(8,128)S(1)}, u32[]{:S(2)}) copy-start(f32[100,1024]{1,0:T(8,128)S(1)} %collective-permute-done.1.refs_1_) | copy-start | bytes 1228804
  20.2 9.6 %copy-start.2 = (f32[100,1024]{1,0:T(8,128)}, f32[100,1024]{1,0:T(8,128)S(1)}, u32[]{:S(2)}) copy-start(f32[100,1024]{1,0:T(8,128)S(1)} %collective-permute-done.2.refs_1_) | copy-start | bytes 1228804
  20.2 3.2 %collective-permute-start.3 = (f32[100,1024]{1,0:T(8,128)S(1)}, f32[100,1024]{1,0:T(8,128)S(1)}, u32[]{:S(2)}, u32[]{:S(2)}) collective-permute-start(f32[100,1024]{1,0:T(8,128)S(1)} %collective-permute-done.refs_2_), channel_id=1, source_target_pairs={{0,32},{4,36},{8,40},{12,44},{64,96},{68,100},{72,104},{76,108},{1... | collective-permute-start | bytes 1228808 | tf_op jit(solution)/shard_map/ppermute | solution.py:48
  21.2 11.6 %collective-permute-start.4 = (f32[100,1024]{1,0:T(8,128)}, f32[100,1024]{1,0:T(8,128)S(1)}, u32[]{:S(2)}, u32[]{:S(2)}) collective-permute-start(f32[100,1024]{1,0:T(8,128)} %get-tuple-element.46.refs_0_), channel_id=1, source_target_pairs={{0,64},{4,68},{8,72},{12,76},{64,0},{68,4},{72,8},{76,12},{16,80},... | collective-permute-start | bytes 1228808 | tf_op jit(solution)/shard_map/ppermute | solution.py:48
  23.4 0.8 copy-start.6
  32.8 2.3 %copy-start.5 = (f32[100,1024]{1,0:T(8,128)}, f32[100,1024]{1,0:T(8,128)S(1)}, u32[]{:S(2)}) copy-start(f32[100,1024]{1,0:T(8,128)S(1)} %collective-permute-done.4.refs_2_) | copy-start | bytes 1228804
  32.8 2.3 %collective-permute-start.5 = (f32[100,1024]{1,0:T(8,128)S(1)}, f32[100,1024]{1,0:T(8,128)S(1)}, u32[]{:S(2)}, u32[]{:S(2)}) collective-permute-start(f32[100,1024]{1,0:T(8,128)S(1)} %collective-permute-done.4.refs_2_), channel_id=1, source_target_pairs={{0,32},{4,36},{8,40},{12,44},{64,96},{68,100},{72,104},{76,108},{1... | collective-permute-start | bytes 1228808 | tf_op jit(solution)/shard_map/ppermute | solution.py:48
  35.1 0.8 copy-start.7
  47.1 7.1 %collective-permute-start.6 = (f32[4,288,512]{2,1,0:T(8,128)}, f32[4,288,512]{2,1,0:T(8,128)S(1)}, u32[]{:S(2)}, u32[]{:S(2)}) collective-permute-start(f32[4,288,512]{2,1,0:T(8,128)} %get-tuple-element.61), channel_id=1, source_target_pairs={{0,32},{4,36},{8,40},{12,44},{64,96},{68,100},{72,104},{76,108},{1... | collective-permute-start | bytes 7077896 | tf_op jit(solution)/shard_map/ppermute | solution.py:48
  54.3 2.5 %copy-start.1 = (f32[4,288,512]{2,1,0:T(8,128)S(1)}, f32[4,288,512]{2,1,0:T(8,128)}, u32[]{:S(2)}) copy-start(f32[4,288,512]{2,1,0:T(8,128)} %shard_map.131) | copy-start | bytes 7077892
  56.9 15.9 %collective-permute-start.9 = (f32[288,512]{1,0:T(8,128)S(1)}, f32[288,512]{1,0:T(8,128)S(1)}, u32[]{:S(2)}, u32[]{:S(2)}) collective-permute-start(f32[288,512]{1,0:T(8,128)S(1)} %add_bitcast_fusion.1), channel_id=1, source_target_pairs={{0,12},{4,0},{8,4},{12,8},{64,76},{68,64},{72,68},{76,72},{16,28},... | collective-permute-start | bytes 1769480 | tf_op jit(solution)/shard_map/ppermute | solution.py:48
  59.6 16.6 %collective-permute-start.8 = (f32[288,512]{1,0:T(8,128)S(1)}, f32[288,512]{1,0:T(8,128)S(1)}, u32[]{:S(2)}, u32[]{:S(2)}) collective-permute-start(f32[288,512]{1,0:T(8,128)S(1)} %add_bitcast_fusion.2), channel_id=1, source_target_pairs={{0,4},{4,8},{8,12},{12,0},{64,68},{68,72},{72,76},{76,64},{16,20},... | collective-permute-start | bytes 1769480 | tf_op jit(solution)/shard_map/ppermute | solution.py:48
  59.6 16.6 %collective-permute-start.7 = (f32[288,512]{1,0:T(8,128)S(1)}, f32[288,512]{1,0:T(8,128)S(1)}, u32[]{:S(2)}, u32[]{:S(2)}) collective-permute-start(f32[288,512]{1,0:T(8,128)S(1)} %fusion), channel_id=1, source_target_pairs={{0,8},{4,12},{8,0},{12,4},{64,72},{68,76},{72,64},{76,68},{16,24},... | collective-permute-start | bytes 1769480 | tf_op jit(solution)/shard_map/ppermute | solution.py:48
  76.4 6.1 %collective-permute-start.10 = (f32[72,512]{1,0:T(8,128)S(1)}, f32[72,512]{1,0:T(8,128)S(1)}, u32[]{:S(2)}, u32[]{:S(2)}) collective-permute-start(f32[72,512]{1,0:T(8,128)S(1)} %get-tuple-element.84), channel_id=1, source_target_pairs={{0,1},{4,5},{8,9},{12,13},{64,65},{68,69},{72,73},{76,77},{16,17},... | collective-permute-start | bytes 442376 | tf_op jit(solution)/shard_map/ppermute | solution.py:48
  77.9 4.7 %collective-permute-start.11 = (f32[72,512]{1,0:T(8,128)S(1)}, f32[72,512]{1,0:T(8,128)S(1)}, u32[]{:S(2)}, u32[]{:S(2)}) collective-permute-start(f32[72,512]{1,0:T(8,128)S(1)} %get-tuple-element.86), channel_id=1, source_target_pairs={{0,3},{4,7},{8,11},{12,15},{64,67},{68,71},{72,75},{76,79},{16,19}... | collective-permute-start | bytes 442376 | tf_op jit(solution)/shard_map/ppermute | solution.py:48
  80.1 5.5 %collective-permute-start.12 = (f32[72,512]{1,0:T(8,128)S(1)}, f32[72,512]{1,0:T(8,128)S(1)}, u32[]{:S(2)}, u32[]{:S(2)}) collective-permute-start(f32[72,512]{1,0:T(8,128)S(1)} %get-tuple-element.85), channel_id=1, source_target_pairs={{0,2},{4,6},{8,10},{12,14},{64,66},{68,70},{72,74},{76,78},{16,18}... | collective-permute-start | bytes 442376 | tf_op jit(solution)/shard_map/ppermute | solution.py:48
  81.3 48.5 %copy-start = (s32[4]{0:T(128)S(1)}, s32[4]{0:T(128)}, u32[]{:S(2)}) copy-start(s32[4]{0:T(128)} %pad_add_fusion.where) | copy-start | bytes 52
  85.6 5.3 %collective-permute-start.13 = (f32[72,512]{1,0:T(8,128)S(1)}, f32[72,512]{1,0:T(8,128)S(1)}, u32[]{:S(2)}, u32[]{:S(2)}) collective-permute-start(f32[72,512]{1,0:T(8,128)S(1)} %fusion.2), channel_id=1, source_target_pairs={{0,64},{4,68},{8,72},{12,76},{64,16},{68,20},{72,24},{76,28},{16,8... | collective-permute-start | bytes 442376 | tf_op jit(solution)/shard_map/ppermute | solution.py:48
  87.0 4.0 %collective-permute-start.14 = (f32[72,512]{1,0:T(8,128)S(1)}, f32[72,512]{1,0:T(8,128)S(1)}, u32[]{:S(2)}, u32[]{:S(2)}) collective-permute-start(f32[72,512]{1,0:T(8,128)S(1)} %fusion.2), channel_id=1, source_target_pairs={{0,80},{4,84},{8,88},{12,92},{64,0},{68,4},{72,8},{76,12},{16,64},... | collective-permute-start | bytes 442376 | tf_op jit(solution)/shard_map/ppermute | solution.py:48
  88.5 5.6 %collective-permute-start.15 = (f32[72,512]{1,0:T(8,128)S(1)}, f32[72,512]{1,0:T(8,128)S(1)}, u32[]{:S(2)}, u32[]{:S(2)}) collective-permute-start(f32[72,512]{1,0:T(8,128)S(1)} %fusion.2), channel_id=1, source_target_pairs={{0,16},{4,20},{8,24},{12,28},{64,80},{68,84},{72,88},{76,92},{16,0... | collective-permute-start | bytes 442376 | tf_op jit(solution)/shard_map/ppermute | solution.py:48
  94.1 6.9 %collective-permute-start.16 = (f32[72,512]{1,0:T(8,128)S(1)}, f32[72,512]{1,0:T(8,128)S(1)}, u32[]{:S(2)}, u32[]{:S(2)}) collective-permute-start(f32[72,512]{1,0:T(8,128)S(1)} %add_add_fusion.1), channel_id=1, source_target_pairs={{0,3},{4,7},{8,11},{12,15},{64,67},{68,71},{72,75},{76,79},{16,19}... | collective-permute-start | bytes 442376 | tf_op jit(solution)/shard_map/ppermute | solution.py:48
  97.3 5.5 %collective-permute-start.17 = (f32[72,512]{1,0:T(8,128)S(1)}, f32[72,512]{1,0:T(8,128)S(1)}, u32[]{:S(2)}, u32[]{:S(2)}) collective-permute-start(f32[72,512]{1,0:T(8,128)S(1)} %add_add_fusion.1), channel_id=1, source_target_pairs={{0,2},{4,6},{8,10},{12,14},{64,66},{68,70},{72,74},{76,78},{16,18}... | collective-permute-start | bytes 442376 | tf_op jit(solution)/shard_map/ppermute | solution.py:48
  98.9 5.5 %collective-permute-start.18 = (f32[72,512]{1,0:T(8,128)S(1)}, f32[72,512]{1,0:T(8,128)S(1)}, u32[]{:S(2)}, u32[]{:S(2)}) collective-permute-start(f32[72,512]{1,0:T(8,128)S(1)} %add_add_fusion.1), channel_id=1, source_target_pairs={{0,1},{4,5},{8,9},{12,13},{64,65},{68,69},{72,73},{76,77},{16,17},... | collective-permute-start | bytes 442376 | tf_op jit(solution)/shard_map/ppermute | solution.py:48
  104.5 16.6 %collective-permute-start.19 = (f32[288,512]{1,0:T(8,128)S(1)}, f32[288,512]{1,0:T(8,128)S(1)}, u32[]{:S(2)}, u32[]{:S(2)}) collective-permute-start(f32[288,512]{1,0:T(8,128)S(1)} %constant_dynamic-slice_fusion.refs_0_), channel_id=1, source_target_pairs={{0,4},{4,8},{8,12},{12,0},{64,68},{68,72},{72,76},{76,64},{16,20},... | collective-permute-start | bytes 1769480 | tf_op jit(solution)/shard_map/ppermute | solution.py:48
  104.6 21.8 %collective-permute-start.20 = (f32[288,512]{1,0:T(8,128)S(1)}, f32[288,512]{1,0:T(8,128)S(1)}, u32[]{:S(2)}, u32[]{:S(2)}) collective-permute-start(f32[288,512]{1,0:T(8,128)S(1)} %constant_dynamic-slice_fusion.refs_0_), channel_id=1, source_target_pairs={{0,8},{4,12},{8,0},{12,4},{64,72},{68,76},{72,64},{76,68},{16,24},... | collective-permute-start | bytes 1769480 | tf_op jit(solution)/shard_map/ppermute | solution.py:48
  105.5 20.9 %collective-permute-start.21 = (f32[288,512]{1,0:T(8,128)S(1)}, f32[288,512]{1,0:T(8,128)S(1)}, u32[]{:S(2)}, u32[]{:S(2)}) collective-permute-start(f32[288,512]{1,0:T(8,128)S(1)} %constant_dynamic-slice_fusion.refs_0_), channel_id=1, source_target_pairs={{0,12},{4,0},{8,4},{12,8},{64,76},{68,64},{72,68},{76,72},{16,28},... | collective-permute-start | bytes 1769480 | tf_op jit(solution)/shard_map/ppermute | solution.py:48
  107.3 20.1 %collective-permute-start.22 = (f32[288,512]{1,0:T(8,128)S(1)}, f32[288,512]{1,0:T(8,128)S(1)}, u32[]{:S(2)}, u32[]{:S(2)}) collective-permute-start(f32[288,512]{1,0:T(8,128)S(1)} %constant_dynamic-slice_fusion.refs_0_), channel_id=1, source_target_pairs={{0,32},{4,36},{8,40},{12,44},{64,96},{68,100},{72,104},{76,108},{1... | collective-permute-start | bytes 1769480 | tf_op jit(solution)/shard_map/ppermute | solution.py:48
  121.2 6.9 %collective-permute-start.23 = (f32[288,512]{1,0:T(8,128)S(1)}, f32[288,512]{1,0:T(8,128)S(1)}, u32[]{:S(2)}, u32[]{:S(2)}) collective-permute-start(f32[288,512]{1,0:T(8,128)S(1)} %collective-permute-done.19.refs_1_), channel_id=1, source_target_pairs={{0,32},{4,36},{8,40},{12,44},{64,96},{68,100},{72,104},{76,108},{1... | collective-permute-start | bytes 1769480 | tf_op jit(solution)/shard_map/ppermute | solution.py:48
  126.5 2.5 %collective-permute-start.24 = (f32[288,512]{1,0:T(8,128)S(1)}, f32[288,512]{1,0:T(8,128)S(1)}, u32[]{:S(2)}, u32[]{:S(2)}) collective-permute-start(f32[288,512]{1,0:T(8,128)S(1)} %collective-permute-done.20.refs_2_), channel_id=1, source_target_pairs={{0,32},{4,36},{8,40},{12,44},{64,96},{68,100},{72,104},{76,108},{1... | collective-permute-start | bytes 1769480 | tf_op jit(solution)/shard_map/ppermute | solution.py:48
  126.5 3.3 %collective-permute-start.25 = (f32[288,512]{1,0:T(8,128)S(1)}, f32[288,512]{1,0:T(8,128)S(1)}, u32[]{:S(2)}, u32[]{:S(2)}) collective-permute-start(f32[288,512]{1,0:T(8,128)S(1)} %collective-permute-done.21.refs_3_), channel_id=1, source_target_pairs={{0,32},{4,36},{8,40},{12,44},{64,96},{68,100},{72,104},{76,108},{1... | collective-permute-start | bytes 1769480 | tf_op jit(solution)/shard_map/ppermute | solution.py:48

commit v5 on v4

--- a/solution.py
+++ b/solution.py
@@ -162,41 +162,61 @@
     dpre[...] = cot_tile(*numbers, *refs[:10], rest)
 
 
-def weight_blocks(scale, which, where, step, lats, dpres, rest, out):
-    rows, half = lats[0].shape[1], out.shape[2]
-    for j, lat in enumerate(lats):
-        total, start = 0.0, 0
-        for d in dpres:
-            n = d.shape[0]
-            total += lax.dot_general(
-                lat[start : start + n, :], d, (((0,), (0,)), ((), ())), preferred_element_type=F32
-            )
-            start += n
-        block = lax.rem(where[2 + which] + 2 * step + j, 4)
-        out[j, 0:rows, :] = total * scale
-        cols = pl.ds(pl.multiple_of(where[which] * half, half), half)
-        out[j, rows : rows + 32, :] = rest[pl.ds(pl.multiple_of(block * 32, 32), 32), cols]
+def block_copies(which, where, lat, held, sems, dpre, to):
+    rows, half = held.shape[2], to.shape[1]
+    cols = pl.ds(pl.multiple_of(where[which] * half, half), half)
+
+    def columns(k):
+        block = lax.rem(where[2 + which] + k, 4)
+        at = pl.ds(pl.multiple_of(block * rows, rows), rows)
+        return pltpu.make_async_copy(lat.at[:, at], held.at[k], sems.at[k])
+
+    return columns, pltpu.make_async_copy(dpre.at[:, cols], to, sems.at[4])
+
+
+def weight_block(scale, which, where, k, lat, dpres, rest, out, j=0):
+    rows, half = lat.shape[1], out.shape[2]
+    total, start = 0.0, 0
+    for d in dpres:
+        n = d.shape[0]
+        total += lax.dot_general(lat[start : start + n, :], d, (((0,), (0,)), ((), ())), preferred_element_type=F32)
+        start += n
+    block = lax.rem(where[2 + which] + k, 4)
+    out[j, 0:rows, :] = total * scale
+    cols = pl.ds(pl.multiple_of(where[which] * half, half), half)
+    out[j, rows : rows + 32, :] = rest[pl.ds(pl.multiple_of(block * 32, 32), 32), cols]
 
 
 def cot_weight_kernel(numbers, steps, which, where, *refs):
-    ins, (rest_in, lat0, lat1, dpre0), (dpre, rest, out, held) = refs[:10], refs[10:14], refs[14:]
+    ins, (rest_in, lat, dpre0), (dpre, rest, out, mine, lat_held, half0, sems) = refs[:10], refs[10:13], refs[13:]
     g = pl.program_id(0)
     tile, half = dpre.shape[0], out.shape[2]
+    columns, first_half = block_copies(which, where, lat, lat_held, sems, dpre0, half0)
 
     @pl.when(g == 0)
     def _():
+        first_half.start()
+        for k in range(4):
+            columns(k).start()
         rest[...] = rest_in[...]
 
     @pl.when(g < steps)
     def _():
         d = cot_tile(*numbers, *ins, rest)
         dpre[...] = d
-        held[pl.ds(pl.multiple_of(g * tile, tile), tile), :] = d
+        mine[pl.ds(pl.multiple_of(g * tile, tile), tile), :] = d
+
+    @pl.when(g == steps)
+    def _():
+        first_half.wait()
 
     @pl.when(g >= steps)
     def _():
+        columns(g - steps).wait()
         cols = pl.ds(pl.multiple_of(where[which] * half, half), half)
-        weight_blocks(numbers[1], which, where, g - steps, (lat0, lat1), (dpre0[...], held[:, cols]), rest, out)
+        weight_block(
+            numbers[1], which, where, g - steps, lat_held.at[g - steps], (half0[...], mine[:, cols]), rest, out
+        )
 
 
 def cotangent(numbers, part, own, others, target, area, var, sp, hid, w_output, tile=512):
@@ -238,12 +258,12 @@
     whole = lambda shape: pl.BlockSpec(shape, lambda g, s: (0, 0))
     local = pl.BlockSpec((n_vars, tile), lambda g, s: (0, at(g)))
     rows = pl.BlockSpec((tile, width), lambda g, s: (at(g), 0))
-    lat = lambda j: pl.BlockSpec((points, block), lambda g, s: (0, lax.rem(s[2 + which] + 2 * step(g) + j, 4)))
+    hbm = pl.BlockSpec(memory_space=pl.ANY)
     return pl.pallas_call(
         functools.partial(cot_weight_kernel, numbers, steps, which),
         grid_spec=pltpu.PrefetchScalarGridSpec(
             num_scalar_prefetch=1,
-            grid=(steps + 2,),
+            grid=(steps + 4,),
             in_specs=[local] * 4
             + [
                 pl.BlockSpec((n_vars, tile), lambda g, s: (0, part * steps + at(g))),
@@ -253,12 +273,16 @@
                 rows,
                 whole(w_output.shape),
                 whole((128, width)),
-                lat(0),
-                lat(1),
-                pl.BlockSpec((n, half), lambda g, s: (0, s[which])),
+                hbm,
+                hbm,
             ],
-            out_specs=[rows, whole((128, width)), pl.BlockSpec((2, block + 32, half), lambda g, s: (step(g), 0, 0))],
-            scratch_shapes=[pltpu.VMEM((n, width), BF16)],
+            out_specs=[rows, whole((128, width)), pl.BlockSpec((1, block + 32, half), lambda g, s: (step(g), 0, 0))],
+            scratch_shapes=[
+                pltpu.VMEM((n, width), BF16),
+                pltpu.VMEM((4, points, block), BF16),
+                pltpu.VMEM((points - n, half), BF16),
+                pltpu.SemaphoreType.DMA((5,)),
+            ],
         ),
         out_shape=[
             jax.ShapeDtypeStruct((n, width), BF16),
@@ -267,11 +291,12 @@
         ],
         compiler_params=params(),
         cost_estimate=cost(2 * points * half * depth, points * 2 * depth + n * (n_vars * 20 + 8 * width) + 4 * depth * half),
-    )(where, own, *others, target, area, var, sp, hid, w_output, rest, latent, latent, dpre0)
+    )(where, own, *others, target, area, var, sp, hid, w_output, rest, latent, dpre0)
 
 
 def weight_kernel(scale, which, where, lat0, lat1, dpre0, dpre1, rest, out):
-    weight_blocks(scale, which, where, pl.program_id(0), (lat0, lat1), (dpre0[...], dpre1[...]), rest, out)
+    for j, lat in enumerate((lat0, lat1)):
+        weight_block(scale, which, where, 2 * pl.program_id(0) + j, lat, (dpre0[...], dpre1[...]), rest, out, j)
 
 
 def weight_grad(which, where, latent, dpre, rest, scale):

time: 133 us -> 132 us (level)
  no operation moved by 1% of the time
where the time goes in v5:
time: 132 us
  Pallas kernels  48.7 us (37%)
  starting transfers between devices  38.7 us (29%)
  waiting for transfers between devices  37.4 us (28%)
  other arithmetic  3.64 us (3%)
  local copies, waits for them, and re-layouts  2.5 us (2%)
    ppermute x26, starting transfers between devices, send(): return lax.ppermute(array, ALL, pairs)  38.7 us
    ppermute x26, waiting for transfers between devices, send(): return lax.ppermute(array, ALL, pairs)  37.4 us
    pallas_call x2, Pallas kernels, forward(): pl.pallas_call(forward_kernel, grid=(steps,), in_specs=[pl.BlockSpec((til...  14.4 us
    pallas_call x1, Pallas kernels, cotangent_weight(): pl.pallas_call(functools.partial(cot_weight_kernel, numbers, steps, which...  10.3 us
    pallas_call x1, Pallas kernels, latent_gradient(): pl.pallas_call(functools.partial(latent_kernel, steps), grid=(2 * steps,)...  8.76 us
    pallas_call x1, Pallas kernels, weight_grad(): pl.pallas_call(functools.partial(weight_kernel, scale, which), grid_spec=...  6.66 us
    pallas_call x1, Pallas kernels, cotangent(): pl.pallas_call(functools.partial(cot_kernel, numbers), grid=(steps,), in_...  5.66 us
    pallas_call x1, Pallas kernels, join(): pl.pallas_call(functools.partial(join_kernel, n_vars), in_specs=[pl.Block...  2.9 us
  transfers between devices with their start and end apart: 26, of which 17 were waited for; matrix products, arithmetic and copies ran while one was open for 1% of the time, Pallas kernels for 21%

profile of v5, /device:TPU:1, one launch (start us, length us, event | category | flops | bytes accessed | tf_op | source)
XLA Modules:
  0.0 131.7 jit_solution(641007822807422589)
XLA Ops:
  0.6 7.3 %shard_map.127 = (f32[100,1024]{1,0:T(8,128)}, bf16[1024,1024]{1,0:T(8,128)(2,1)}, f32[1024,1024]{1,0:T(8,128)}) custom-call(bf16[2048,1024]{1,0:T(8,128)(2,1)} %bitcast.33, bf16[1024,1024]{1,0:T(8,128)(2,1)} %w.5, f32[1,1024]{1,0:T(1,128)} %bitcast.43, bf16[100,1024]{1,0:T(8,128)(2,1)} %refs_9_.3, f32[1,100]{1,0:T(1,128)} %bitcast.46), custom_call_target="tpu_custom_call" | custom-call | flops 2357198848 | bytes 10485760 | tf_op jit(solution)/shard_map/pallas_call | solution.py:104
  7.9 2.2 %collective-permute-start = (f32[100,1024]{1,0:T(8,128)}, f32[100,1024]{1,0:T(8,128)S(1)}, u32[]{:S(2)}, u32[]{:S(2)}) collective-permute-start(f32[100,1024]{1,0:T(8,128)} %get-tuple-element.45.refs_0_), channel_id=1, source_target_pairs={{0,64},{4,68},{8,72},{12,76},{64,0},{68,4},{72,8},{76,12},{16,80},... | collective-permute-start | bytes 1228808 | tf_op jit(solution)/shard_map/ppermute | solution.py:48
  10.1 1.0 collective-permute-start.1
  11.1 7.1 %shard_map.128 = (f32[100,1024]{1,0:T(8,128)}, bf16[1024,1024]{1,0:T(8,128)(2,1)}, f32[1024,1024]{1,0:T(8,128)}) custom-call(bf16[2048,1024]{1,0:T(8,128)(2,1)} %bitcast.34, bf16[1024,1024]{1,0:T(8,128)(2,1)} %w.5, f32[1,1024]{1,0:T(1,128)} %bitcast.44, bf16[100,1024]{1,0:T(8,128)(2,1)} %refs_9_.3, f32[1,100]{1,0:T(1,128)} %bitcast.47), custom_call_target="tpu_custom_call" | custom-call | flops 2357198848 | bytes 10485760 | tf_op jit(solution)/shard_map/pallas_call | solution.py:104
  18.3 0.6 pad_add_fusion.where
  19.5 0.7 collective-permute-done.2.refs_1_
  20.2 1.0 collective-permute-start.3
  21.2 1.5 %collective-permute-start.4 = (f32[100,1024]{1,0:T(8,128)}, f32[100,1024]{1,0:T(8,128)S(1)}, u32[]{:S(2)}, u32[]{:S(2)}) collective-permute-start(f32[100,1024]{1,0:T(8,128)} %get-tuple-element.46.refs_0_), channel_id=1, source_target_pairs={{0,64},{4,68},{8,72},{12,76},{64,0},{68,4},{72,8},{76,12},{16,80},... | collective-permute-start | bytes 1228808 | tf_op jit(solution)/shard_map/ppermute | solution.py:48
  22.7 0.7 copy.14.refs_6_
  23.4 0.8 copy-done.6
  24.2 5.7 %shard_map.129 = (bf16[1024,1024]{1,0:T(8,128)(2,1)}, f32[128,1024]{1,0:T(8,128)}) custom-call(f32[100,1024]{1,0:T(8,128)} %get-tuple-element.45.refs_0_, f32[100,1024]{1,0:T(8,128)} %copy-done.4, f32[100,1024]{1,0:T(8,128)} %copy-done.3, f32[100,1024]{1,0:T(8,128)} %copy-done.6, f32[100,2048]{1,0:T(8,128)} %refs_4_.3, f32[1,2048]{1,0:T(1,128)} %bitcast.40, ...), custom_call_target="tpu_custom_call" | custom-call | flops 1 | bytes 1 | tf_op jit(solution)/shard_map/pallas_call | solution.py:228
  29.9 2.9 %collective-permute-done.4.refs_2_ = f32[100,1024]{1,0:T(8,128)S(1)} collective-permute-done((f32[100,1024]{1,0:T(8,128)}, f32[100,1024]{1,0:T(8,128)S(1)}, u32[]{:S(2)}, u32[]{:S(2)}) %collective-permute-start.4) | collective-permute-done | bytes 409632 | tf_op jit(solution)/shard_map/ppermute | solution.py:48
  32.8 0.9 collective-permute-start.5
  33.7 1.4 %collective-permute-done.5.refs_3_ = f32[100,1024]{1,0:T(8,128)S(1)} collective-permute-done((f32[100,1024]{1,0:T(8,128)S(1)}, f32[100,1024]{1,0:T(8,128)S(1)}, u32[]{:S(2)}, u32[]{:S(2)}) %collective-permute-start.5) | collective-permute-done | bytes 409632 | tf_op jit(solution)/shard_map/ppermute | solution.py:48
  35.1 0.8 copy-done.7
  35.9 10.3 %shard_map.130 = (bf16[1024,1024]{1,0:T(8,128)(2,1)}, f32[128,1024]{1,0:T(8,128)}, f32[4,288,512]{2,1,0:T(8,128)}) custom-call(s32[4]{0:T(128)} %pad_add_fusion.where, f32[100,1024]{1,0:T(8,128)} %get-tuple-element.46.refs_0_, f32[100,1024]{1,0:T(8,128)} %copy-done.2, f32[100,1024]{1,0:T(8,128)} %copy-done.5, f32[100,1024]{1,0:T(8,128)} %copy-done.7, ...), custom_call_target="tpu_custom_call" | custom-call | flops 2147483648 | bytes 16728064 | tf_op jit(solution)/shard_map/pallas_call | solution.py:262
  46.7 6.7 %shard_map.131 = f32[4,288,512]{2,1,0:T(8,128)} custom-call(s32[4]{0:T(128)} %pad_add_fusion.where, bf16[2048,1024]{1,0:T(8,128)(2,1)} %bitcast.36, bf16[2048,1024]{1,0:T(8,128)(2,1)} %bitcast.37, bf16[1024,1024]{1,0:T(8,128)(2,1)} %get-tuple-element.73.refs_12_.dpre0, bf16[1024,1024]{1,0:T(8,128)(2,1)} %get-tuple-element.74.dpre1, ...), custom_call_target="tpu_custom_call" | custom-call | flops 2147483648 | bytes 8388608 | tf_op jit(solution)/shard_map/pallas_call | solution.py:307
  53.4 1.3 fusion
  54.7 1.2 add_bitcast_fusion.2
  56.0 2.7 %collective-permute-start.9 = (f32[288,512]{1,0:T(8,128)S(1)}, f32[288,512]{1,0:T(8,128)S(1)}, u32[]{:S(2)}, u32[]{:S(2)}) collective-permute-start(f32[288,512]{1,0:T(8,128)S(1)} %add_bitcast_fusion.1), channel_id=1, source_target_pairs={{0,12},{4,0},{8,4},{12,8},{64,76},{68,64},{72,68},{76,72},{16,28},... | collective-permute-start | bytes 1769480 | tf_op jit(solution)/shard_map/ppermute | solution.py:48
  58.7 1.7 %collective-permute-start.7 = (f32[288,512]{1,0:T(8,128)S(1)}, f32[288,512]{1,0:T(8,128)S(1)}, u32[]{:S(2)}, u32[]{:S(2)}) collective-permute-start(f32[288,512]{1,0:T(8,128)S(1)} %fusion), channel_id=1, source_target_pairs={{0,8},{4,12},{8,0},{12,4},{64,72},{68,76},{72,64},{76,68},{16,24},... | collective-permute-start | bytes 1769480 | tf_op jit(solution)/shard_map/ppermute | solution.py:48
  60.5 8.8 %shard_map.132 = bf16[1,2048,1024]{2,1,0:T(8,128)(2,1)} custom-call(bf16[1024,1024]{1,0:T(8,128)(2,1)} %get-tuple-element.73.refs_12_.dpre0, bf16[1024,1024]{1,0:T(8,128)(2,1)} %get-tuple-element.74.dpre1, bf16[1024,1024]{1,0:T(8,128)(2,1)} %w.5), custom_call_target="tpu_custom_call" | custom-call | flops 4294967296 | bytes 10485760 | tf_op jit(solution)/shard_map/pallas_call | solution.py:341
  69.3 2.6 %collective-permute-done.9 = f32[288,512]{1,0:T(8,128)S(1)} collective-permute-done((f32[288,512]{1,0:T(8,128)S(1)}, f32[288,512]{1,0:T(8,128)S(1)}, u32[]{:S(2)}, u32[]{:S(2)}) %collective-permute-start.9) | collective-permute-done | bytes 589856 | tf_op jit(solution)/shard_map/ppermute | solution.py:48
  71.8 3.4 %collective-permute-done.8 = f32[288,512]{1,0:T(8,128)S(1)} collective-permute-done((f32[288,512]{1,0:T(8,128)S(1)}, f32[288,512]{1,0:T(8,128)S(1)}, u32[]{:S(2)}, u32[]{:S(2)}) %collective-permute-start.8) | collective-permute-done | bytes 589856 | tf_op jit(solution)/shard_map/ppermute | solution.py:48
  75.5 1.4 %collective-permute-start.10 = (f32[72,512]{1,0:T(8,128)S(1)}, f32[72,512]{1,0:T(8,128)S(1)}, u32[]{:S(2)}, u32[]{:S(2)}) collective-permute-start(f32[72,512]{1,0:T(8,128)S(1)} %get-tuple-element.84), channel_id=1, source_target_pairs={{0,1},{4,5},{8,9},{12,13},{64,65},{68,69},{72,73},{76,77},{16,17},... | collective-permute-start | bytes 442376 | tf_op jit(solution)/shard_map/ppermute | solution.py:48
  76.9 2.2 %collective-permute-start.11 = (f32[72,512]{1,0:T(8,128)S(1)}, f32[72,512]{1,0:T(8,128)S(1)}, u32[]{:S(2)}, u32[]{:S(2)}) collective-permute-start(f32[72,512]{1,0:T(8,128)S(1)} %get-tuple-element.86), channel_id=1, source_target_pairs={{0,3},{4,7},{8,11},{12,15},{64,67},{68,71},{72,75},{76,79},{16,19}... | collective-permute-start | bytes 442376 | tf_op jit(solution)/shard_map/ppermute | solution.py:48
  79.1 1.2 collective-permute-start.12
  80.4 1.2 collective-permute-done.10
  81.6 3.0 %collective-permute-done.12 = f32[72,512]{1,0:T(8,128)S(1)} collective-permute-done((f32[72,512]{1,0:T(8,128)S(1)}, f32[72,512]{1,0:T(8,128)S(1)}, u32[]{:S(2)}, u32[]{:S(2)}) %collective-permute-start.12) | collective-permute-done | bytes 147488 | tf_op jit(solution)/shard_map/ppermute | solution.py:48
  84.7 1.4 %collective-permute-start.13 = (f32[72,512]{1,0:T(8,128)S(1)}, f32[72,512]{1,0:T(8,128)S(1)}, u32[]{:S(2)}, u32[]{:S(2)}) collective-permute-start(f32[72,512]{1,0:T(8,128)S(1)} %fusion.2), channel_id=1, source_target_pairs={{0,64},{4,68},{8,72},{12,76},{64,16},{68,20},{72,24},{76,28},{16,8... | collective-permute-start | bytes 442376 | tf_op jit(solution)/shard_map/ppermute | solution.py:48
  86.0 1.5 %collective-permute-start.14 = (f32[72,512]{1,0:T(8,128)S(1)}, f32[72,512]{1,0:T(8,128)S(1)}, u32[]{:S(2)}, u32[]{:S(2)}) collective-permute-start(f32[72,512]{1,0:T(8,128)S(1)} %fusion.2), channel_id=1, source_target_pairs={{0,80},{4,84},{8,88},{12,92},{64,0},{68,4},{72,8},{76,12},{16,64},... | collective-permute-start | bytes 442376 | tf_op jit(solution)/shard_map/ppermute | solution.py:48
  87.6 1.6 %collective-permute-start.15 = (f32[72,512]{1,0:T(8,128)S(1)}, f32[72,512]{1,0:T(8,128)S(1)}, u32[]{:S(2)}, u32[]{:S(2)}) collective-permute-start(f32[72,512]{1,0:T(8,128)S(1)} %fusion.2), channel_id=1, source_target_pairs={{0,16},{4,20},{8,24},{12,28},{64,80},{68,84},{72,88},{76,92},{16,0... | collective-permute-start | bytes 442376 | tf_op jit(solution)/shard_map/ppermute | solution.py:48
  89.1 0.9 collective-permute-done.13
  90.0 3.1 %collective-permute-done.15 = f32[72,512]{1,0:T(8,128)S(1)} collective-permute-done((f32[72,512]{1,0:T(8,128)S(1)}, f32[72,512]{1,0:T(8,128)S(1)}, u32[]{:S(2)}, u32[]{:S(2)}) %collective-permute-start.15) | collective-permute-done | bytes 147488 | tf_op jit(solution)/shard_map/ppermute | solution.py:48
  93.2 3.5 %collective-permute-start.16 = (f32[72,512]{1,0:T(8,128)S(1)}, f32[72,512]{1,0:T(8,128)S(1)}, u32[]{:S(2)}, u32[]{:S(2)}) collective-permute-start(f32[72,512]{1,0:T(8,128)S(1)} %add_add_fusion.1), channel_id=1, source_target_pairs={{0,3},{4,7},{8,11},{12,15},{64,67},{68,71},{72,75},{76,79},{16,19}... | collective-permute-start | bytes 442376 | tf_op jit(solution)/shard_map/ppermute | solution.py:48
  96.7 1.2 collective-permute-start.17
  98.0 2.4 %collective-permute-done.16 = f32[72,512]{1,0:T(8,128)S(1)} collective-permute-done((f32[72,512]{1,0:T(8,128)S(1)}, f32[72,512]{1,0:T(8,128)S(1)}, u32[]{:S(2)}, u32[]{:S(2)}) %collective-permute-start.16) | collective-permute-done | bytes 147488 | tf_op jit(solution)/shard_map/ppermute | solution.py:48
  100.4 1.9 %collective-permute-done.17 = f32[72,512]{1,0:T(8,128)S(1)} collective-permute-done((f32[72,512]{1,0:T(8,128)S(1)}, f32[72,512]{1,0:T(8,128)S(1)}, u32[]{:S(2)}, u32[]{:S(2)}) %collective-permute-start.17) | collective-permute-done | bytes 147488 | tf_op jit(solution)/shard_map/ppermute | solution.py:48
  102.3 1.5 %collective-permute-done.18 = f32[72,512]{1,0:T(8,128)S(1)} collective-permute-done((f32[72,512]{1,0:T(8,128)S(1)}, f32[72,512]{1,0:T(8,128)S(1)}, u32[]{:S(2)}, u32[]{:S(2)}) %collective-permute-start.18) | collective-permute-done | bytes 147488 | tf_op jit(solution)/shard_map/ppermute | solution.py:48
  104.6 2.1 %collective-permute-start.21 = (f32[288,512]{1,0:T(8,128)S(1)}, f32[288,512]{1,0:T(8,128)S(1)}, u32[]{:S(2)}, u32[]{:S(2)}) collective-permute-start(f32[288,512]{1,0:T(8,128)S(1)} %constant_dynamic-slice_fusion.refs_0_), channel_id=1, source_target_pairs={{0,12},{4,0},{8,4},{12,8},{64,76},{68,64},{72,68},{76,72},{16,28},... | collective-permute-start | bytes 1769480 | tf_op jit(solution)/shard_map/ppermute | solution.py:48
  106.7 4.6 %collective-permute-start.22 = (f32[288,512]{1,0:T(8,128)S(1)}, f32[288,512]{1,0:T(8,128)S(1)}, u32[]{:S(2)}, u32[]{:S(2)}) collective-permute-start(f32[288,512]{1,0:T(8,128)S(1)} %constant_dynamic-slice_fusion.refs_0_), channel_id=1, source_target_pairs={{0,32},{4,36},{8,40},{12,44},{64,96},{68,100},{72,104},{76,108},{1... | collective-permute-start | bytes 1769480 | tf_op jit(solution)/shard_map/ppermute | solution.py:48
  111.3 9.3 %collective-permute-done.19.refs_1_ = f32[288,512]{1,0:T(8,128)S(1)} collective-permute-done((f32[288,512]{1,0:T(8,128)S(1)}, f32[288,512]{1,0:T(8,128)S(1)}, u32[]{:S(2)}, u32[]{:S(2)}) %collective-permute-start.19) | collective-permute-done | bytes 589856 | tf_op jit(solution)/shard_map/ppermute | solution.py:48
  120.6 4.9 %collective-permute-start.23 = (f32[288,512]{1,0:T(8,128)S(1)}, f32[288,512]{1,0:T(8,128)S(1)}, u32[]{:S(2)}, u32[]{:S(2)}) collective-permute-start(f32[288,512]{1,0:T(8,128)S(1)} %collective-permute-done.19.refs_1_), channel_id=1, source_target_pairs={{0,32},{4,36},{8,40},{12,44},{64,96},{68,100},{72,104},{76,108},{1... | collective-permute-start | bytes 1769480 | tf_op jit(solution)/shard_map/ppermute | solution.py:48
  125.5 0.9 collective-permute-start.25
  126.4 0.7 collective-permute-done.23.refs_5_
  127.2 0.8 collective-permute-done.24.refs_6_
  128.0 0.8 collective-permute-done.25.refs_7_
  128.8 2.9 %shard_map.133 = (f32[1024,1024]{1,0:T(8,128)}, f32[100,1024]{1,0:T(8,128)}, f32[1,1024]{1,0:T(1,128)}, f32[1,100]{1,0:T(1,128)}, f32[1,1]{1,0:T(1,128)}) custom-call(s32[4]{0:T(128)S(1)} %copy-done, f32[288,512]{1,0:T(8,128)S(1)} %constant_dynamic-slice_fusion.refs_0_, f32[288,512]{1,0:T(8,128)S(1)} %collective-permute-done.19.refs_1_, ...), custom_call_target="tpu_custom_call" | custom-call | bytes 8388608 | tf_op jit(solution)/shard_map/pallas_call | solution.py:375
  (47 shorter events, 2.5 us)
Async XLA Ops:
  7.9 14.8 %copy-start.8 = (f32[100]{0:T(128)S(1)}, f32[100]{0:T(128)}, u32[]{:S(2)}) copy-start(f32[100]{0:T(128)} %param.11) | copy-start | bytes 1204
  7.9 11.5 %collective-permute-start = (f32[100,1024]{1,0:T(8,128)}, f32[100,1024]{1,0:T(8,128)S(1)}, u32[]{:S(2)}, u32[]{:S(2)}) collective-permute-start(f32[100,1024]{1,0:T(8,128)} %get-tuple-element.45.refs_0_), channel_id=1, source_target_pairs={{0,64},{4,68},{8,72},{12,76},{64,0},{68,4},{72,8},{76,12},{16,80},... | collective-permute-start | bytes 1228808 | tf_op jit(solution)/shard_map/ppermute | solution.py:48
  10.1 9.3 %collective-permute-start.1 = (f32[100,1024]{1,0:T(8,128)}, f32[100,1024]{1,0:T(8,128)S(1)}, u32[]{:S(2)}, u32[]{:S(2)}) collective-permute-start(f32[100,1024]{1,0:T(8,128)} %get-tuple-element.45.refs_0_), channel_id=1, source_target_pairs={{0,32},{4,36},{8,40},{12,44},{64,96},{68,100},{72,104},{76,108},{1... | collective-permute-start | bytes 1228808 | tf_op jit(solution)/shard_map/ppermute | solution.py:48
  18.2 2.0 %collective-permute-start.2 = (f32[100,1024]{1,0:T(8,128)}, f32[100,1024]{1,0:T(8,128)S(1)}, u32[]{:S(2)}, u32[]{:S(2)}) collective-permute-start(f32[100,1024]{1,0:T(8,128)} %get-tuple-element.46.refs_0_), channel_id=1, source_target_pairs={{0,32},{4,36},{8,40},{12,44},{64,96},{68,100},{72,104},{76,108},{1... | collective-permute-start | bytes 1228808 | tf_op jit(solution)/shard_map/ppermute | solution.py:48
  19.5 4.0 %copy-start.3 = (f32[100,1024]{1,0:T(8,128)}, f32[100,1024]{1,0:T(8,128)S(1)}, u32[]{:S(2)}) copy-start(f32[100,1024]{1,0:T(8,128)S(1)} %collective-permute-done.refs_2_) | copy-start | bytes 1228804
  19.5 4.0 %copy-start.4 = (f32[100,1024]{1,0:T(8,128)}, f32[100,1024]{1,0:T(8,128)S(1)}, u32[]{:S(2)}) copy-start(f32[100,1024]{1,0:T(8,128)S(1)} %collective-permute-done.1.refs_1_) | copy-start | bytes 1228804
  20.2 9.6 %copy-start.2 = (f32[100,1024]{1,0:T(8,128)}, f32[100,1024]{1,0:T(8,128)S(1)}, u32[]{:S(2)}) copy-start(f32[100,1024]{1,0:T(8,128)S(1)} %collective-permute-done.2.refs_1_) | copy-start | bytes 1228804
  20.2 3.2 %collective-permute-start.3 = (f32[100,1024]{1,0:T(8,128)S(1)}, f32[100,1024]{1,0:T(8,128)S(1)}, u32[]{:S(2)}, u32[]{:S(2)}) collective-permute-start(f32[100,1024]{1,0:T(8,128)S(1)} %collective-permute-done.refs_2_), channel_id=1, source_target_pairs={{0,32},{4,36},{8,40},{12,44},{64,96},{68,100},{72,104},{76,108},{1... | collective-permute-start | bytes 1228808 | tf_op jit(solution)/shard_map/ppermute | solution.py:48
  21.2 11.6 %collective-permute-start.4 = (f32[100,1024]{1,0:T(8,128)}, f32[100,1024]{1,0:T(8,128)S(1)}, u32[]{:S(2)}, u32[]{:S(2)}) collective-permute-start(f32[100,1024]{1,0:T(8,128)} %get-tuple-element.46.refs_0_), channel_id=1, source_target_pairs={{0,64},{4,68},{8,72},{12,76},{64,0},{68,4},{72,8},{76,12},{16,80},... | collective-permute-start | bytes 1228808 | tf_op jit(solution)/shard_map/ppermute | solution.py:48
  23.4 0.8 copy-start.6
  32.8 2.3 %copy-start.5 = (f32[100,1024]{1,0:T(8,128)}, f32[100,1024]{1,0:T(8,128)S(1)}, u32[]{:S(2)}) copy-start(f32[100,1024]{1,0:T(8,128)S(1)} %collective-permute-done.4.refs_2_) | copy-start | bytes 1228804
  32.8 2.3 %collective-permute-start.5 = (f32[100,1024]{1,0:T(8,128)S(1)}, f32[100,1024]{1,0:T(8,128)S(1)}, u32[]{:S(2)}, u32[]{:S(2)}) collective-permute-start(f32[100,1024]{1,0:T(8,128)S(1)} %collective-permute-done.4.refs_2_), channel_id=1, source_target_pairs={{0,32},{4,36},{8,40},{12,44},{64,96},{68,100},{72,104},{76,108},{1... | collective-permute-start | bytes 1228808 | tf_op jit(solution)/shard_map/ppermute | solution.py:48
  35.1 0.8 copy-start.7
  46.2 7.2 %collective-permute-start.6 = (f32[4,288,512]{2,1,0:T(8,128)}, f32[4,288,512]{2,1,0:T(8,128)S(1)}, u32[]{:S(2)}, u32[]{:S(2)}) collective-permute-start(f32[4,288,512]{2,1,0:T(8,128)} %get-tuple-element.61), channel_id=1, source_target_pairs={{0,32},{4,36},{8,40},{12,44},{64,96},{68,100},{72,104},{76,108},{1... | collective-permute-start | bytes 7077896 | tf_op jit(solution)/shard_map/ppermute | solution.py:48
  53.4 2.5 %copy-start.1 = (f32[4,288,512]{2,1,0:T(8,128)S(1)}, f32[4,288,512]{2,1,0:T(8,128)}, u32[]{:S(2)}) copy-start(f32[4,288,512]{2,1,0:T(8,128)} %shard_map.131) | copy-start | bytes 7077892
  56.0 15.8 %collective-permute-start.9 = (f32[288,512]{1,0:T(8,128)S(1)}, f32[288,512]{1,0:T(8,128)S(1)}, u32[]{:S(2)}, u32[]{:S(2)}) collective-permute-start(f32[288,512]{1,0:T(8,128)S(1)} %add_bitcast_fusion.1), channel_id=1, source_target_pairs={{0,12},{4,0},{8,4},{12,8},{64,76},{68,64},{72,68},{76,72},{16,28},... | collective-permute-start | bytes 1769480 | tf_op jit(solution)/shard_map/ppermute | solution.py:48
  58.7 16.6 %collective-permute-start.8 = (f32[288,512]{1,0:T(8,128)S(1)}, f32[288,512]{1,0:T(8,128)S(1)}, u32[]{:S(2)}, u32[]{:S(2)}) collective-permute-start(f32[288,512]{1,0:T(8,128)S(1)} %add_bitcast_fusion.2), channel_id=1, source_target_pairs={{0,4},{4,8},{8,12},{12,0},{64,68},{68,72},{72,76},{76,64},{16,20},... | collective-permute-start | bytes 1769480 | tf_op jit(solution)/shard_map/ppermute | solution.py:48
  58.7 16.6 %collective-permute-start.7 = (f32[288,512]{1,0:T(8,128)S(1)}, f32[288,512]{1,0:T(8,128)S(1)}, u32[]{:S(2)}, u32[]{:S(2)}) collective-permute-start(f32[288,512]{1,0:T(8,128)S(1)} %fusion), channel_id=1, source_target_pairs={{0,8},{4,12},{8,0},{12,4},{64,72},{68,76},{72,64},{76,68},{16,24},... | collective-permute-start | bytes 1769480 | tf_op jit(solution)/shard_map/ppermute | solution.py:48
  75.5 6.0 %collective-permute-start.10 = (f32[72,512]{1,0:T(8,128)S(1)}, f32[72,512]{1,0:T(8,128)S(1)}, u32[]{:S(2)}, u32[]{:S(2)}) collective-permute-start(f32[72,512]{1,0:T(8,128)S(1)} %get-tuple-element.84), channel_id=1, source_target_pairs={{0,1},{4,5},{8,9},{12,13},{64,65},{68,69},{72,73},{76,77},{16,17},... | collective-permute-start | bytes 442376 | tf_op jit(solution)/shard_map/ppermute | solution.py:48
  76.9 4.7 %collective-permute-start.11 = (f32[72,512]{1,0:T(8,128)S(1)}, f32[72,512]{1,0:T(8,128)S(1)}, u32[]{:S(2)}, u32[]{:S(2)}) collective-permute-start(f32[72,512]{1,0:T(8,128)S(1)} %get-tuple-element.86), channel_id=1, source_target_pairs={{0,3},{4,7},{8,11},{12,15},{64,67},{68,71},{72,75},{76,79},{16,19}... | collective-permute-start | bytes 442376 | tf_op jit(solution)/shard_map/ppermute | solution.py:48
  79.1 5.5 %collective-permute-start.12 = (f32[72,512]{1,0:T(8,128)S(1)}, f32[72,512]{1,0:T(8,128)S(1)}, u32[]{:S(2)}, u32[]{:S(2)}) collective-permute-start(f32[72,512]{1,0:T(8,128)S(1)} %get-tuple-element.85), channel_id=1, source_target_pairs={{0,2},{4,6},{8,10},{12,14},{64,66},{68,70},{72,74},{76,78},{16,18}... | collective-permute-start | bytes 442376 | tf_op jit(solution)/shard_map/ppermute | solution.py:48
  80.4 48.5 %copy-start = (s32[4]{0:T(128)S(1)}, s32[4]{0:T(128)}, u32[]{:S(2)}) copy-start(s32[4]{0:T(128)} %pad_add_fusion.where) | copy-start | bytes 52
  84.7 5.4 %collective-permute-start.13 = (f32[72,512]{1,0:T(8,128)S(1)}, f32[72,512]{1,0:T(8,128)S(1)}, u32[]{:S(2)}, u32[]{:S(2)}) collective-permute-start(f32[72,512]{1,0:T(8,128)S(1)} %fusion.2), channel_id=1, source_target_pairs={{0,64},{4,68},{8,72},{12,76},{64,16},{68,20},{72,24},{76,28},{16,8... | collective-permute-start | bytes 442376 | tf_op jit(solution)/shard_map/ppermute | solution.py:48
  86.0 4.0 %collective-permute-start.14 = (f32[72,512]{1,0:T(8,128)S(1)}, f32[72,512]{1,0:T(8,128)S(1)}, u32[]{:S(2)}, u32[]{:S(2)}) collective-permute-start(f32[72,512]{1,0:T(8,128)S(1)} %fusion.2), channel_id=1, source_target_pairs={{0,80},{4,84},{8,88},{12,92},{64,0},{68,4},{72,8},{76,12},{16,64},... | collective-permute-start | bytes 442376 | tf_op jit(solution)/shard_map/ppermute | solution.py:48
  87.6 5.6 %collective-permute-start.15 = (f32[72,512]{1,0:T(8,128)S(1)}, f32[72,512]{1,0:T(8,128)S(1)}, u32[]{:S(2)}, u32[]{:S(2)}) collective-permute-start(f32[72,512]{1,0:T(8,128)S(1)} %fusion.2), channel_id=1, source_target_pairs={{0,16},{4,20},{8,24},{12,28},{64,80},{68,84},{72,88},{76,92},{16,0... | collective-permute-start | bytes 442376 | tf_op jit(solution)/shard_map/ppermute | solution.py:48
  93.2 7.2 %collective-permute-start.16 = (f32[72,512]{1,0:T(8,128)S(1)}, f32[72,512]{1,0:T(8,128)S(1)}, u32[]{:S(2)}, u32[]{:S(2)}) collective-permute-start(f32[72,512]{1,0:T(8,128)S(1)} %add_add_fusion.1), channel_id=1, source_target_pairs={{0,3},{4,7},{8,11},{12,15},{64,67},{68,71},{72,75},{76,79},{16,19}... | collective-permute-start | bytes 442376 | tf_op jit(solution)/shard_map/ppermute | solution.py:48
  96.7 5.6 %collective-permute-start.17 = (f32[72,512]{1,0:T(8,128)S(1)}, f32[72,512]{1,0:T(8,128)S(1)}, u32[]{:S(2)}, u32[]{:S(2)}) collective-permute-start(f32[72,512]{1,0:T(8,128)S(1)} %add_add_fusion.1), channel_id=1, source_target_pairs={{0,2},{4,6},{8,10},{12,14},{64,66},{68,70},{72,74},{76,78},{16,18}... | collective-permute-start | bytes 442376 | tf_op jit(solution)/shard_map/ppermute | solution.py:48
  98.0 5.8 %collective-permute-start.18 = (f32[72,512]{1,0:T(8,128)S(1)}, f32[72,512]{1,0:T(8,128)S(1)}, u32[]{:S(2)}, u32[]{:S(2)}) collective-permute-start(f32[72,512]{1,0:T(8,128)S(1)} %add_add_fusion.1), channel_id=1, source_target_pairs={{0,1},{4,5},{8,9},{12,13},{64,65},{68,69},{72,73},{76,77},{16,17},... | collective-permute-start | bytes 442376 | tf_op jit(solution)/shard_map/ppermute | solution.py:48
  104.0 16.6 %collective-permute-start.19 = (f32[288,512]{1,0:T(8,128)S(1)}, f32[288,512]{1,0:T(8,128)S(1)}, u32[]{:S(2)}, u32[]{:S(2)}) collective-permute-start(f32[288,512]{1,0:T(8,128)S(1)} %constant_dynamic-slice_fusion.refs_0_), channel_id=1, source_target_pairs={{0,4},{4,8},{8,12},{12,0},{64,68},{68,72},{72,76},{76,64},{16,20},... | collective-permute-start | bytes 1769480 | tf_op jit(solution)/shard_map/ppermute | solution.py:48
  104.1 21.5 %collective-permute-start.20 = (f32[288,512]{1,0:T(8,128)S(1)}, f32[288,512]{1,0:T(8,128)S(1)}, u32[]{:S(2)}, u32[]{:S(2)}) collective-permute-start(f32[288,512]{1,0:T(8,128)S(1)} %constant_dynamic-slice_fusion.refs_0_), channel_id=1, source_target_pairs={{0,8},{4,12},{8,0},{12,4},{64,72},{68,76},{72,64},{76,68},{16,24},... | collective-permute-start | bytes 1769480 | tf_op jit(solution)/shard_map/ppermute | solution.py:48
  104.6 20.9 %collective-permute-start.21 = (f32[288,512]{1,0:T(8,128)S(1)}, f32[288,512]{1,0:T(8,128)S(1)}, u32[]{:S(2)}, u32[]{:S(2)}) collective-permute-start(f32[288,512]{1,0:T(8,128)S(1)} %constant_dynamic-slice_fusion.refs_0_), channel_id=1, source_target_pairs={{0,12},{4,0},{8,4},{12,8},{64,76},{68,64},{72,68},{76,72},{16,28},... | collective-permute-start | bytes 1769480 | tf_op jit(solution)/shard_map/ppermute | solution.py:48
  106.7 19.7 %collective-permute-start.22 = (f32[288,512]{1,0:T(8,128)S(1)}, f32[288,512]{1,0:T(8,128)S(1)}, u32[]{:S(2)}, u32[]{:S(2)}) collective-permute-start(f32[288,512]{1,0:T(8,128)S(1)} %constant_dynamic-slice_fusion.refs_0_), channel_id=1, source_target_pairs={{0,32},{4,36},{8,40},{12,44},{64,96},{68,100},{72,104},{76,108},{1... | collective-permute-start | bytes 1769480 | tf_op jit(solution)/shard_map/ppermute | solution.py:48
  120.6 6.5 %collective-permute-start.23 = (f32[288,512]{1,0:T(8,128)S(1)}, f32[288,512]{1,0:T(8,128)S(1)}, u32[]{:S(2)}, u32[]{:S(2)}) collective-permute-start(f32[288,512]{1,0:T(8,128)S(1)} %collective-permute-done.19.refs_1_), channel_id=1, source_target_pairs={{0,32},{4,36},{8,40},{12,44},{64,96},{68,100},{72,104},{76,108},{1... | collective-permute-start | bytes 1769480 | tf_op jit(solution)/shard_map/ppermute | solution.py:48
  125.5 2.5 %collective-permute-start.24 = (f32[288,512]{1,0:T(8,128)S(1)}, f32[288,512]{1,0:T(8,128)S(1)}, u32[]{:S(2)}, u32[]{:S(2)}) collective-permute-start(f32[288,512]{1,0:T(8,128)S(1)} %collective-permute-done.20.refs_2_), channel_id=1, source_target_pairs={{0,32},{4,36},{8,40},{12,44},{64,96},{68,100},{72,104},{76,108},{1... | collective-permute-start | bytes 1769480 | tf_op jit(solution)/shard_map/ppermute | solution.py:48
  125.5 3.3 %collective-permute-start.25 = (f32[288,512]{1,0:T(8,128)S(1)}, f32[288,512]{1,0:T(8,128)S(1)}, u32[]{:S(2)}, u32[]{:S(2)}) collective-permute-start(f32[288,512]{1,0:T(8,128)S(1)} %collective-permute-done.21.refs_3_), channel_id=1, source_target_pairs={{0,32},{4,36},{8,40},{12,44},{64,96},{68,100},{72,104},{76,108},{1... | collective-permute-start | bytes 1769480 | tf_op jit(solution)/shard_map/ppermute | solution.py:48

commit v6 on v5

--- a/solution.py
+++ b/solution.py
@@ -212,11 +212,13 @@
 
     @pl.when(g >= steps)
     def _():
-        columns(g - steps).wait()
+        for j in range(out.shape[0]):
+            columns(out.shape[0] * (g - steps) + j).wait()
         cols = pl.ds(pl.multiple_of(where[which] * half, half), half)
-        weight_block(
-            numbers[1], which, where, g - steps, lat_held.at[g - steps], (half0[...], mine[:, cols]), rest, out
-        )
+        dpres = (half0[...], mine[:, cols])
+        for j in range(out.shape[0]):
+            k = out.shape[0] * (g - steps) + j
+            weight_block(numbers[1], which, where, k, lat_held.at[k], dpres, rest, out, j)
 
 
 def cotangent(numbers, part, own, others, target, area, var, sp, hid, w_output, tile=512):
@@ -263,7 +265,7 @@
         functools.partial(cot_weight_kernel, numbers, steps, which),
         grid_spec=pltpu.PrefetchScalarGridSpec(
             num_scalar_prefetch=1,
-            grid=(steps + 4,),
+            grid=(steps + 2,),
             in_specs=[local] * 4
             + [
                 pl.BlockSpec((n_vars, tile), lambda g, s: (0, part * steps + at(g))),
@@ -276,7 +278,7 @@
                 hbm,
                 hbm,
             ],
-            out_specs=[rows, whole((128, width)), pl.BlockSpec((1, block + 32, half), lambda g, s: (step(g), 0, 0))],
+            out_specs=[rows, whole((128, width)), pl.BlockSpec((2, block + 32, half), lambda g, s: (step(g), 0, 0))],
             scratch_shapes=[
                 pltpu.VMEM((n, width), BF16),
                 pltpu.VMEM((4, points, block), BF16),

time: 132 us -> 132 us (level)
  waiting for transfers between devices: 37.4 us -> 30.3 us
  starting transfers between devices: 38.7 us -> 45.8 us
    ppermute x26, waiting for transfers between devices: 37.4 us -> 30.3 us  [send(): return lax.ppermute(array, ALL, pairs)]
    ppermute x26, starting transfers between devices: 38.7 us -> 45.8 us  [send(): return lax.ppermute(array, ALL, pairs)]
where the time goes in v6:
time: 132 us; the launch traced here: 131 us
  Pallas kernels  48.5 us (37%)
  starting transfers between devices  45.8 us (35%)
  waiting for transfers between devices  30.3 us (23%)
  other arithmetic  3.64 us (3%)
  local copies, waits for them, and re-layouts  2.5 us (2%)
    ppermute x26, starting transfers between devices, send(): return lax.ppermute(array, ALL, pairs)  45.8 us
    ppermute x26, waiting for transfers between devices, send(): return lax.ppermute(array, ALL, pairs)  30.3 us
    pallas_call x2, Pallas kernels, forward(): pl.pallas_call(forward_kernel, grid=(steps,), in_specs=[pl.BlockSpec((til...  14.4 us
    pallas_call x1, Pallas kernels, cotangent_weight(): pl.pallas_call(functools.partial(cot_weight_kernel, numbers, steps, which...  10.1 us
    pallas_call x1, Pallas kernels, latent_gradient(): pl.pallas_call(functools.partial(latent_kernel, steps), grid=(2 * steps,)...  8.76 us
    pallas_call x1, Pallas kernels, weight_grad(): pl.pallas_call(functools.partial(weight_kernel, scale, which), grid_spec=...  6.66 us
    pallas_call x1, Pallas kernels, cotangent(): pl.pallas_call(functools.partial(cot_kernel, numbers), grid=(steps,), in_...  5.66 us
    pallas_call x1, Pallas kernels, join(): pl.pallas_call(functools.partial(join_kernel, n_vars), in_specs=[pl.Block...  2.9 us
  transfers between devices with their start and end apart: 26, of which 17 were waited for; matrix products, arithmetic and copies ran while one was open for 1% of the time, Pallas kernels for 21%

profile of v6, /device:TPU:1, one launch (start us, length us, event | category | flops | bytes accessed | tf_op | source)
XLA Modules:
  0.0 131.5 jit_solution(2632312835261874821)
XLA Ops:
  0.6 7.3 %shard_map.127 = (f32[100,1024]{1,0:T(8,128)}, bf16[1024,1024]{1,0:T(8,128)(2,1)}, f32[1024,1024]{1,0:T(8,128)}) custom-call(bf16[2048,1024]{1,0:T(8,128)(2,1)} %bitcast.33, bf16[1024,1024]{1,0:T(8,128)(2,1)} %w.5, f32[1,1024]{1,0:T(1,128)} %bitcast.43, bf16[100,1024]{1,0:T(8,128)(2,1)} %refs_9_.3, f32[1,100]{1,0:T(1,128)} %bitcast.46), custom_call_target="tpu_custom_call" | custom-call | flops 2357198848 | bytes 10485760 | tf_op jit(solution)/shard_map/pallas_call | solution.py:104
  7.9 2.2 %collective-permute-start = (f32[100,1024]{1,0:T(8,128)}, f32[100,1024]{1,0:T(8,128)S(1)}, u32[]{:S(2)}, u32[]{:S(2)}) collective-permute-start(f32[100,1024]{1,0:T(8,128)} %get-tuple-element.45.refs_0_), channel_id=1, source_target_pairs={{0,64},{4,68},{8,72},{12,76},{64,0},{68,4},{72,8},{76,12},{16,80},... | collective-permute-start | bytes 1228808 | tf_op jit(solution)/shard_map/ppermute | solution.py:48
  10.1 1.0 collective-permute-start.1
  11.1 7.1 %shard_map.128 = (f32[100,1024]{1,0:T(8,128)}, bf16[1024,1024]{1,0:T(8,128)(2,1)}, f32[1024,1024]{1,0:T(8,128)}) custom-call(bf16[2048,1024]{1,0:T(8,128)(2,1)} %bitcast.34, bf16[1024,1024]{1,0:T(8,128)(2,1)} %w.5, f32[1,1024]{1,0:T(1,128)} %bitcast.44, bf16[100,1024]{1,0:T(8,128)(2,1)} %refs_9_.3, f32[1,100]{1,0:T(1,128)} %bitcast.47), custom_call_target="tpu_custom_call" | custom-call | flops 2357198848 | bytes 10485760 | tf_op jit(solution)/shard_map/pallas_call | solution.py:104
  19.5 0.7 collective-permute-done.2.refs_1_
  20.2 1.0 collective-permute-start.3
  21.2 1.5 %collective-permute-start.4 = (f32[100,1024]{1,0:T(8,128)}, f32[100,1024]{1,0:T(8,128)S(1)}, u32[]{:S(2)}, u32[]{:S(2)}) collective-permute-start(f32[100,1024]{1,0:T(8,128)} %get-tuple-element.46.refs_0_), channel_id=1, source_target_pairs={{0,64},{4,68},{8,72},{12,76},{64,0},{68,4},{72,8},{76,12},{16,80},... | collective-permute-start | bytes 1228808 | tf_op jit(solution)/shard_map/ppermute | solution.py:48
  22.7 0.7 copy.14.refs_6_
  23.4 0.8 copy-done.6
  24.2 5.7 %shard_map.129 = (bf16[1024,1024]{1,0:T(8,128)(2,1)}, f32[128,1024]{1,0:T(8,128)}) custom-call(f32[100,1024]{1,0:T(8,128)} %get-tuple-element.45.refs_0_, f32[100,1024]{1,0:T(8,128)} %copy-done.4, f32[100,1024]{1,0:T(8,128)} %copy-done.3, f32[100,1024]{1,0:T(8,128)} %copy-done.6, f32[100,2048]{1,0:T(8,128)} %refs_4_.3, f32[1,2048]{1,0:T(1,128)} %bitcast.40, ...), custom_call_target="tpu_custom_call" | custom-call | flops 1 | bytes 1 | tf_op jit(solution)/shard_map/pallas_call | solution.py:230
  29.9 2.9 %collective-permute-done.4.refs_2_ = f32[100,1024]{1,0:T(8,128)S(1)} collective-permute-done((f32[100,1024]{1,0:T(8,128)}, f32[100,1024]{1,0:T(8,128)S(1)}, u32[]{:S(2)}, u32[]{:S(2)}) %collective-permute-start.4) | collective-permute-done | bytes 409632 | tf_op jit(solution)/shard_map/ppermute | solution.py:48
  32.8 0.9 collective-permute-start.5
  33.7 1.4 %collective-permute-done.5.refs_3_ = f32[100,1024]{1,0:T(8,128)S(1)} collective-permute-done((f32[100,1024]{1,0:T(8,128)S(1)}, f32[100,1024]{1,0:T(8,128)S(1)}, u32[]{:S(2)}, u32[]{:S(2)}) %collective-permute-start.5) | collective-permute-done | bytes 409632 | tf_op jit(solution)/shard_map/ppermute | solution.py:48
  35.1 0.8 copy-done.7
  35.9 10.1 %shard_map.130 = (bf16[1024,1024]{1,0:T(8,128)(2,1)}, f32[128,1024]{1,0:T(8,128)}, f32[4,288,512]{2,1,0:T(8,128)}) custom-call(s32[4]{0:T(128)} %pad_add_fusion.where, f32[100,1024]{1,0:T(8,128)} %get-tuple-element.46.refs_0_, f32[100,1024]{1,0:T(8,128)} %copy-done.2, f32[100,1024]{1,0:T(8,128)} %copy-done.5, f32[100,1024]{1,0:T(8,128)} %copy-done.7, ...), custom_call_target="tpu_custom_call" | custom-call | flops 2147483648 | bytes 16728064 | tf_op jit(solution)/shard_map/pallas_call | solution.py:264
  46.4 6.7 %shard_map.131 = f32[4,288,512]{2,1,0:T(8,128)} custom-call(s32[4]{0:T(128)} %pad_add_fusion.where, bf16[2048,1024]{1,0:T(8,128)(2,1)} %bitcast.36, bf16[2048,1024]{1,0:T(8,128)(2,1)} %bitcast.37, bf16[1024,1024]{1,0:T(8,128)(2,1)} %get-tuple-element.73.refs_12_.dpre0, bf16[1024,1024]{1,0:T(8,128)(2,1)} %get-tuple-element.74.dpre1, ...), custom_call_target="tpu_custom_call" | custom-call | flops 2147483648 | bytes 8388608 | tf_op jit(solution)/shard_map/pallas_call | solution.py:309
  53.1 1.3 fusion
  54.4 1.2 add_bitcast_fusion.2
  55.7 2.7 %collective-permute-start.9 = (f32[288,512]{1,0:T(8,128)S(1)}, f32[288,512]{1,0:T(8,128)S(1)}, u32[]{:S(2)}, u32[]{:S(2)}) collective-permute-start(f32[288,512]{1,0:T(8,128)S(1)} %add_bitcast_fusion.1), channel_id=1, source_target_pairs={{0,12},{4,0},{8,4},{12,8},{64,76},{68,64},{72,68},{76,72},{16,28},... | collective-permute-start | bytes 1769480 | tf_op jit(solution)/shard_map/ppermute | solution.py:48
  58.4 1.8 %collective-permute-start.7 = (f32[288,512]{1,0:T(8,128)S(1)}, f32[288,512]{1,0:T(8,128)S(1)}, u32[]{:S(2)}, u32[]{:S(2)}) collective-permute-start(f32[288,512]{1,0:T(8,128)S(1)} %fusion), channel_id=1, source_target_pairs={{0,8},{4,12},{8,0},{12,4},{64,72},{68,76},{72,64},{76,68},{16,24},... | collective-permute-start | bytes 1769480 | tf_op jit(solution)/shard_map/ppermute | solution.py:48
  60.2 8.8 %shard_map.132 = bf16[1,2048,1024]{2,1,0:T(8,128)(2,1)} custom-call(bf16[1024,1024]{1,0:T(8,128)(2,1)} %get-tuple-element.73.refs_12_.dpre0, bf16[1024,1024]{1,0:T(8,128)(2,1)} %get-tuple-element.74.dpre1, bf16[1024,1024]{1,0:T(8,128)(2,1)} %w.5), custom_call_target="tpu_custom_call" | custom-call | flops 4294967296 | bytes 10485760 | tf_op jit(solution)/shard_map/pallas_call | solution.py:343
  69.0 2.5 %collective-permute-done.9 = f32[288,512]{1,0:T(8,128)S(1)} collective-permute-done((f32[288,512]{1,0:T(8,128)S(1)}, f32[288,512]{1,0:T(8,128)S(1)}, u32[]{:S(2)}, u32[]{:S(2)}) %collective-permute-start.9) | collective-permute-done | bytes 589856 | tf_op jit(solution)/shard_map/ppermute | solution.py:48
  71.5 3.4 %collective-permute-done.8 = f32[288,512]{1,0:T(8,128)S(1)} collective-permute-done((f32[288,512]{1,0:T(8,128)S(1)}, f32[288,512]{1,0:T(8,128)S(1)}, u32[]{:S(2)}, u32[]{:S(2)}) %collective-permute-start.8) | collective-permute-done | bytes 589856 | tf_op jit(solution)/shard_map/ppermute | solution.py:48
  75.2 1.5 %collective-permute-start.10 = (f32[72,512]{1,0:T(8,128)S(1)}, f32[72,512]{1,0:T(8,128)S(1)}, u32[]{:S(2)}, u32[]{:S(2)}) collective-permute-start(f32[72,512]{1,0:T(8,128)S(1)} %get-tuple-element.84), channel_id=1, source_target_pairs={{0,1},{4,5},{8,9},{12,13},{64,65},{68,69},{72,73},{76,77},{16,17},... | collective-permute-start | bytes 442376 | tf_op jit(solution)/shard_map/ppermute | solution.py:48
  76.7 2.2 %collective-permute-start.11 = (f32[72,512]{1,0:T(8,128)S(1)}, f32[72,512]{1,0:T(8,128)S(1)}, u32[]{:S(2)}, u32[]{:S(2)}) collective-permute-start(f32[72,512]{1,0:T(8,128)S(1)} %get-tuple-element.86), channel_id=1, source_target_pairs={{0,3},{4,7},{8,11},{12,15},{64,67},{68,71},{72,75},{76,79},{16,19}... | collective-permute-start | bytes 442376 | tf_op jit(solution)/shard_map/ppermute | solution.py:48
  78.9 1.2 collective-permute-start.12
  80.1 1.2 collective-permute-done.10
  81.3 3.0 %collective-permute-done.12 = f32[72,512]{1,0:T(8,128)S(1)} collective-permute-done((f32[72,512]{1,0:T(8,128)S(1)}, f32[72,512]{1,0:T(8,128)S(1)}, u32[]{:S(2)}, u32[]{:S(2)}) %collective-permute-start.12) | collective-permute-done | bytes 147488 | tf_op jit(solution)/shard_map/ppermute | solution.py:48
  84.4 1.3 %collective-permute-start.13 = (f32[72,512]{1,0:T(8,128)S(1)}, f32[72,512]{1,0:T(8,128)S(1)}, u32[]{:S(2)}, u32[]{:S(2)}) collective-permute-start(f32[72,512]{1,0:T(8,128)S(1)} %fusion.2), channel_id=1, source_target_pairs={{0,64},{4,68},{8,72},{12,76},{64,16},{68,20},{72,24},{76,28},{16,8... | collective-permute-start | bytes 442376 | tf_op jit(solution)/shard_map/ppermute | solution.py:48
  85.8 1.5 %collective-permute-start.14 = (f32[72,512]{1,0:T(8,128)S(1)}, f32[72,512]{1,0:T(8,128)S(1)}, u32[]{:S(2)}, u32[]{:S(2)}) collective-permute-start(f32[72,512]{1,0:T(8,128)S(1)} %fusion.2), channel_id=1, source_target_pairs={{0,80},{4,84},{8,88},{12,92},{64,0},{68,4},{72,8},{76,12},{16,64},... | collective-permute-start | bytes 442376 | tf_op jit(solution)/shard_map/ppermute | solution.py:48
  87.3 1.6 %collective-permute-start.15 = (f32[72,512]{1,0:T(8,128)S(1)}, f32[72,512]{1,0:T(8,128)S(1)}, u32[]{:S(2)}, u32[]{:S(2)}) collective-permute-start(f32[72,512]{1,0:T(8,128)S(1)} %fusion.2), channel_id=1, source_target_pairs={{0,16},{4,20},{8,24},{12,28},{64,80},{68,84},{72,88},{76,92},{16,0... | collective-permute-start | bytes 442376 | tf_op jit(solution)/shard_map/ppermute | solution.py:48
  88.8 0.9 collective-permute-done.13
  89.8 3.1 %collective-permute-done.15 = f32[72,512]{1,0:T(8,128)S(1)} collective-permute-done((f32[72,512]{1,0:T(8,128)S(1)}, f32[72,512]{1,0:T(8,128)S(1)}, u32[]{:S(2)}, u32[]{:S(2)}) %collective-permute-start.15) | collective-permute-done | bytes 147488 | tf_op jit(solution)/shard_map/ppermute | solution.py:48
  92.9 3.2 %collective-permute-start.16 = (f32[72,512]{1,0:T(8,128)S(1)}, f32[72,512]{1,0:T(8,128)S(1)}, u32[]{:S(2)}, u32[]{:S(2)}) collective-permute-start(f32[72,512]{1,0:T(8,128)S(1)} %add_add_fusion.1), channel_id=1, source_target_pairs={{0,3},{4,7},{8,11},{12,15},{64,67},{68,71},{72,75},{76,79},{16,19}... | collective-permute-start | bytes 442376 | tf_op jit(solution)/shard_map/ppermute | solution.py:48
  96.1 1.7 %collective-permute-start.17 = (f32[72,512]{1,0:T(8,128)S(1)}, f32[72,512]{1,0:T(8,128)S(1)}, u32[]{:S(2)}, u32[]{:S(2)}) collective-permute-start(f32[72,512]{1,0:T(8,128)S(1)} %add_add_fusion.1), channel_id=1, source_target_pairs={{0,2},{4,6},{8,10},{12,14},{64,66},{68,70},{72,74},{76,78},{16,18}... | collective-permute-start | bytes 442376 | tf_op jit(solution)/shard_map/ppermute | solution.py:48
  97.7 2.0 %collective-permute-done.16 = f32[72,512]{1,0:T(8,128)S(1)} collective-permute-done((f32[72,512]{1,0:T(8,128)S(1)}, f32[72,512]{1,0:T(8,128)S(1)}, u32[]{:S(2)}, u32[]{:S(2)}) %collective-permute-start.16) | collective-permute-done | bytes 147488 | tf_op jit(solution)/shard_map/ppermute | solution.py:48
  99.8 1.8 %collective-permute-done.17 = f32[72,512]{1,0:T(8,128)S(1)} collective-permute-done((f32[72,512]{1,0:T(8,128)S(1)}, f32[72,512]{1,0:T(8,128)S(1)}, u32[]{:S(2)}, u32[]{:S(2)}) %collective-permute-start.17) | collective-permute-done | bytes 147488 | tf_op jit(solution)/shard_map/ppermute | solution.py:48
  101.6 1.5 %collective-permute-done.18 = f32[72,512]{1,0:T(8,128)S(1)} collective-permute-done((f32[72,512]{1,0:T(8,128)S(1)}, f32[72,512]{1,0:T(8,128)S(1)}, u32[]{:S(2)}, u32[]{:S(2)}) %collective-permute-start.18) | collective-permute-done | bytes 147488 | tf_op jit(solution)/shard_map/ppermute | solution.py:48
  103.4 0.9 collective-permute-start.20
  104.3 1.8 %collective-permute-start.21 = (f32[288,512]{1,0:T(8,128)S(1)}, f32[288,512]{1,0:T(8,128)S(1)}, u32[]{:S(2)}, u32[]{:S(2)}) collective-permute-start(f32[288,512]{1,0:T(8,128)S(1)} %constant_dynamic-slice_fusion.refs_0_), channel_id=1, source_target_pairs={{0,12},{4,0},{8,4},{12,8},{64,76},{68,64},{72,68},{76,72},{16,28},... | collective-permute-start | bytes 1769480 | tf_op jit(solution)/shard_map/ppermute | solution.py:48
  106.1 5.0 %collective-permute-start.22 = (f32[288,512]{1,0:T(8,128)S(1)}, f32[288,512]{1,0:T(8,128)S(1)}, u32[]{:S(2)}, u32[]{:S(2)}) collective-permute-start(f32[288,512]{1,0:T(8,128)S(1)} %constant_dynamic-slice_fusion.refs_0_), channel_id=1, source_target_pairs={{0,32},{4,36},{8,40},{12,44},{64,96},{68,100},{72,104},{76,108},{1... | collective-permute-start | bytes 1769480 | tf_op jit(solution)/shard_map/ppermute | solution.py:48
  111.1 2.6 %collective-permute-done.19.refs_1_ = f32[288,512]{1,0:T(8,128)S(1)} collective-permute-done((f32[288,512]{1,0:T(8,128)S(1)}, f32[288,512]{1,0:T(8,128)S(1)}, u32[]{:S(2)}, u32[]{:S(2)}) %collective-permute-start.19) | collective-permute-done | bytes 589856 | tf_op jit(solution)/shard_map/ppermute | solution.py:48
  113.6 11.6 %collective-permute-start.23 = (f32[288,512]{1,0:T(8,128)S(1)}, f32[288,512]{1,0:T(8,128)S(1)}, u32[]{:S(2)}, u32[]{:S(2)}) collective-permute-start(f32[288,512]{1,0:T(8,128)S(1)} %collective-permute-done.19.refs_1_), channel_id=1, source_target_pairs={{0,32},{4,36},{8,40},{12,44},{64,96},{68,100},{72,104},{76,108},{1... | collective-permute-start | bytes 1769480 | tf_op jit(solution)/shard_map/ppermute | solution.py:48
  125.3 0.9 collective-permute-start.25
  126.1 0.7 collective-permute-done.23.refs_5_
  126.9 0.8 collective-permute-done.24.refs_6_
  127.7 0.8 collective-permute-done.25.refs_7_
  128.6 2.9 %shard_map.133 = (f32[1024,1024]{1,0:T(8,128)}, f32[100,1024]{1,0:T(8,128)}, f32[1,1024]{1,0:T(1,128)}, f32[1,100]{1,0:T(1,128)}, f32[1,1]{1,0:T(1,128)}) custom-call(s32[4]{0:T(128)S(1)} %copy-done, f32[288,512]{1,0:T(8,128)S(1)} %constant_dynamic-slice_fusion.refs_0_, f32[288,512]{1,0:T(8,128)S(1)} %collective-permute-done.19.refs_1_, ...), custom_call_target="tpu_custom_call" | custom-call | bytes 8388608 | tf_op jit(solution)/shard_map/pallas_call | solution.py:377
  (47 shorter events, 2.6 us)
Async XLA Ops:
  7.9 14.8 %copy-start.8 = (f32[100]{0:T(128)S(1)}, f32[100]{0:T(128)}, u32[]{:S(2)}) copy-start(f32[100]{0:T(128)} %param.11) | copy-start | bytes 1204
  7.9 11.5 %collective-permute-start = (f32[100,1024]{1,0:T(8,128)}, f32[100,1024]{1,0:T(8,128)S(1)}, u32[]{:S(2)}, u32[]{:S(2)}) collective-permute-start(f32[100,1024]{1,0:T(8,128)} %get-tuple-element.45.refs_0_), channel_id=1, source_target_pairs={{0,64},{4,68},{8,72},{12,76},{64,0},{68,4},{72,8},{76,12},{16,80},... | collective-permute-start | bytes 1228808 | tf_op jit(solution)/shard_map/ppermute | solution.py:48
  10.1 9.3 %collective-permute-start.1 = (f32[100,1024]{1,0:T(8,128)}, f32[100,1024]{1,0:T(8,128)S(1)}, u32[]{:S(2)}, u32[]{:S(2)}) collective-permute-start(f32[100,1024]{1,0:T(8,128)} %get-tuple-element.45.refs_0_), channel_id=1, source_target_pairs={{0,32},{4,36},{8,40},{12,44},{64,96},{68,100},{72,104},{76,108},{1... | collective-permute-start | bytes 1228808 | tf_op jit(solution)/shard_map/ppermute | solution.py:48
  18.2 2.0 %collective-permute-start.2 = (f32[100,1024]{1,0:T(8,128)}, f32[100,1024]{1,0:T(8,128)S(1)}, u32[]{:S(2)}, u32[]{:S(2)}) collective-permute-start(f32[100,1024]{1,0:T(8,128)} %get-tuple-element.46.refs_0_), channel_id=1, source_target_pairs={{0,32},{4,36},{8,40},{12,44},{64,96},{68,100},{72,104},{76,108},{1... | collective-permute-start | bytes 1228808 | tf_op jit(solution)/shard_map/ppermute | solution.py:48
  19.5 4.0 %copy-start.3 = (f32[100,1024]{1,0:T(8,128)}, f32[100,1024]{1,0:T(8,128)S(1)}, u32[]{:S(2)}) copy-start(f32[100,1024]{1,0:T(8,128)S(1)} %collective-permute-done.refs_2_) | copy-start | bytes 1228804
  19.5 4.0 %copy-start.4 = (f32[100,1024]{1,0:T(8,128)}, f32[100,1024]{1,0:T(8,128)S(1)}, u32[]{:S(2)}) copy-start(f32[100,1024]{1,0:T(8,128)S(1)} %collective-permute-done.1.refs_1_) | copy-start | bytes 1228804
  20.2 9.6 %copy-start.2 = (f32[100,1024]{1,0:T(8,128)}, f32[100,1024]{1,0:T(8,128)S(1)}, u32[]{:S(2)}) copy-start(f32[100,1024]{1,0:T(8,128)S(1)} %collective-permute-done.2.refs_1_) | copy-start | bytes 1228804
  20.2 3.2 %collective-permute-start.3 = (f32[100,1024]{1,0:T(8,128)S(1)}, f32[100,1024]{1,0:T(8,128)S(1)}, u32[]{:S(2)}, u32[]{:S(2)}) collective-permute-start(f32[100,1024]{1,0:T(8,128)S(1)} %collective-permute-done.refs_2_), channel_id=1, source_target_pairs={{0,32},{4,36},{8,40},{12,44},{64,96},{68,100},{72,104},{76,108},{1... | collective-permute-start | bytes 1228808 | tf_op jit(solution)/shard_map/ppermute | solution.py:48
  21.2 11.6 %collective-permute-start.4 = (f32[100,1024]{1,0:T(8,128)}, f32[100,1024]{1,0:T(8,128)S(1)}, u32[]{:S(2)}, u32[]{:S(2)}) collective-permute-start(f32[100,1024]{1,0:T(8,128)} %get-tuple-element.46.refs_0_), channel_id=1, source_target_pairs={{0,64},{4,68},{8,72},{12,76},{64,0},{68,4},{72,8},{76,12},{16,80},... | collective-permute-start | bytes 1228808 | tf_op jit(solution)/shard_map/ppermute | solution.py:48
  23.4 0.8 copy-start.6
  32.8 2.3 %copy-start.5 = (f32[100,1024]{1,0:T(8,128)}, f32[100,1024]{1,0:T(8,128)S(1)}, u32[]{:S(2)}) copy-start(f32[100,1024]{1,0:T(8,128)S(1)} %collective-permute-done.4.refs_2_) | copy-start | bytes 1228804
  32.8 2.3 %collective-permute-start.5 = (f32[100,1024]{1,0:T(8,128)S(1)}, f32[100,1024]{1,0:T(8,128)S(1)}, u32[]{:S(2)}, u32[]{:S(2)}) collective-permute-start(f32[100,1024]{1,0:T(8,128)S(1)} %collective-permute-done.4.refs_2_), channel_id=1, source_target_pairs={{0,32},{4,36},{8,40},{12,44},{64,96},{68,100},{72,104},{76,108},{1... | collective-permute-start | bytes 1228808 | tf_op jit(solution)/shard_map/ppermute | solution.py:48
  35.1 0.8 copy-start.7
  45.9 7.1 %collective-permute-start.6 = (f32[4,288,512]{2,1,0:T(8,128)}, f32[4,288,512]{2,1,0:T(8,128)S(1)}, u32[]{:S(2)}, u32[]{:S(2)}) collective-permute-start(f32[4,288,512]{2,1,0:T(8,128)} %get-tuple-element.61), channel_id=1, source_target_pairs={{0,32},{4,36},{8,40},{12,44},{64,96},{68,100},{72,104},{76,108},{1... | collective-permute-start | bytes 7077896 | tf_op jit(solution)/shard_map/ppermute | solution.py:48
  53.1 2.5 %copy-start.1 = (f32[4,288,512]{2,1,0:T(8,128)S(1)}, f32[4,288,512]{2,1,0:T(8,128)}, u32[]{:S(2)}) copy-start(f32[4,288,512]{2,1,0:T(8,128)} %shard_map.131) | copy-start | bytes 7077892
  55.7 15.8 %collective-permute-start.9 = (f32[288,512]{1,0:T(8,128)S(1)}, f32[288,512]{1,0:T(8,128)S(1)}, u32[]{:S(2)}, u32[]{:S(2)}) collective-permute-start(f32[288,512]{1,0:T(8,128)S(1)} %add_bitcast_fusion.1), channel_id=1, source_target_pairs={{0,12},{4,0},{8,4},{12,8},{64,76},{68,64},{72,68},{76,72},{16,28},... | collective-permute-start | bytes 1769480 | tf_op jit(solution)/shard_map/ppermute | solution.py:48
  58.4 16.6 %collective-permute-start.8 = (f32[288,512]{1,0:T(8,128)S(1)}, f32[288,512]{1,0:T(8,128)S(1)}, u32[]{:S(2)}, u32[]{:S(2)}) collective-permute-start(f32[288,512]{1,0:T(8,128)S(1)} %add_bitcast_fusion.2), channel_id=1, source_target_pairs={{0,4},{4,8},{8,12},{12,0},{64,68},{68,72},{72,76},{76,64},{16,20},... | collective-permute-start | bytes 1769480 | tf_op jit(solution)/shard_map/ppermute | solution.py:48
  58.4 16.6 %collective-permute-start.7 = (f32[288,512]{1,0:T(8,128)S(1)}, f32[288,512]{1,0:T(8,128)S(1)}, u32[]{:S(2)}, u32[]{:S(2)}) collective-permute-start(f32[288,512]{1,0:T(8,128)S(1)} %fusion), channel_id=1, source_target_pairs={{0,8},{4,12},{8,0},{12,4},{64,72},{68,76},{72,64},{76,68},{16,24},... | collective-permute-start | bytes 1769480 | tf_op jit(solution)/shard_map/ppermute | solution.py:48
  75.2 6.1 %collective-permute-start.10 = (f32[72,512]{1,0:T(8,128)S(1)}, f32[72,512]{1,0:T(8,128)S(1)}, u32[]{:S(2)}, u32[]{:S(2)}) collective-permute-start(f32[72,512]{1,0:T(8,128)S(1)} %get-tuple-element.84), channel_id=1, source_target_pairs={{0,1},{4,5},{8,9},{12,13},{64,65},{68,69},{72,73},{76,77},{16,17},... | collective-permute-start | bytes 442376 | tf_op jit(solution)/shard_map/ppermute | solution.py:48
  76.7 4.7 %collective-permute-start.11 = (f32[72,512]{1,0:T(8,128)S(1)}, f32[72,512]{1,0:T(8,128)S(1)}, u32[]{:S(2)}, u32[]{:S(2)}) collective-permute-start(f32[72,512]{1,0:T(8,128)S(1)} %get-tuple-element.86), channel_id=1, source_target_pairs={{0,3},{4,7},{8,11},{12,15},{64,67},{68,71},{72,75},{76,79},{16,19}... | collective-permute-start | bytes 442376 | tf_op jit(solution)/shard_map/ppermute | solution.py:48
  78.9 5.5 %collective-permute-start.12 = (f32[72,512]{1,0:T(8,128)S(1)}, f32[72,512]{1,0:T(8,128)S(1)}, u32[]{:S(2)}, u32[]{:S(2)}) collective-permute-start(f32[72,512]{1,0:T(8,128)S(1)} %get-tuple-element.85), channel_id=1, source_target_pairs={{0,2},{4,6},{8,10},{12,14},{64,66},{68,70},{72,74},{76,78},{16,18}... | collective-permute-start | bytes 442376 | tf_op jit(solution)/shard_map/ppermute | solution.py:48
  80.1 48.5 %copy-start = (s32[4]{0:T(128)S(1)}, s32[4]{0:T(128)}, u32[]{:S(2)}) copy-start(s32[4]{0:T(128)} %pad_add_fusion.where) | copy-start | bytes 52
  84.4 5.3 %collective-permute-start.13 = (f32[72,512]{1,0:T(8,128)S(1)}, f32[72,512]{1,0:T(8,128)S(1)}, u32[]{:S(2)}, u32[]{:S(2)}) collective-permute-start(f32[72,512]{1,0:T(8,128)S(1)} %fusion.2), channel_id=1, source_target_pairs={{0,64},{4,68},{8,72},{12,76},{64,16},{68,20},{72,24},{76,28},{16,8... | collective-permute-start | bytes 442376 | tf_op jit(solution)/shard_map/ppermute | solution.py:48
  85.8 4.0 %collective-permute-start.14 = (f32[72,512]{1,0:T(8,128)S(1)}, f32[72,512]{1,0:T(8,128)S(1)}, u32[]{:S(2)}, u32[]{:S(2)}) collective-permute-start(f32[72,512]{1,0:T(8,128)S(1)} %fusion.2), channel_id=1, source_target_pairs={{0,80},{4,84},{8,88},{12,92},{64,0},{68,4},{72,8},{76,12},{16,64},... | collective-permute-start | bytes 442376 | tf_op jit(solution)/shard_map/ppermute | solution.py:48
  87.3 5.6 %collective-permute-start.15 = (f32[72,512]{1,0:T(8,128)S(1)}, f32[72,512]{1,0:T(8,128)S(1)}, u32[]{:S(2)}, u32[]{:S(2)}) collective-permute-start(f32[72,512]{1,0:T(8,128)S(1)} %fusion.2), channel_id=1, source_target_pairs={{0,16},{4,20},{8,24},{12,28},{64,80},{68,84},{72,88},{76,92},{16,0... | collective-permute-start | bytes 442376 | tf_op jit(solution)/shard_map/ppermute | solution.py:48
  92.9 6.9 %collective-permute-start.16 = (f32[72,512]{1,0:T(8,128)S(1)}, f32[72,512]{1,0:T(8,128)S(1)}, u32[]{:S(2)}, u32[]{:S(2)}) collective-permute-start(f32[72,512]{1,0:T(8,128)S(1)} %add_add_fusion.1), channel_id=1, source_target_pairs={{0,3},{4,7},{8,11},{12,15},{64,67},{68,71},{72,75},{76,79},{16,19}... | collective-permute-start | bytes 442376 | tf_op jit(solution)/shard_map/ppermute | solution.py:48
  96.1 5.5 %collective-permute-start.17 = (f32[72,512]{1,0:T(8,128)S(1)}, f32[72,512]{1,0:T(8,128)S(1)}, u32[]{:S(2)}, u32[]{:S(2)}) collective-permute-start(f32[72,512]{1,0:T(8,128)S(1)} %add_add_fusion.1), channel_id=1, source_target_pairs={{0,2},{4,6},{8,10},{12,14},{64,66},{68,70},{72,74},{76,78},{16,18}... | collective-permute-start | bytes 442376 | tf_op jit(solution)/shard_map/ppermute | solution.py:48
  97.7 5.4 %collective-permute-start.18 = (f32[72,512]{1,0:T(8,128)S(1)}, f32[72,512]{1,0:T(8,128)S(1)}, u32[]{:S(2)}, u32[]{:S(2)}) collective-permute-start(f32[72,512]{1,0:T(8,128)S(1)} %add_add_fusion.1), channel_id=1, source_target_pairs={{0,1},{4,5},{8,9},{12,13},{64,65},{68,69},{72,73},{76,77},{16,17},... | collective-permute-start | bytes 442376 | tf_op jit(solution)/shard_map/ppermute | solution.py:48
  103.3 10.3 %collective-permute-start.19 = (f32[288,512]{1,0:T(8,128)S(1)}, f32[288,512]{1,0:T(8,128)S(1)}, u32[]{:S(2)}, u32[]{:S(2)}) collective-permute-start(f32[288,512]{1,0:T(8,128)S(1)} %constant_dynamic-slice_fusion.refs_0_), channel_id=1, source_target_pairs={{0,4},{4,8},{8,12},{12,0},{64,68},{68,72},{72,76},{76,64},{16,20},... | collective-permute-start | bytes 1769480 | tf_op jit(solution)/shard_map/ppermute | solution.py:48
  103.4 21.8 %collective-permute-start.20 = (f32[288,512]{1,0:T(8,128)S(1)}, f32[288,512]{1,0:T(8,128)S(1)}, u32[]{:S(2)}, u32[]{:S(2)}) collective-permute-start(f32[288,512]{1,0:T(8,128)S(1)} %constant_dynamic-slice_fusion.refs_0_), channel_id=1, source_target_pairs={{0,8},{4,12},{8,0},{12,4},{64,72},{68,76},{72,64},{76,68},{16,24},... | collective-permute-start | bytes 1769480 | tf_op jit(solution)/shard_map/ppermute | solution.py:48
  104.3 20.9 %collective-permute-start.21 = (f32[288,512]{1,0:T(8,128)S(1)}, f32[288,512]{1,0:T(8,128)S(1)}, u32[]{:S(2)}, u32[]{:S(2)}) collective-permute-start(f32[288,512]{1,0:T(8,128)S(1)} %constant_dynamic-slice_fusion.refs_0_), channel_id=1, source_target_pairs={{0,12},{4,0},{8,4},{12,8},{64,76},{68,64},{72,68},{76,72},{16,28},... | collective-permute-start | bytes 1769480 | tf_op jit(solution)/shard_map/ppermute | solution.py:48
  106.1 20.1 %collective-permute-start.22 = (f32[288,512]{1,0:T(8,128)S(1)}, f32[288,512]{1,0:T(8,128)S(1)}, u32[]{:S(2)}, u32[]{:S(2)}) collective-permute-start(f32[288,512]{1,0:T(8,128)S(1)} %constant_dynamic-slice_fusion.refs_0_), channel_id=1, source_target_pairs={{0,32},{4,36},{8,40},{12,44},{64,96},{68,100},{72,104},{76,108},{1... | collective-permute-start | bytes 1769480 | tf_op jit(solution)/shard_map/ppermute | solution.py:48
  113.6 13.2 %collective-permute-start.23 = (f32[288,512]{1,0:T(8,128)S(1)}, f32[288,512]{1,0:T(8,128)S(1)}, u32[]{:S(2)}, u32[]{:S(2)}) collective-permute-start(f32[288,512]{1,0:T(8,128)S(1)} %collective-permute-done.19.refs_1_), channel_id=1, source_target_pairs={{0,32},{4,36},{8,40},{12,44},{64,96},{68,100},{72,104},{76,108},{1... | collective-permute-start | bytes 1769480 | tf_op jit(solution)/shard_map/ppermute | solution.py:48
  125.2 2.5 %collective-permute-start.24 = (f32[288,512]{1,0:T(8,128)S(1)}, f32[288,512]{1,0:T(8,128)S(1)}, u32[]{:S(2)}, u32[]{:S(2)}) collective-permute-start(f32[288,512]{1,0:T(8,128)S(1)} %collective-permute-done.20.refs_2_), channel_id=1, source_target_pairs={{0,32},{4,36},{8,40},{12,44},{64,96},{68,100},{72,104},{76,108},{1... | collective-permute-start | bytes 1769480 | tf_op jit(solution)/shard_map/ppermute | solution.py:48
  125.3 3.3 %collective-permute-start.25 = (f32[288,512]{1,0:T(8,128)S(1)}, f32[288,512]{1,0:T(8,128)S(1)}, u32[]{:S(2)}, u32[]{:S(2)}) collective-permute-start(f32[288,512]{1,0:T(8,128)S(1)} %collective-permute-done.21.refs_3_), channel_id=1, source_target_pairs={{0,32},{4,36},{8,40},{12,44},{64,96},{68,100},{72,104},{76,108},{1... | collective-permute-start | bytes 1769480 | tf_op jit(solution)/shard_map/ppermute | solution.py:48

commit v7 on v6

--- a/solution.py
+++ b/solution.py
@@ -291,7 +291,7 @@
             jax.ShapeDtypeStruct((128, width), F32),
             jax.ShapeDtypeStruct((4, block + 32, half), F32),
         ],
-        compiler_params=params(),
+        compiler_params=params(52),
         cost_estimate=cost(2 * points * half * depth, points * 2 * depth + n * (n_vars * 20 + 8 * width) + 4 * depth * half),
     )(where, own, *others, target, area, var, sp, hid, w_output, rest, latent, dpre0)
 

time: 132 us -> 130 us (0.985)
  waiting for transfers between devices: 30.3 us -> 37.2 us
  starting transfers between devices: 45.8 us -> 39.3 us
    ppermute x26, waiting for transfers between devices: 30.3 us -> 37.2 us  [send(): return lax.ppermute(array, ALL, pairs)]
    ppermute x26, starting transfers between devices: 45.8 us -> 39.3 us  [send(): return lax.ppermute(array, ALL, pairs)]
  transfers between devices with their start and end apart: 26 -> 26, of which waited for: 17 -> 17; matrix products, arithmetic and copies ran while one was open for 1% -> 1% of each run, Pallas kernels for 21% -> 22%
where the time goes in v7:
time: 130 us
  Pallas kernels  47.6 us (37%)
  starting transfers between devices  39.3 us (30%)
  waiting for transfers between devices  37.2 us (29%)
  other arithmetic  3.07 us (2%)
  local copies, waits for them, and re-layouts  1.74 us (1%)
    ppermute x26, starting transfers between devices, send(): return lax.ppermute(array, ALL, pairs)  39.3 us
    ppermute x26, waiting for transfers between devices, send(): return lax.ppermute(array, ALL, pairs)  37.2 us
    pallas_call x2, Pallas kernels, forward(): pl.pallas_call(forward_kernel, grid=(steps,), in_specs=[pl.BlockSpec((til...  14.4 us
    pallas_call x1, Pallas kernels, cotangent_weight(): pl.pallas_call(functools.partial(cot_weight_kernel, numbers, steps, which...  9.14 us
    pallas_call x1, Pallas kernels, latent_gradient(): pl.pallas_call(functools.partial(latent_kernel, steps), grid=(2 * steps,)...  8.76 us
    pallas_call x1, Pallas kernels, weight_grad(): pl.pallas_call(functools.partial(weight_kernel, scale, which), grid_spec=...  6.65 us
    pallas_call x1, Pallas kernels, cotangent(): pl.pallas_call(functools.partial(cot_kernel, numbers), grid=(steps,), in_...  5.8 us
    pallas_call x1, Pallas kernels, join(): pl.pallas_call(functools.partial(join_kernel, n_vars), in_specs=[pl.Block...  2.9 us
  transfers between devices with their start and end apart: 26, of which 17 were waited for; matrix products, arithmetic and copies ran while one was open for 1% of the time, Pallas kernels for 22%

profile of v7, /device:TPU:1, one launch (start us, length us, event | category | flops | bytes accessed | tf_op | source)
XLA Modules:
  0.0 129.7 jit_solution(2232816551487830930)
XLA Ops:
  0.6 7.3 %shard_map.127 = (f32[100,1024]{1,0:T(8,128)}, bf16[1024,1024]{1,0:T(8,128)(2,1)}, f32[1024,1024]{1,0:T(8,128)}) custom-call(bf16[2048,1024]{1,0:T(8,128)(2,1)} %bitcast.35, bf16[1024,1024]{1,0:T(8,128)(2,1)} %w.5, f32[1,1024]{1,0:T(1,128)} %bitcast.43, bf16[100,1024]{1,0:T(8,128)(2,1)} %refs_9_.3, f32[1,100]{1,0:T(1,128)} %bitcast.46), custom_call_target="tpu_custom_call" | custom-call | flops 2357198848 | bytes 10485760 | tf_op jit(solution)/shard_map/pallas_call | solution.py:104
  7.9 2.2 %collective-permute-start = (f32[100,1024]{1,0:T(8,128)}, f32[100,1024]{1,0:T(8,128)S(1)}, u32[]{:S(2)}, u32[]{:S(2)}) collective-permute-start(f32[100,1024]{1,0:T(8,128)} %get-tuple-element.45.refs_0_), channel_id=1, source_target_pairs={{0,64},{4,68},{8,72},{12,76},{64,0},{68,4},{72,8},{76,12},{16,80},... | collective-permute-start | bytes 1228808 | tf_op jit(solution)/shard_map/ppermute | solution.py:48
  10.1 1.0 collective-permute-start.1
  11.1 7.2 %shard_map.128 = (f32[100,1024]{1,0:T(8,128)}, bf16[1024,1024]{1,0:T(8,128)(2,1)}, f32[1024,1024]{1,0:T(8,128)}) custom-call(bf16[2048,1024]{1,0:T(8,128)(2,1)} %bitcast.36, bf16[1024,1024]{1,0:T(8,128)(2,1)} %w.5, f32[1,1024]{1,0:T(1,128)} %bitcast.44, bf16[100,1024]{1,0:T(8,128)(2,1)} %refs_9_.3, f32[1,100]{1,0:T(1,128)} %bitcast.47), custom_call_target="tpu_custom_call" | custom-call | flops 2357198848 | bytes 10485760 | tf_op jit(solution)/shard_map/pallas_call | solution.py:104
  18.3 1.1 collective-permute-done.refs_2_
  19.4 0.8 collective-permute-done.2.refs_1_
  20.2 1.0 collective-permute-start.3
  21.2 1.5 %collective-permute-start.4 = (f32[100,1024]{1,0:T(8,128)}, f32[100,1024]{1,0:T(8,128)S(1)}, u32[]{:S(2)}, u32[]{:S(2)}) collective-permute-start(f32[100,1024]{1,0:T(8,128)} %get-tuple-element.46.refs_0_), channel_id=1, source_target_pairs={{0,64},{4,68},{8,72},{12,76},{64,0},{68,4},{72,8},{76,12},{16,80},... | collective-permute-start | bytes 1228808 | tf_op jit(solution)/shard_map/ppermute | solution.py:48
  22.7 0.7 copy.14.refs_6_
  23.4 0.8 copy-done.9
  24.2 5.8 %shard_map.129 = (bf16[1024,1024]{1,0:T(8,128)(2,1)}, f32[128,1024]{1,0:T(8,128)}) custom-call(f32[100,1024]{1,0:T(8,128)} %get-tuple-element.45.refs_0_, f32[100,1024]{1,0:T(8,128)} %copy-done.8, f32[100,1024]{1,0:T(8,128)} %copy-done.7, f32[100,1024]{1,0:T(8,128)} %copy-done.9, f32[100,2048]{1,0:T(8,128)} %refs_4_.3, f32[1,2048]{1,0:T(1,128)} %bitcast.33, ...), custom_call_target="tpu_custom_call" | custom-call | flops 1 | bytes 1 | tf_op jit(solution)/shard_map/pallas_call | solution.py:230
  30.0 2.8 %collective-permute-done.4.refs_2_ = f32[100,1024]{1,0:T(8,128)S(1)} collective-permute-done((f32[100,1024]{1,0:T(8,128)}, f32[100,1024]{1,0:T(8,128)S(1)}, u32[]{:S(2)}, u32[]{:S(2)}) %collective-permute-start.4) | collective-permute-done | bytes 409632 | tf_op jit(solution)/shard_map/ppermute | solution.py:48
  32.8 0.9 collective-permute-start.5
  33.6 1.4 %collective-permute-done.5.refs_3_ = f32[100,1024]{1,0:T(8,128)S(1)} collective-permute-done((f32[100,1024]{1,0:T(8,128)S(1)}, f32[100,1024]{1,0:T(8,128)S(1)}, u32[]{:S(2)}, u32[]{:S(2)}) %collective-permute-start.5) | collective-permute-done | bytes 409632 | tf_op jit(solution)/shard_map/ppermute | solution.py:48
  35.1 9.1 %shard_map.130 = (bf16[1024,1024]{1,0:T(8,128)(2,1)}, f32[128,1024]{1,0:T(8,128)}, f32[4,288,512]{2,1,0:T(8,128)}) custom-call(s32[4]{0:T(128)S(1)} %pad_add_fusion.where, f32[100,1024]{1,0:T(8,128)S(1)} %copy-done.2, f32[100,1024]{1,0:T(8,128)S(1)} %collective-permute-done.2.refs_1_, f32[100,1024]{1,0:T(8,128)S(1)} %collective-permute-done.4.refs_2_, ...), custom_call_target="tpu_custom_call" | custom-call | flops 2147483648 | bytes 16728064 | tf_op jit(solution)/shard_map/pallas_call | solution.py:264
  44.7 6.7 %shard_map.131 = f32[4,288,512]{2,1,0:T(8,128)} custom-call(s32[4]{0:T(128)} %copy-done.4, bf16[2048,1024]{1,0:T(8,128)(2,1)} %bitcast.38, bf16[2048,1024]{1,0:T(8,128)(2,1)} %bitcast.39, bf16[1024,1024]{1,0:T(8,128)(2,1)} %get-tuple-element.73.refs_12_.dpre0, bf16[1024,1024]{1,0:T(8,128)(2,1)} %get-tuple-element.74.dpre1, f32[128,1024]{1,0:T(8,128)} %get-tuple-element.60.rest), custom_call_target="tpu_custom_call" | custom-call | flops 2147483648 | bytes 8388608 | tf_op jit(solution)/shard_map/pallas_call | solution.py:309
  51.4 1.3 %fusion = f32[288,512]{1,0:T(8,128)S(1)} fusion(f32[4,288,512]{2,1,0:T(8,128)S(1)} %collective-permute-done.6, f32[4,288,512]{2,1,0:T(8,128)} %shard_map.131), kind=kLoop, calls=%fused_computation.1 | loop fusion | flops 147456 | bytes 1769472 | tf_op jit(solution)/shard_map/add | solution.py:57
  52.7 1.2 add_bitcast_fusion.2
  53.9 2.7 %collective-permute-start.9 = (f32[288,512]{1,0:T(8,128)S(1)}, f32[288,512]{1,0:T(8,128)S(1)}, u32[]{:S(2)}, u32[]{:S(2)}) collective-permute-start(f32[288,512]{1,0:T(8,128)S(1)} %add_bitcast_fusion.1), channel_id=1, source_target_pairs={{0,12},{4,0},{8,4},{12,8},{64,76},{68,64},{72,68},{76,72},{16,28},... | collective-permute-start | bytes 1769480 | tf_op jit(solution)/shard_map/ppermute | solution.py:48
  56.7 1.7 %collective-permute-start.7 = (f32[288,512]{1,0:T(8,128)S(1)}, f32[288,512]{1,0:T(8,128)S(1)}, u32[]{:S(2)}, u32[]{:S(2)}) collective-permute-start(f32[288,512]{1,0:T(8,128)S(1)} %fusion), channel_id=1, source_target_pairs={{0,8},{4,12},{8,0},{12,4},{64,72},{68,76},{72,64},{76,68},{16,24},... | collective-permute-start | bytes 1769480 | tf_op jit(solution)/shard_map/ppermute | solution.py:48
  58.5 8.8 %shard_map.132 = bf16[1,2048,1024]{2,1,0:T(8,128)(2,1)} custom-call(bf16[1024,1024]{1,0:T(8,128)(2,1)} %get-tuple-element.73.refs_12_.dpre0, bf16[1024,1024]{1,0:T(8,128)(2,1)} %get-tuple-element.74.dpre1, bf16[1024,1024]{1,0:T(8,128)(2,1)} %w.5), custom_call_target="tpu_custom_call" | custom-call | flops 4294967296 | bytes 10485760 | tf_op jit(solution)/shard_map/pallas_call | solution.py:343
  67.2 2.6 %collective-permute-done.9 = f32[288,512]{1,0:T(8,128)S(1)} collective-permute-done((f32[288,512]{1,0:T(8,128)S(1)}, f32[288,512]{1,0:T(8,128)S(1)}, u32[]{:S(2)}, u32[]{:S(2)}) %collective-permute-start.9) | collective-permute-done | bytes 589856 | tf_op jit(solution)/shard_map/ppermute | solution.py:48
  69.8 3.4 %collective-permute-done.8 = f32[288,512]{1,0:T(8,128)S(1)} collective-permute-done((f32[288,512]{1,0:T(8,128)S(1)}, f32[288,512]{1,0:T(8,128)S(1)}, u32[]{:S(2)}, u32[]{:S(2)}) %collective-permute-start.8) | collective-permute-done | bytes 589856 | tf_op jit(solution)/shard_map/ppermute | solution.py:48
  73.5 1.4 %collective-permute-start.10 = (f32[72,512]{1,0:T(8,128)S(1)}, f32[72,512]{1,0:T(8,128)S(1)}, u32[]{:S(2)}, u32[]{:S(2)}) collective-permute-start(f32[72,512]{1,0:T(8,128)S(1)} %get-tuple-element.84), channel_id=1, source_target_pairs={{0,1},{4,5},{8,9},{12,13},{64,65},{68,69},{72,73},{76,77},{16,17},... | collective-permute-start | bytes 442376 | tf_op jit(solution)/shard_map/ppermute | solution.py:48
  74.9 2.2 %collective-permute-start.11 = (f32[72,512]{1,0:T(8,128)S(1)}, f32[72,512]{1,0:T(8,128)S(1)}, u32[]{:S(2)}, u32[]{:S(2)}) collective-permute-start(f32[72,512]{1,0:T(8,128)S(1)} %get-tuple-element.86), channel_id=1, source_target_pairs={{0,3},{4,7},{8,11},{12,15},{64,67},{68,71},{72,75},{76,79},{16,19}... | collective-permute-start | bytes 442376 | tf_op jit(solution)/shard_map/ppermute | solution.py:48
  77.2 1.2 collective-permute-start.12
  78.4 1.2 collective-permute-done.10
  79.6 3.0 %collective-permute-done.12 = f32[72,512]{1,0:T(8,128)S(1)} collective-permute-done((f32[72,512]{1,0:T(8,128)S(1)}, f32[72,512]{1,0:T(8,128)S(1)}, u32[]{:S(2)}, u32[]{:S(2)}) %collective-permute-start.12) | collective-permute-done | bytes 147488 | tf_op jit(solution)/shard_map/ppermute | solution.py:48
  82.7 1.4 %collective-permute-start.13 = (f32[72,512]{1,0:T(8,128)S(1)}, f32[72,512]{1,0:T(8,128)S(1)}, u32[]{:S(2)}, u32[]{:S(2)}) collective-permute-start(f32[72,512]{1,0:T(8,128)S(1)} %fusion.2), channel_id=1, source_target_pairs={{0,64},{4,68},{8,72},{12,76},{64,16},{68,20},{72,24},{76,28},{16,8... | collective-permute-start | bytes 442376 | tf_op jit(solution)/shard_map/ppermute | solution.py:48
  84.1 1.5 %collective-permute-start.14 = (f32[72,512]{1,0:T(8,128)S(1)}, f32[72,512]{1,0:T(8,128)S(1)}, u32[]{:S(2)}, u32[]{:S(2)}) collective-permute-start(f32[72,512]{1,0:T(8,128)S(1)} %fusion.2), channel_id=1, source_target_pairs={{0,80},{4,84},{8,88},{12,92},{64,0},{68,4},{72,8},{76,12},{16,64},... | collective-permute-start | bytes 442376 | tf_op jit(solution)/shard_map/ppermute | solution.py:48
  85.6 1.6 %collective-permute-start.15 = (f32[72,512]{1,0:T(8,128)S(1)}, f32[72,512]{1,0:T(8,128)S(1)}, u32[]{:S(2)}, u32[]{:S(2)}) collective-permute-start(f32[72,512]{1,0:T(8,128)S(1)} %fusion.2), channel_id=1, source_target_pairs={{0,16},{4,20},{8,24},{12,28},{64,80},{68,84},{72,88},{76,92},{16,0... | collective-permute-start | bytes 442376 | tf_op jit(solution)/shard_map/ppermute | solution.py:48
  87.1 0.9 collective-permute-done.13
  88.1 3.1 %collective-permute-done.15 = f32[72,512]{1,0:T(8,128)S(1)} collective-permute-done((f32[72,512]{1,0:T(8,128)S(1)}, f32[72,512]{1,0:T(8,128)S(1)}, u32[]{:S(2)}, u32[]{:S(2)}) %collective-permute-start.15) | collective-permute-done | bytes 147488 | tf_op jit(solution)/shard_map/ppermute | solution.py:48
  91.2 3.2 %collective-permute-start.16 = (f32[72,512]{1,0:T(8,128)S(1)}, f32[72,512]{1,0:T(8,128)S(1)}, u32[]{:S(2)}, u32[]{:S(2)}) collective-permute-start(f32[72,512]{1,0:T(8,128)S(1)} %add_add_fusion.1), channel_id=1, source_target_pairs={{0,3},{4,7},{8,11},{12,15},{64,67},{68,71},{72,75},{76,79},{16,19}... | collective-permute-start | bytes 442376 | tf_op jit(solution)/shard_map/ppermute | solution.py:48
  94.4 1.5 %collective-permute-start.17 = (f32[72,512]{1,0:T(8,128)S(1)}, f32[72,512]{1,0:T(8,128)S(1)}, u32[]{:S(2)}, u32[]{:S(2)}) collective-permute-start(f32[72,512]{1,0:T(8,128)S(1)} %add_add_fusion.1), channel_id=1, source_target_pairs={{0,2},{4,6},{8,10},{12,14},{64,66},{68,70},{72,74},{76,78},{16,18}... | collective-permute-start | bytes 442376 | tf_op jit(solution)/shard_map/ppermute | solution.py:48
  96.0 2.1 %collective-permute-done.16 = f32[72,512]{1,0:T(8,128)S(1)} collective-permute-done((f32[72,512]{1,0:T(8,128)S(1)}, f32[72,512]{1,0:T(8,128)S(1)}, u32[]{:S(2)}, u32[]{:S(2)}) %collective-permute-start.16) | collective-permute-done | bytes 147488 | tf_op jit(solution)/shard_map/ppermute | solution.py:48
  98.1 1.8 %collective-permute-done.17 = f32[72,512]{1,0:T(8,128)S(1)} collective-permute-done((f32[72,512]{1,0:T(8,128)S(1)}, f32[72,512]{1,0:T(8,128)S(1)}, u32[]{:S(2)}, u32[]{:S(2)}) %collective-permute-start.17) | collective-permute-done | bytes 147488 | tf_op jit(solution)/shard_map/ppermute | solution.py:48
  100.0 1.5 %collective-permute-done.18 = f32[72,512]{1,0:T(8,128)S(1)} collective-permute-done((f32[72,512]{1,0:T(8,128)S(1)}, f32[72,512]{1,0:T(8,128)S(1)}, u32[]{:S(2)}, u32[]{:S(2)}) %collective-permute-start.18) | collective-permute-done | bytes 147488 | tf_op jit(solution)/shard_map/ppermute | solution.py:48
  101.8 0.9 collective-permute-start.20
  102.6 1.8 %collective-permute-start.21 = (f32[288,512]{1,0:T(8,128)S(1)}, f32[288,512]{1,0:T(8,128)S(1)}, u32[]{:S(2)}, u32[]{:S(2)}) collective-permute-start(f32[288,512]{1,0:T(8,128)S(1)} %constant_dynamic-slice_fusion.refs_0_), channel_id=1, source_target_pairs={{0,12},{4,0},{8,4},{12,8},{64,76},{68,64},{72,68},{76,72},{16,28},... | collective-permute-start | bytes 1769480 | tf_op jit(solution)/shard_map/ppermute | solution.py:48
  104.4 4.9 %collective-permute-start.22 = (f32[288,512]{1,0:T(8,128)S(1)}, f32[288,512]{1,0:T(8,128)S(1)}, u32[]{:S(2)}, u32[]{:S(2)}) collective-permute-start(f32[288,512]{1,0:T(8,128)S(1)} %constant_dynamic-slice_fusion.refs_0_), channel_id=1, source_target_pairs={{0,32},{4,36},{8,40},{12,44},{64,96},{68,100},{72,104},{76,108},{1... | collective-permute-start | bytes 1769480 | tf_op jit(solution)/shard_map/ppermute | solution.py:48
  109.3 9.0 %collective-permute-done.19.refs_1_ = f32[288,512]{1,0:T(8,128)S(1)} collective-permute-done((f32[288,512]{1,0:T(8,128)S(1)}, f32[288,512]{1,0:T(8,128)S(1)}, u32[]{:S(2)}, u32[]{:S(2)}) %collective-permute-start.19) | collective-permute-done | bytes 589856 | tf_op jit(solution)/shard_map/ppermute | solution.py:48
  118.3 5.2 %collective-permute-start.23 = (f32[288,512]{1,0:T(8,128)S(1)}, f32[288,512]{1,0:T(8,128)S(1)}, u32[]{:S(2)}, u32[]{:S(2)}) collective-permute-start(f32[288,512]{1,0:T(8,128)S(1)} %collective-permute-done.19.refs_1_), channel_id=1, source_target_pairs={{0,32},{4,36},{8,40},{12,44},{64,96},{68,100},{72,104},{76,108},{1... | collective-permute-start | bytes 1769480 | tf_op jit(solution)/shard_map/ppermute | solution.py:48
  123.5 0.9 collective-permute-start.25
  124.4 0.7 collective-permute-done.23.refs_5_
  125.1 0.8 collective-permute-done.24.refs_6_
  126.0 0.8 collective-permute-done.25.refs_7_
  126.8 2.9 %shard_map.133 = (f32[1024,1024]{1,0:T(8,128)}, f32[100,1024]{1,0:T(8,128)}, f32[1,1024]{1,0:T(1,128)}, f32[1,100]{1,0:T(1,128)}, f32[1,1]{1,0:T(1,128)}) custom-call(s32[4]{0:T(128)S(1)} %copy-done.5, f32[288,512]{1,0:T(8,128)S(1)} %constant_dynamic-slice_fusion.refs_0_, f32[288,512]{1,0:T(8,128)S(1)} %collective-permute-done.19.refs_1_, ...), custom_call_target="tpu_custom_call" | custom-call | bytes 8388608 | tf_op jit(solution)/shard_map/pallas_call | solution.py:377
  (51 shorter events, 1.5 us)
Async XLA Ops:
  7.9 14.8 %copy-start.10 = (f32[100]{0:T(128)S(1)}, f32[100]{0:T(128)}, u32[]{:S(2)}) copy-start(f32[100]{0:T(128)} %param.11) | copy-start | bytes 1204
  7.9 11.5 %collective-permute-start = (f32[100,1024]{1,0:T(8,128)}, f32[100,1024]{1,0:T(8,128)S(1)}, u32[]{:S(2)}, u32[]{:S(2)}) collective-permute-start(f32[100,1024]{1,0:T(8,128)} %get-tuple-element.45.refs_0_), channel_id=1, source_target_pairs={{0,64},{4,68},{8,72},{12,76},{64,0},{68,4},{72,8},{76,12},{16,80},... | collective-permute-start | bytes 1228808 | tf_op jit(solution)/shard_map/ppermute | solution.py:48
  10.1 9.3 %collective-permute-start.1 = (f32[100,1024]{1,0:T(8,128)}, f32[100,1024]{1,0:T(8,128)S(1)}, u32[]{:S(2)}, u32[]{:S(2)}) collective-permute-start(f32[100,1024]{1,0:T(8,128)} %get-tuple-element.45.refs_0_), channel_id=1, source_target_pairs={{0,32},{4,36},{8,40},{12,44},{64,96},{68,100},{72,104},{76,108},{1... | collective-permute-start | bytes 1228808 | tf_op jit(solution)/shard_map/ppermute | solution.py:48
  18.2 2.0 %collective-permute-start.2 = (f32[100,1024]{1,0:T(8,128)}, f32[100,1024]{1,0:T(8,128)S(1)}, u32[]{:S(2)}, u32[]{:S(2)}) collective-permute-start(f32[100,1024]{1,0:T(8,128)} %get-tuple-element.46.refs_0_), channel_id=1, source_target_pairs={{0,32},{4,36},{8,40},{12,44},{64,96},{68,100},{72,104},{76,108},{1... | collective-permute-start | bytes 1228808 | tf_op jit(solution)/shard_map/ppermute | solution.py:48
  18.3 16.7 %copy-start.4 = (s32[4]{0:T(128)}, s32[4]{0:T(128)S(1)}, u32[]{:S(2)}) copy-start(s32[4]{0:T(128)S(1)} %pad_add_fusion.where) | copy-start | bytes 52
  19.4 4.0 %copy-start.7 = (f32[100,1024]{1,0:T(8,128)}, f32[100,1024]{1,0:T(8,128)S(1)}, u32[]{:S(2)}) copy-start(f32[100,1024]{1,0:T(8,128)S(1)} %collective-permute-done.refs_2_) | copy-start | bytes 1228804
  19.4 4.0 %copy-start.8 = (f32[100,1024]{1,0:T(8,128)}, f32[100,1024]{1,0:T(8,128)S(1)}, u32[]{:S(2)}) copy-start(f32[100,1024]{1,0:T(8,128)S(1)} %collective-permute-done.1.refs_1_) | copy-start | bytes 1228804
  20.2 3.2 %collective-permute-start.3 = (f32[100,1024]{1,0:T(8,128)S(1)}, f32[100,1024]{1,0:T(8,128)S(1)}, u32[]{:S(2)}, u32[]{:S(2)}) collective-permute-start(f32[100,1024]{1,0:T(8,128)S(1)} %collective-permute-done.refs_2_), channel_id=1, source_target_pairs={{0,32},{4,36},{8,40},{12,44},{64,96},{68,100},{72,104},{76,108},{1... | collective-permute-start | bytes 1228808 | tf_op jit(solution)/shard_map/ppermute | solution.py:48
  21.2 11.6 %collective-permute-start.4 = (f32[100,1024]{1,0:T(8,128)}, f32[100,1024]{1,0:T(8,128)S(1)}, u32[]{:S(2)}, u32[]{:S(2)}) collective-permute-start(f32[100,1024]{1,0:T(8,128)} %get-tuple-element.46.refs_0_), channel_id=1, source_target_pairs={{0,64},{4,68},{8,72},{12,76},{64,0},{68,4},{72,8},{76,12},{16,80},... | collective-permute-start | bytes 1228808 | tf_op jit(solution)/shard_map/ppermute | solution.py:48
  23.4 0.8 copy-start.9
  24.2 10.8 %copy-start = (bf16[100,1024]{1,0:T(8,128)(2,1)S(1)}, bf16[100,1024]{1,0:T(8,128)(2,1)}, u32[]{:S(2)}) copy-start(bf16[100,1024]{1,0:T(8,128)(2,1)} %refs_9_.3) | copy-start | bytes 614404
  24.2 10.8 %copy-start.1 = (f32[100,1]{1,0:T(8,128)S(1)}, f32[100,1]{1,0:T(8,128)}, u32[]{:S(2)}) copy-start(f32[100,1]{1,0:T(8,128)} %copy.14.refs_6_) | copy-start | bytes 1204
  24.2 10.8 %copy-start.2 = (f32[100,1024]{1,0:T(8,128)S(1)}, f32[100,1024]{1,0:T(8,128)}, u32[]{:S(2)}) copy-start(f32[100,1024]{1,0:T(8,128)} %get-tuple-element.46.refs_0_) | copy-start | bytes 1228804
  24.2 10.8 %copy-start.3 = (f32[2048]{0:T(1024)S(1)}, f32[2048]{0:T(1024)}, u32[]{:S(2)}) copy-start(f32[2048]{0:T(1024)} %param.10) | copy-start | bytes 24580
  32.8 2.3 %collective-permute-start.5 = (f32[100,1024]{1,0:T(8,128)S(1)}, f32[100,1024]{1,0:T(8,128)S(1)}, u32[]{:S(2)}, u32[]{:S(2)}) collective-permute-start(f32[100,1024]{1,0:T(8,128)S(1)} %collective-permute-done.4.refs_2_), channel_id=1, source_target_pairs={{0,32},{4,36},{8,40},{12,44},{64,96},{68,100},{72,104},{76,108},{1... | collective-permute-start | bytes 1228808 | tf_op jit(solution)/shard_map/ppermute | solution.py:48
  44.2 7.2 %collective-permute-start.6 = (f32[4,288,512]{2,1,0:T(8,128)}, f32[4,288,512]{2,1,0:T(8,128)S(1)}, u32[]{:S(2)}, u32[]{:S(2)}) collective-permute-start(f32[4,288,512]{2,1,0:T(8,128)} %get-tuple-element.61), channel_id=1, source_target_pairs={{0,32},{4,36},{8,40},{12,44},{64,96},{68,100},{72,104},{76,108},{1... | collective-permute-start | bytes 7077896 | tf_op jit(solution)/shard_map/ppermute | solution.py:48
  51.4 2.5 %copy-start.6 = (f32[4,288,512]{2,1,0:T(8,128)S(1)}, f32[4,288,512]{2,1,0:T(8,128)}, u32[]{:S(2)}) copy-start(f32[4,288,512]{2,1,0:T(8,128)} %shard_map.131) | copy-start | bytes 7077892
  53.9 15.9 %collective-permute-start.9 = (f32[288,512]{1,0:T(8,128)S(1)}, f32[288,512]{1,0:T(8,128)S(1)}, u32[]{:S(2)}, u32[]{:S(2)}) collective-permute-start(f32[288,512]{1,0:T(8,128)S(1)} %add_bitcast_fusion.1), channel_id=1, source_target_pairs={{0,12},{4,0},{8,4},{12,8},{64,76},{68,64},{72,68},{76,72},{16,28},... | collective-permute-start | bytes 1769480 | tf_op jit(solution)/shard_map/ppermute | solution.py:48
  56.7 16.6 %collective-permute-start.8 = (f32[288,512]{1,0:T(8,128)S(1)}, f32[288,512]{1,0:T(8,128)S(1)}, u32[]{:S(2)}, u32[]{:S(2)}) collective-permute-start(f32[288,512]{1,0:T(8,128)S(1)} %add_bitcast_fusion.2), channel_id=1, source_target_pairs={{0,4},{4,8},{8,12},{12,0},{64,68},{68,72},{72,76},{76,64},{16,20},... | collective-permute-start | bytes 1769480 | tf_op jit(solution)/shard_map/ppermute | solution.py:48
  56.7 16.6 %collective-permute-start.7 = (f32[288,512]{1,0:T(8,128)S(1)}, f32[288,512]{1,0:T(8,128)S(1)}, u32[]{:S(2)}, u32[]{:S(2)}) collective-permute-start(f32[288,512]{1,0:T(8,128)S(1)} %fusion), channel_id=1, source_target_pairs={{0,8},{4,12},{8,0},{12,4},{64,72},{68,76},{72,64},{76,68},{16,24},... | collective-permute-start | bytes 1769480 | tf_op jit(solution)/shard_map/ppermute | solution.py:48
  73.5 6.1 %collective-permute-start.10 = (f32[72,512]{1,0:T(8,128)S(1)}, f32[72,512]{1,0:T(8,128)S(1)}, u32[]{:S(2)}, u32[]{:S(2)}) collective-permute-start(f32[72,512]{1,0:T(8,128)S(1)} %get-tuple-element.84), channel_id=1, source_target_pairs={{0,1},{4,5},{8,9},{12,13},{64,65},{68,69},{72,73},{76,77},{16,17},... | collective-permute-start | bytes 442376 | tf_op jit(solution)/shard_map/ppermute | solution.py:48
  74.9 4.7 %collective-permute-start.11 = (f32[72,512]{1,0:T(8,128)S(1)}, f32[72,512]{1,0:T(8,128)S(1)}, u32[]{:S(2)}, u32[]{:S(2)}) collective-permute-start(f32[72,512]{1,0:T(8,128)S(1)} %get-tuple-element.86), channel_id=1, source_target_pairs={{0,3},{4,7},{8,11},{12,15},{64,67},{68,71},{72,75},{76,79},{16,19}... | collective-permute-start | bytes 442376 | tf_op jit(solution)/shard_map/ppermute | solution.py:48
  77.2 5.5 %collective-permute-start.12 = (f32[72,512]{1,0:T(8,128)S(1)}, f32[72,512]{1,0:T(8,128)S(1)}, u32[]{:S(2)}, u32[]{:S(2)}) collective-permute-start(f32[72,512]{1,0:T(8,128)S(1)} %get-tuple-element.85), channel_id=1, source_target_pairs={{0,2},{4,6},{8,10},{12,14},{64,66},{68,70},{72,74},{76,78},{16,18}... | collective-permute-start | bytes 442376 | tf_op jit(solution)/shard_map/ppermute | solution.py:48
  78.4 48.5 %copy-start.5 = (s32[4]{0:T(128)S(1)}, s32[4]{0:T(128)}, u32[]{:S(2)}) copy-start(s32[4]{0:T(128)} %copy-done.4) | copy-start | bytes 52
  82.7 5.3 %collective-permute-start.13 = (f32[72,512]{1,0:T(8,128)S(1)}, f32[72,512]{1,0:T(8,128)S(1)}, u32[]{:S(2)}, u32[]{:S(2)}) collective-permute-start(f32[72,512]{1,0:T(8,128)S(1)} %fusion.2), channel_id=1, source_target_pairs={{0,64},{4,68},{8,72},{12,76},{64,16},{68,20},{72,24},{76,28},{16,8... | collective-permute-start | bytes 442376 | tf_op jit(solution)/shard_map/ppermute | solution.py:48
  84.1 4.0 %collective-permute-start.14 = (f32[72,512]{1,0:T(8,128)S(1)}, f32[72,512]{1,0:T(8,128)S(1)}, u32[]{:S(2)}, u32[]{:S(2)}) collective-permute-start(f32[72,512]{1,0:T(8,128)S(1)} %fusion.2), channel_id=1, source_target_pairs={{0,80},{4,84},{8,88},{12,92},{64,0},{68,4},{72,8},{76,12},{16,64},... | collective-permute-start | bytes 442376 | tf_op jit(solution)/shard_map/ppermute | solution.py:48
  85.6 5.6 %collective-permute-start.15 = (f32[72,512]{1,0:T(8,128)S(1)}, f32[72,512]{1,0:T(8,128)S(1)}, u32[]{:S(2)}, u32[]{:S(2)}) collective-permute-start(f32[72,512]{1,0:T(8,128)S(1)} %fusion.2), channel_id=1, source_target_pairs={{0,16},{4,20},{8,24},{12,28},{64,80},{68,84},{72,88},{76,92},{16,0... | collective-permute-start | bytes 442376 | tf_op jit(solution)/shard_map/ppermute | solution.py:48
  91.2 6.9 %collective-permute-start.16 = (f32[72,512]{1,0:T(8,128)S(1)}, f32[72,512]{1,0:T(8,128)S(1)}, u32[]{:S(2)}, u32[]{:S(2)}) collective-permute-start(f32[72,512]{1,0:T(8,128)S(1)} %add_add_fusion.1), channel_id=1, source_target_pairs={{0,3},{4,7},{8,11},{12,15},{64,67},{68,71},{72,75},{76,79},{16,19}... | collective-permute-start | bytes 442376 | tf_op jit(solution)/shard_map/ppermute | solution.py:48
  94.4 5.5 %collective-permute-start.17 = (f32[72,512]{1,0:T(8,128)S(1)}, f32[72,512]{1,0:T(8,128)S(1)}, u32[]{:S(2)}, u32[]{:S(2)}) collective-permute-start(f32[72,512]{1,0:T(8,128)S(1)} %add_add_fusion.1), channel_id=1, source_target_pairs={{0,2},{4,6},{8,10},{12,14},{64,66},{68,70},{72,74},{76,78},{16,18}... | collective-permute-start | bytes 442376 | tf_op jit(solution)/shard_map/ppermute | solution.py:48
  96.0 5.5 %collective-permute-start.18 = (f32[72,512]{1,0:T(8,128)S(1)}, f32[72,512]{1,0:T(8,128)S(1)}, u32[]{:S(2)}, u32[]{:S(2)}) collective-permute-start(f32[72,512]{1,0:T(8,128)S(1)} %add_add_fusion.1), channel_id=1, source_target_pairs={{0,1},{4,5},{8,9},{12,13},{64,65},{68,69},{72,73},{76,77},{16,17},... | collective-permute-start | bytes 442376 | tf_op jit(solution)/shard_map/ppermute | solution.py:48
  101.7 16.6 %collective-permute-start.19 = (f32[288,512]{1,0:T(8,128)S(1)}, f32[288,512]{1,0:T(8,128)S(1)}, u32[]{:S(2)}, u32[]{:S(2)}) collective-permute-start(f32[288,512]{1,0:T(8,128)S(1)} %constant_dynamic-slice_fusion.refs_0_), channel_id=1, source_target_pairs={{0,4},{4,8},{8,12},{12,0},{64,68},{68,72},{72,76},{76,64},{16,20},... | collective-permute-start | bytes 1769480 | tf_op jit(solution)/shard_map/ppermute | solution.py:48
  101.8 21.8 %collective-permute-start.20 = (f32[288,512]{1,0:T(8,128)S(1)}, f32[288,512]{1,0:T(8,128)S(1)}, u32[]{:S(2)}, u32[]{:S(2)}) collective-permute-start(f32[288,512]{1,0:T(8,128)S(1)} %constant_dynamic-slice_fusion.refs_0_), channel_id=1, source_target_pairs={{0,8},{4,12},{8,0},{12,4},{64,72},{68,76},{72,64},{76,68},{16,24},... | collective-permute-start | bytes 1769480 | tf_op jit(solution)/shard_map/ppermute | solution.py:48
  102.6 20.9 %collective-permute-start.21 = (f32[288,512]{1,0:T(8,128)S(1)}, f32[288,512]{1,0:T(8,128)S(1)}, u32[]{:S(2)}, u32[]{:S(2)}) collective-permute-start(f32[288,512]{1,0:T(8,128)S(1)} %constant_dynamic-slice_fusion.refs_0_), channel_id=1, source_target_pairs={{0,12},{4,0},{8,4},{12,8},{64,76},{68,64},{72,68},{76,72},{16,28},... | collective-permute-start | bytes 1769480 | tf_op jit(solution)/shard_map/ppermute | solution.py:48
  104.4 20.0 %collective-permute-start.22 = (f32[288,512]{1,0:T(8,128)S(1)}, f32[288,512]{1,0:T(8,128)S(1)}, u32[]{:S(2)}, u32[]{:S(2)}) collective-permute-start(f32[288,512]{1,0:T(8,128)S(1)} %constant_dynamic-slice_fusion.refs_0_), channel_id=1, source_target_pairs={{0,32},{4,36},{8,40},{12,44},{64,96},{68,100},{72,104},{76,108},{1... | collective-permute-start | bytes 1769480 | tf_op jit(solution)/shard_map/ppermute | solution.py:48
  118.3 6.8 %collective-permute-start.23 = (f32[288,512]{1,0:T(8,128)S(1)}, f32[288,512]{1,0:T(8,128)S(1)}, u32[]{:S(2)}, u32[]{:S(2)}) collective-permute-start(f32[288,512]{1,0:T(8,128)S(1)} %collective-permute-done.19.refs_1_), channel_id=1, source_target_pairs={{0,32},{4,36},{8,40},{12,44},{64,96},{68,100},{72,104},{76,108},{1... | collective-permute-start | bytes 1769480 | tf_op jit(solution)/shard_map/ppermute | solution.py:48
  123.5 2.5 %collective-permute-start.24 = (f32[288,512]{1,0:T(8,128)S(1)}, f32[288,512]{1,0:T(8,128)S(1)}, u32[]{:S(2)}, u32[]{:S(2)}) collective-permute-start(f32[288,512]{1,0:T(8,128)S(1)} %collective-permute-done.20.refs_2_), channel_id=1, source_target_pairs={{0,32},{4,36},{8,40},{12,44},{64,96},{68,100},{72,104},{76,108},{1... | collective-permute-start | bytes 1769480 | tf_op jit(solution)/shard_map/ppermute | solution.py:48
  123.5 3.3 %collective-permute-start.25 = (f32[288,512]{1,0:T(8,128)S(1)}, f32[288,512]{1,0:T(8,128)S(1)}, u32[]{:S(2)}, u32[]{:S(2)}) collective-permute-start(f32[288,512]{1,0:T(8,128)S(1)} %collective-permute-done.21.refs_3_), channel_id=1, source_target_pairs={{0,32},{4,36},{8,40},{12,44},{64,96},{68,100},{72,104},{76,108},{1... | collective-permute-start | bytes 1769480 | tf_op jit(solution)/shard_map/ppermute | solution.py:48
